TPU v7x, 1024 devices: a whole 8x8x8 slice. The times are simulated.
1024 devices in a mesh: dp: 4 (over x_lo), expert: 8 (over y), tensor: 32 (over x_hi, z, core).
Axes of the slice: x: 8 (x_hi: 2, x_lo: 4; x = x_hi * 4 + x_lo), y: 8, z: 8, core: 2. Of those that a mesh axis runs over, the one named last changes fastest.
Arguments:
- tokens: bfloat16 [4096, 4096], P(('dp', 'expert'), 'tensor'), may hold values from -6 to 6
- cotangent: bfloat16 [4096, 4096], P(('dp', 'expert'), 'tensor'), may hold values from -1.1953125 to 1.1953125
- routes: int32 [4096, 2], P(('dp', 'expert')), may hold values from 0 to 7, all different within a row; in each aligned block of 128 rows (0 to 127, 128 to 255, ...) at most 64 rows name the same one
- route_weight: float32 [4096, 2], P(('dp', 'expert')), may hold values from 0.05 to 1
- w_gate_up: bfloat16 [8, 4096, 3072], P('expert', 'tensor'), may hold values from -0.09375 to 0.09375
- w_down: bfloat16 [8, 1536, 4096], P('expert', None, 'tensor'), may hold values from -0.15625 to 0.15625
Outputs:
- expert_out: bfloat16 [16384, 4096], P(('dp', 'expert'), 'tensor')
- w_down_grad: float32 [8, 1536, 4096], P('expert', 'dp', 'tensor')
Inputs may be any that keep to these rules, and one draw needn't show every extreme that they name: `routes`: each row names 2 different experts. In each aligned block of 128 rows (the rows of one index pair of dp and expert) no expert is named by more than 64 rows, a bound that some block reaches.
All inputs are finite; a program needn't handle non-finite values.
Results may differ from a plain program's by a relative error of at most 0.0049.
Values may be sent and summed in bfloat16 or wider, within the bound.
No kernel may reach another device: no remote copies, remote signals or barrier semaphores. Data moves between devices by JAX's collectives and lax.ppermute only.
A program may use at most 32 MiB of HBM per device.

v0:
```python
import jax
import jax.numpy as jnp
from jax import lax
from jax.sharding import PartitionSpec as P


def per_device(tokens, cotangent, routes, route_weight, w_gate_up, w_down):
    tok_rows, local_width = tokens.shape
    top_count = routes.shape[1]
    experts = lax.axis_size("expert")
    capacity = min(tok_rows, 2 * tok_rows * top_count // experts)
    owner_rows = experts * capacity
    flat_routes = routes.reshape(-1)
    onehot = (flat_routes[:, None] == jnp.arange(experts, dtype=jnp.int32)[None, :]).astype(
        jnp.int32
    )
    before = jnp.cumsum(onehot, axis=0) - onehot
    slot_index = jnp.sum(before * onehot, axis=1)
    target = flat_routes * capacity + slot_index
    matches = jnp.arange(owner_rows, dtype=jnp.int32)[:, None] == target[None, :]
    select = jnp.sum(
        matches.reshape(owner_rows, tok_rows, top_count).astype(jnp.float32), axis=2
    ).astype(jnp.bfloat16)
    weights_slot = jnp.sum(jnp.where(matches, route_weight.reshape(1, -1), 0.0), axis=1)
    sent_rows = jnp.dot(select, tokens, preferred_element_type=jnp.float32).astype(jnp.bfloat16)
    sent_rows = sent_rows.reshape(experts, capacity, local_width)
    sent_grads = (
        jnp.dot(select, cotangent, preferred_element_type=jnp.float32) * weights_slot[:, None]
    ).astype(jnp.bfloat16)
    sent_grads = sent_grads.reshape(experts, capacity, local_width)
    moved_rows, moved_grads = (
        lax.all_to_all(sent_rows, "expert", split_axis=0, concat_axis=0, tiled=True),
        lax.all_to_all(sent_grads, "expert", split_axis=0, concat_axis=0, tiled=True),
    )
    slot_rows = moved_rows.reshape(owner_rows, local_width)
    weights = w_gate_up[0]
    down_local = w_down[0]
    hidden_units = weights.shape[1] // 2
    shares = lax.psum_scatter(
        jnp.dot(slot_rows, weights, preferred_element_type=jnp.float32),
        "tensor",
        scatter_dimension=0,
        tiled=True,
    )
    hidden_share = (jax.nn.silu(shares[:, :hidden_units]) * shares[:, hidden_units:]).astype(
        jnp.bfloat16
    )
    slot_grads = moved_grads.reshape(owner_rows, local_width)
    portion = lax.all_gather(hidden_share, "tensor", axis=0, tiled=True)
    outputs = jnp.dot(portion, down_local, preferred_element_type=jnp.float32)
    grad_total = lax.dot_general(
        portion, slot_grads, (((0,), (0,)), ((), ())), preferred_element_type=jnp.float32
    )
    outputs, grad_total = (outputs, grad_total)
    grad_share = lax.psum_scatter(grad_total, "dp", scatter_dimension=0, tiled=True)
    return (
        outputs.astype(jnp.bfloat16),
        grad_share.reshape(1, grad_share.shape[0], grad_share.shape[1]),
    )


def solution(mesh):
    in_specs = (
        P(("dp", "expert"), "tensor"),
        P(("dp", "expert"), "tensor"),
        P(("dp", "expert"), None),
        P(("dp", "expert"), None),
        P("expert", "tensor", None),
        P("expert", None, "tensor"),
    )
    out_specs = (P(("dp", "expert"), "tensor"), P("expert", "dp", "tensor"))
    return jax.shard_map(
        per_device, mesh=mesh, in_specs=in_specs, out_specs=out_specs, check_vma=False
    )
```

profile of v0, /device:TPU:1, one launch (start us, length us, event | category | flops | bytes accessed | tf_op | source)
XLA Modules:
  0.0 347.3 jit_solution(3112325442703351901)
XLA Ops:
  7.2 0.0 copy-start
  7.2 0.0 reduce-scatter.3.cloned.1.call-start
  7.2 0.9 copy.20
  8.1 0.1 eq.46
  8.2 0.1 eq.50
  8.4 0.6 reduce-window.6
  9.0 0.2 slice_reduce_fusion
  9.2 0.1 fusion.8
  9.3 0.1 reduce_sum.30
  9.5 0.1 copy.22
  9.5 0.7 multiply_add_fusion.1
  10.2 0.1 convert_reduce_fusion
  10.3 0.9 convolution_convert_fusion
  11.2 15.8 %all_to_all.10 = bf16[8,64,128]{2,1,0:T(8,128)(2,1)S(1)} all-to-all(bf16[8,64,128]{2,1,0:T(8,128)(2,1)S(1)} %bitcast.30), channel_id=1, replica_groups=mesh['dp'=4,'expert'=8,'tensor'=32] {'expert'}, dimensions={0} | all-to-all | bytes 262144 | tf_op jit(solution)/shard_map/all_to_all | solution.py:32
  27.1 0.0 copy-done
  27.1 3.6 %fusion.1 = f32[512,3072]{1,0:T(8,128)} fusion(bf16[512,128]{1,0:T(8,128)(2,1)S(1)} %bitcast.27, bf16[1,128,3072]{2,1,0:T(8,128)(2,1)S(1)} %copy-done), kind=kOutput, calls=%fused_computation.4 | convolution fusion | flops 402653184 | bytes 7208960 | tf_op jit(solution)/shard_map/dot_general | solution.py:40
  30.7 0.0 copy-start.4
  30.7 0.0 copy-start.3
  30.7 0.0 reduce-scatter.3.cloned.1.call-update
  30.7 0.0 all-gather.2.cloned.1.call-start
  30.8 178.0 %reduce-scatter.3.cloned.1.call-done = f32[16,3072]{1,0:T(8,128)} async-done(((f32[512,3072]{1,0:T(8,128)}), f32[16,3072]{1,0:T(8,128)}) %reduce-scatter.3.cloned.1.call-update) | async-done | bytes 196624 | tf_op jit(solution)/shard_map/reduce_scatter | solution.py:39
  208.8 1.6 fusion.4
  210.4 0.0 all-gather.2.cloned.1.call-update
  210.4 0.0 reduce-scatter.5.cloned.1.call-start
  210.5 0.0 copy-done.4
  210.5 0.1 copy.23
  210.6 0.1 broadcast_in_dim.18
  210.8 0.1 select_reduce_fusion
  210.9 0.0 copy-done.3
  210.9 0.2 fusion
  211.1 14.3 %all_to_all.11 = bf16[8,64,128]{2,1,0:T(8,128)(2,1)S(1)} all-to-all(bf16[8,64,128]{2,1,0:T(8,128)(2,1)S(1)} %bitcast.29), channel_id=1, replica_groups=mesh['dp'=4,'expert'=8,'tensor'=32] {'expert'}, dimensions={0} | all-to-all | bytes 262144 | tf_op jit(solution)/shard_map/all_to_all | solution.py:33
  225.4 84.2 %all-gather.2.cloned.1.call-done = bf16[512,1536]{1,0:T(8,128)(2,1)} async-done(((bf16[16,1536]{1,0:T(8,128)(2,1)}), bf16[512,1536]{1,0:T(8,128)(2,1)}) %all-gather.2.cloned.1.call-update) | async-done | bytes 1572880 | tf_op jit(solution)/shard_map/all_gather | solution.py:49
  309.6 0.0 copy-start.1
  309.6 0.0 copy-start.2
  309.6 3.0 fusion.10
  312.7 0.0 reduce-scatter.5.cloned.1.call-update
  312.7 0.0 copy-done.1
  312.7 0.0 copy-done.2
  312.7 1.2 convolution_convert_fusion.1
  313.9 26.8 %reduce-scatter.5.cloned.1.call-done = f32[384,128]{1,0:T(8,128)} async-done(((f32[1536,128]{1,0:T(8,128)}), f32[384,128]{1,0:T(8,128)}) %reduce-scatter.5.cloned.1.call-update) | async-done | bytes 196624 | tf_op jit(solution)/shard_map/reduce_scatter | solution.py:55
  (4 shorter events, 0.1 us)
Async XLA Ops:
  7.2 19.9 %copy-start = (bf16[1,128,3072]{2,1,0:T(8,128)(2,1)S(1)}, bf16[1,128,3072]{2,1,0:T(8,128)(2,1)}, u32[]{:S(2)}) copy-start(bf16[1,128,3072]{2,1,0:T(8,128)(2,1)} %param.10) | copy-start | bytes 2359300
  7.2 201.6 %reduce-scatter.3.cloned.1.call-start = ((), (), s32[]{:S(2)}) async-start(), calls=%async_computation.4 | async-start | bytes 6488064 | tf_op jit(solution)/shard_map/reduce_scatter | solution.py:39
  30.7 179.8 %copy-start.4 = (f32[128,2]{0,1:T(2,128)S(1)}, f32[128,2]{0,1:T(2,128)}, u32[]{:S(2)}) copy-start(f32[128,2]{0,1:T(2,128)} %param.9) | copy-start | bytes 3076
  30.7 180.2 %copy-start.3 = (bf16[128,128]{1,0:T(8,128)(2,1)S(1)}, bf16[128,128]{1,0:T(8,128)(2,1)}, u32[]{:S(2)}) copy-start(bf16[128,128]{1,0:T(8,128)(2,1)} %param.7) | copy-start | bytes 98308
  30.7 278.9 %all-gather.2.cloned.1.call-start = ((), (), s32[]{:S(2)}) async-start(), calls=%async_computation.5 | async-start | bytes 1622016 | tf_op jit(solution)/shard_map/all_gather | solution.py:49
  210.4 130.3 %reduce-scatter.5.cloned.1.call-start = ((), (), s32[]{:S(2)}) async-start(), calls=%async_computation.6 | async-start | bytes 983040 | tf_op jit(solution)/shard_map/reduce_scatter | solution.py:55
  309.6 3.1 copy-start.1
  309.6 3.1 copy-start.2
Sparse Core Ops, SparseCore 0:
  30.8 177.9 reduce-scatter.2
  213.9 95.6 all-gather.1
  313.6 27.0 reduce-scatter.4
where the time goes:
time: 348 us; the launch traced here: 347 us
  waiting for transfers between devices  289 us (83%)
  blocking collectives  30.1 us (9%)
  between operations  13.8 us (4%)
  matrix products  9.01 us (3%)
    reduce_scatter x1, waiting for transfers between devices, per_device(): lax.psum_scatter(jnp.dot(slot_rows, weights, preferred_element_type=jnp.f...  178 us
    all_gather x1, waiting for transfers between devices, per_device(): portion = lax.all_gather(hidden_share, 'tensor', axis=0, tiled=True)  84.2 us
    reduce_scatter x1, waiting for transfers between devices, per_device(): lax.psum_scatter(grad_total, 'dp', scatter_dimension=0, tiled=True)  26.8 us
    all_to_all x1, blocking collectives, per_device(): lax.all_to_all(sent_rows, 'expert', split_axis=0, concat_axis=0, tiled=True)  15.8 us
    all_to_all x1, blocking collectives, per_device(): lax.all_to_all(sent_grads, 'expert', split_axis=0, concat_axis=0, tiled=T...  14.3 us
  transfers between devices with their start and end apart: 3, of which 3 were waited for; matrix products, arithmetic and copies ran while one was open for 1% of the time, Pallas kernels for 0%

commit v1 on v0

v1 whole, which is shorter than its diff:
```python
import jax
import jax.numpy as jnp
from jax import lax
from jax.sharding import Mesh, PartitionSpec as P

BF = jnp.bfloat16
F32 = jnp.float32
XH, Z, CORE = 2, 8, 2
QUARTERS = XH * CORE


def exchange(pieces, axes):
    return lax.all_to_all(pieces, axes, split_axis=0, concat_axis=0, tiled=True)


def slots_of(routes, experts, capacity):
    tok_rows, top_count = routes.shape
    flat = routes.reshape(-1)
    onehot = (flat[:, None] == jnp.arange(experts, dtype=jnp.int32)[None, :]).astype(jnp.int32)
    before = jnp.cumsum(onehot, axis=0) - onehot
    slot = jnp.sum(before * onehot, axis=1)
    target = flat * capacity + slot
    return jnp.arange(experts * capacity, dtype=jnp.int32)[:, None] == target[None, :]


def per_device(tokens, cotangent, routes, route_weight, w_gate_up, w_down):
    tok_rows, width = tokens.shape
    experts = lax.axis_size("expert")
    dps = lax.axis_size("dp")
    top_count = routes.shape[1]
    capacity = min(tok_rows, 2 * tok_rows * top_count // experts)
    rows = experts * capacity
    hidden_units = w_gate_up.shape[2] // 2
    part = hidden_units // QUARTERS
    core = lax.axis_index("core")

    weights = w_gate_up[0].reshape(width, 2, QUARTERS, part).transpose(2, 0, 1, 3)
    weights = exchange(weights.reshape(QUARTERS, width, 2 * part), ("xh", "core"))
    weights = weights.reshape(QUARTERS * width, 2 * part)

    matches = slots_of(routes, experts, capacity)
    select = jnp.sum(
        matches.reshape(rows, tok_rows, top_count).astype(F32), axis=2
    ).astype(BF)
    sent_rows = jnp.dot(select, tokens, preferred_element_type=F32).astype(BF)
    sent_rows = sent_rows.reshape(experts, 1, capacity, width)
    sent_rows = jnp.broadcast_to(sent_rows, (experts, QUARTERS, capacity, width))
    moved = exchange(
        sent_rows.reshape(experts * QUARTERS, capacity, width), ("expert", "xh", "core")
    )
    slot_rows = moved.reshape(experts, QUARTERS, capacity, width)
    slot_rows = slot_rows.transpose(0, 2, 1, 3).reshape(rows, QUARTERS * width)

    partial = jnp.dot(slot_rows, weights, preferred_element_type=F32).astype(BF)
    moved = exchange(partial.reshape(Z, rows // Z, 2 * part), "z")

    weights_slot = jnp.sum(jnp.where(matches, route_weight.reshape(1, -1), 0.0), axis=1)
    sent_grads = (
        jnp.dot(select, cotangent, preferred_element_type=F32) * weights_slot[:, None]
    ).astype(BF)
    slot_grads = exchange(sent_grads.reshape(experts, capacity, width), "expert")
    slot_grads = slot_grads.reshape(rows, width)

    gate_up = jnp.sum(moved.astype(F32), axis=0)
    hidden = (jax.nn.silu(gate_up[:, :part]) * gate_up[:, part:]).astype(BF)

    pair = lax.all_gather(hidden, "xh", axis=0)
    spread = exchange(jnp.broadcast_to(pair[None], (Z,) + pair.shape), "z")
    mine = spread.transpose(1, 0, 2, 3).reshape(XH, rows, part)
    other = lax.ppermute(mine, "core", [(0, 1), (1, 0)])
    first = jnp.where(core == 0, mine, other)
    second = jnp.where(core == 0, other, mine)
    whole = jnp.stack([first, second], axis=1).reshape(QUARTERS, rows, part)

    down = w_down[0].reshape(QUARTERS, part, width)
    grads = lax.dot_general(
        whole, slot_grads, (((1,), (0,)), ((), ())), preferred_element_type=F32
    ).astype(BF)
    moved = exchange(grads.reshape(dps, hidden_units // dps, width), "dp")
    outputs = lax.dot_general(
        whole, down, (((0, 2), (0, 1)), ((), ())), preferred_element_type=F32
    ).astype(BF)
    grad_share = jnp.sum(moved.astype(F32), axis=0)
    return outputs, grad_share[None]


def solution(mesh):
    dps, experts = mesh.shape["dp"], mesh.shape["expert"]
    fine = Mesh(
        mesh.devices.reshape(dps, experts, XH, Z, CORE), ("dp", "expert", "xh", "z", "core")
    )
    tensor = ("xh", "z", "core")
    in_specs = (
        P(("dp", "expert"), tensor),
        P(("dp", "expert"), tensor),
        P(("dp", "expert"), None),
        P(("dp", "expert"), None),
        P("expert", tensor, None),
        P("expert", None, tensor),
    )
    out_specs = (P(("dp", "expert"), tensor), P("expert", "dp", tensor))
    return jax.shard_map(
        per_device, mesh=fine, in_specs=in_specs, out_specs=out_specs, check_vma=False
    )
```

time: 348 us -> 172 us (0.49)
  waiting for transfers between devices: 289 us -> 49.4 us
  starting transfers between devices: 0.12 us -> 56.2 us
  blocking collectives: 30.1 us -> 51.4 us
  between operations: 13.8 us -> 0.83 us
  matrix products: 9.01 us -> 4.93 us
    reduce_scatter x2 -> x0, waiting for transfers between devices: 205 us -> none  [the longest x1 178 us: per_device(): lax.psum_scatter(jnp.dot(slot_rows, weights, preferred_element_type=jnp.f...]
    all_gather x1 -> x0, waiting for transfers between devices: 84.2 us -> none  [per_device(): portion = lax.all_gather(hidden_share, 'tensor', axis=0, tiled=True)]
    all_to_all x0 -> x4, waiting for transfers between devices: none -> 49.4 us  [exchange(): return lax.all_to_all(pieces, axes, split_axis=0, concat_axis=0, tiled=True)]
    all_to_all x0 -> x4, starting transfers between devices: none -> 44.6 us  [exchange(): return lax.all_to_all(pieces, axes, split_axis=0, concat_axis=0, tiled=True)]
    all_to_all x2, blocking collectives: 30.1 us -> 42.5 us  [exchange(): return lax.all_to_all(pieces, axes, split_axis=0, concat_axis=0, tiled=True)]
    ppermute x0 -> x1, starting transfers between devices: none -> 11.6 us  [per_device(): other = lax.ppermute(mine, 'core', [(0, 1), (1, 0)])]
    all_gather x0 -> x1, blocking collectives: none -> 8.91 us  [per_device(): pair = lax.all_gather(hidden, 'xh', axis=0)]
    dot_general x5, matrix products: 9.01 us -> 4.93 us  [the longest x1 1.36 us: per_device(): lax.dot_general(whole, slot_grads, (((1,), (0,)), ((), ())), preferred_el...]
  transfers between devices with their start and end apart: 3 -> 5, of which waited for: 3 -> 4; matrix products, arithmetic and copies ran while one was open for 1% -> 3% of each run, Pallas kernels for 0% -> 0%
where the time goes in v1:
time: 172 us; the launch traced here: 171 us
  starting transfers between devices  56.2 us (33%)
  blocking collectives  51.4 us (30%)
  waiting for transfers between devices  49.4 us (29%)
  local copies, waits for them, and re-layouts  5.1 us (3%)
  matrix products  4.93 us (3%)
  other arithmetic  2.91 us (2%)
    all_to_all x4, waiting for transfers between devices, exchange(): return lax.all_to_all(pieces, axes, split_axis=0, concat_axis=0, tiled=True)  49.4 us
    all_to_all x4, starting transfers between devices, exchange(): return lax.all_to_all(pieces, axes, split_axis=0, concat_axis=0, tiled=True)  44.6 us
    all_to_all x2, blocking collectives, exchange(): return lax.all_to_all(pieces, axes, split_axis=0, concat_axis=0, tiled=True)  42.5 us
    ppermute x1, starting transfers between devices, per_device(): other = lax.ppermute(mine, 'core', [(0, 1), (1, 0)])  11.6 us
    all_gather x1, blocking collectives, per_device(): pair = lax.all_gather(hidden, 'xh', axis=0)  8.91 us
  transfers between devices with their start and end apart: 5, of which 4 were waited for; matrix products, arithmetic and copies ran while one was open for 3% of the time, Pallas kernels for 0%

profile of v1, /device:TPU:1, one launch (start us, length us, event | category | flops | bytes accessed | tf_op | source)
XLA Modules:
  0.0 170.8 jit_solution(4399327966049725142)
XLA Ops:
  0.6 0.0 copy-start
  0.6 0.0 copy-start.1
  0.7 0.9 copy.65
  1.5 0.1 eq.51
  1.7 0.1 eq.55
  1.8 0.6 reduce-window.6
  2.4 0.2 slice_reduce_fusion
  2.7 0.1 fusion.8
  2.8 0.1 reduce_sum.48
  2.9 0.1 copy.67
  3.0 0.7 multiply_add_fusion.1
  3.7 0.1 convert_reduce_fusion.2
  3.8 0.9 convolution_convert_fusion.2
  4.7 0.9 broadcast_in_dim.35
  5.6 17.7 %all-to-all-start = ((bf16[32,64,128]{2,1,0:T(8,128)(2,1)}), bf16[32,64,128]{2,1,0:T(8,128)(2,1)S(1)}, u32[]{:S(2)}, u32[]{:S(2)}) async-start(bf16[32,64,128]{2,1,0:T(8,128)(2,1)} %bitcast.3), calls=%async_computation | async-start | bytes 1048576 | tf_op jit(solution)/shard_map/all_to_all | solution.py:13
  23.3 0.0 copy-done.1
  23.3 0.4 copy.69
  23.7 0.9 copy.70
  24.6 15.0 %all-to-all-done = bf16[32,64,128]{2,1,0:T(8,128)(2,1)S(1)} async-done(((bf16[32,64,128]{2,1,0:T(8,128)(2,1)}), bf16[32,64,128]{2,1,0:T(8,128)(2,1)S(1)}, u32[]{:S(2)}, u32[]{:S(2)}) %all-to-all-start) | async-done | bytes 524320 | tf_op jit(solution)/shard_map/all_to_all | solution.py:13
  39.6 8.4 %all-to-all-start.1 = ((bf16[4,128,768]{1,2,0:T(8,128)(2,1)}), bf16[4,128,768]{1,2,0:T(8,128)(2,1)S(1)}, u32[]{:S(2)}, u32[]{:S(2)}) async-start(bf16[4,128,768]{1,2,0:T(8,128)(2,1)} %bitcast.8), calls=%async_computation.1 | async-start | bytes 1572864 | tf_op jit(solution)/shard_map/all_to_all | solution.py:13
  48.0 0.4 copy.68
  48.4 17.8 %all-to-all-done.1 = bf16[4,128,768]{1,2,0:T(8,128)(2,1)S(1)} async-done(((bf16[4,128,768]{1,2,0:T(8,128)(2,1)}), bf16[4,128,768]{1,2,0:T(8,128)(2,1)S(1)}, u32[]{:S(2)}, u32[]{:S(2)}) %all-to-all-start.1) | async-done | bytes 786464 | tf_op jit(solution)/shard_map/all_to_all | solution.py:13
  66.3 0.3 copy.71
  66.6 0.6 convolution_convert_fusion
  67.1 25.0 %all_to_all.30 = bf16[8,64,768]{2,1,0:T(8,128)(2,1)S(1)} all-to-all(bf16[8,64,768]{2,1,0:T(8,128)(2,1)S(1)} %bitcast.61), channel_id=1, replica_groups=mesh['dp'=4,'expert'=8,'xh'=2,'z'=8,'core'=2] {'z'}, dimensions={0} | all-to-all | bytes 1572864 | tf_op jit(solution)/shard_map/all_to_all | solution.py:13
  92.1 0.1 convert_reduce_fusion
  92.2 8.9 %all-gather = bf16[128,384]{1,0:T(8,128)(2,1)S(1)} all-gather(bf16[64,384]{1,0:T(8,128)(2,1)S(1)} %fusion.4), channel_id=2, replica_groups=mesh['dp'=4,'expert'=8,'xh'=2,'z'=8,'core'=2] {'xh'}, dimensions={0}, use_global_device_ids=true | all-gather | bytes 147456 | tf_op jit(solution)/shard_map/all_gather | solution.py:67
  101.2 0.1 broadcast_in_dim.36
  101.3 0.0 copy-start.3
  101.3 0.0 copy-start.2
  101.3 17.5 %all_to_all.31 = bf16[8,2,64,384]{3,2,1,0:T(8,128)(2,1)S(1)} all-to-all(bf16[8,2,64,384]{3,2,1,0:T(8,128)(2,1)S(1)} %broadcast_in_dim.36), channel_id=1, replica_groups=mesh['dp'=4,'expert'=8,'xh'=2,'z'=8,'core'=2] {'z'}, dimensions={0} | all-to-all | bytes 1572864 | tf_op jit(solution)/shard_map/all_to_all | solution.py:13
  118.8 0.1 copy.72
  118.9 11.6 %collective-permute-start = (bf16[2,512,384]{2,1,0:T(8,128)(2,1)S(1)}, bf16[2,512,384]{2,1,0:T(8,128)(2,1)S(1)}, u32[]{:S(2)}, u32[]{:S(2)}) collective-permute-start(bf16[2,512,384]{2,1,0:T(8,128)(2,1)S(1)} %bitcast.58), channel_id=1, source_target_pairs={{0,1},{1,0},{2,3},{3,2},{4,5},{5,4},{6,7},{7,6},{8,9},{9,8},{10,11... | collective-permute-start | bytes 2359304 | tf_op jit(solution)/shard_map/ppermute | solution.py:70
  130.6 0.0 copy-done.3
  130.6 0.1 copy.74
  130.7 0.1 broadcast_in_dim.37
  130.8 0.1 select_reduce_fusion
  131.0 0.0 copy-done.2
  131.0 0.8 fusion
  131.8 5.7 %all-to-all-start.4 = ((bf16[8,64,128]{2,1,0:T(8,128)(2,1)}), bf16[8,64,128]{2,1,0:T(8,128)(2,1)S(1)}, u32[]{:S(2)}, u32[]{:S(2)}) async-start(bf16[8,64,128]{2,1,0:T(8,128)(2,1)} %bitcast.20), calls=%async_computation.4 | async-start | bytes 262144 | tf_op jit(solution)/shard_map/all_to_all | solution.py:13
  137.6 0.0 collective-permute-done
  137.6 0.2 select_bitcast_fusion.1
  137.8 0.2 pad_maximum_fusion
  138.0 0.2 copy.73
  138.1 8.0 %all-to-all-done.4 = bf16[8,64,128]{2,1,0:T(8,128)(2,1)S(1)} async-done(((bf16[8,64,128]{2,1,0:T(8,128)(2,1)}), bf16[8,64,128]{2,1,0:T(8,128)(2,1)S(1)}, u32[]{:S(2)}, u32[]{:S(2)}) %all-to-all-start.4) | async-done | bytes 131104 | tf_op jit(solution)/shard_map/all_to_all | solution.py:13
  146.2 1.4 convolution_convert_fusion.1
  147.5 12.7 %all-to-all-start.5 = ((bf16[4,384,128]{2,1,0:T(8,128)(2,1)}), bf16[4,384,128]{2,1,0:T(8,128)(2,1)S(1)}, u32[]{:S(2)}, u32[]{:S(2)}) async-start(bf16[4,384,128]{2,1,0:T(8,128)(2,1)} %convolution_convert_fusion.1), calls=%async_computation.5 | async-start | bytes 786432 | tf_op jit(solution)/shard_map/all_to_all | solution.py:13
  160.2 0.0 copy-done
  160.3 1.2 fusion.1
  161.5 8.6 %all-to-all-done.5 = bf16[4,384,128]{2,1,0:T(8,128)(2,1)S(1)} async-done(((bf16[4,384,128]{2,1,0:T(8,128)(2,1)}), bf16[4,384,128]{2,1,0:T(8,128)(2,1)S(1)}, u32[]{:S(2)}, u32[]{:S(2)}) %all-to-all-start.5) | async-done | bytes 393248 | tf_op jit(solution)/shard_map/all_to_all | solution.py:13
  170.1 0.7 convert_reduce_fusion.1
  (5 shorter events, 0.1 us)
Async XLA Ops:
  0.6 159.6 %copy-start = (bf16[1,1536,128]{2,1,0:T(8,128)(2,1)S(1)}, bf16[1,1536,128]{2,1,0:T(8,128)(2,1)}, u32[]{:S(2)}) copy-start(bf16[1,1536,128]{2,1,0:T(8,128)(2,1)} %param.11) | copy-start | bytes 1179652
  0.6 22.7 %copy-start.1 = (bf16[1,128,3072]{2,1,0:T(8,128)(2,1)S(1)}, bf16[1,128,3072]{2,1,0:T(8,128)(2,1)}, u32[]{:S(2)}) copy-start(bf16[1,128,3072]{2,1,0:T(8,128)(2,1)} %param.10) | copy-start | bytes 2359300
  5.6 34.0 %all-to-all-start = ((bf16[32,64,128]{2,1,0:T(8,128)(2,1)}), bf16[32,64,128]{2,1,0:T(8,128)(2,1)S(1)}, u32[]{:S(2)}, u32[]{:S(2)}) async-start(bf16[32,64,128]{2,1,0:T(8,128)(2,1)} %bitcast.3), calls=%async_computation | async-start | bytes 1048576 | tf_op jit(solution)/shard_map/all_to_all | solution.py:13
  39.6 26.7 %all-to-all-start.1 = ((bf16[4,128,768]{1,2,0:T(8,128)(2,1)}), bf16[4,128,768]{1,2,0:T(8,128)(2,1)S(1)}, u32[]{:S(2)}, u32[]{:S(2)}) async-start(bf16[4,128,768]{1,2,0:T(8,128)(2,1)} %bitcast.8), calls=%async_computation.1 | async-start | bytes 1572864 | tf_op jit(solution)/shard_map/all_to_all | solution.py:13
  101.3 29.3 %copy-start.3 = (f32[128,2]{0,1:T(2,128)S(1)}, f32[128,2]{0,1:T(2,128)}, u32[]{:S(2)}) copy-start(f32[128,2]{0,1:T(2,128)} %param.9) | copy-start | bytes 3076
  101.3 29.7 %copy-start.2 = (bf16[128,128]{1,0:T(8,128)(2,1)S(1)}, bf16[128,128]{1,0:T(8,128)(2,1)}, u32[]{:S(2)}) copy-start(bf16[128,128]{1,0:T(8,128)(2,1)} %param.7) | copy-start | bytes 98308
  118.9 18.6 %collective-permute-start = (bf16[2,512,384]{2,1,0:T(8,128)(2,1)S(1)}, bf16[2,512,384]{2,1,0:T(8,128)(2,1)S(1)}, u32[]{:S(2)}, u32[]{:S(2)}) collective-permute-start(bf16[2,512,384]{2,1,0:T(8,128)(2,1)S(1)} %bitcast.58), channel_id=1, source_target_pairs={{0,1},{1,0},{2,3},{3,2},{4,5},{5,4},{6,7},{7,6},{8,9},{9,8},{10,11... | collective-permute-start | bytes 2359304 | tf_op jit(solution)/shard_map/ppermute | solution.py:70
  131.8 14.3 %all-to-all-start.4 = ((bf16[8,64,128]{2,1,0:T(8,128)(2,1)}), bf16[8,64,128]{2,1,0:T(8,128)(2,1)S(1)}, u32[]{:S(2)}, u32[]{:S(2)}) async-start(bf16[8,64,128]{2,1,0:T(8,128)(2,1)} %bitcast.20), calls=%async_computation.4 | async-start | bytes 262144 | tf_op jit(solution)/shard_map/all_to_all | solution.py:13
  147.5 22.6 %all-to-all-start.5 = ((bf16[4,384,128]{2,1,0:T(8,128)(2,1)}), bf16[4,384,128]{2,1,0:T(8,128)(2,1)S(1)}, u32[]{:S(2)}, u32[]{:S(2)}) async-start(bf16[4,384,128]{2,1,0:T(8,128)(2,1)} %convolution_convert_fusion.1), calls=%async_computation.5 | async-start | bytes 786432 | tf_op jit(solution)/shard_map/all_to_all | solution.py:13

commit v2 on v1

v2 whole, which is shorter than its diff:
```python
import jax
import jax.numpy as jnp
from jax import lax
from jax.sharding import Mesh, PartitionSpec as P

BF = jnp.bfloat16
F32 = jnp.float32
XH, Z, CORE = 2, 8, 2
QUARTERS = XH * CORE
SWAP = [(0, 1), (1, 0)]


def exchange(pieces, axes):
    return lax.all_to_all(pieces, axes, split_axis=0, concat_axis=0, tiled=True)


def dot(a, b):
    return jnp.dot(a, b, preferred_element_type=F32)


def pick(index, pair):
    first = index == 0
    return jnp.where(first, pair[0], pair[1]), jnp.where(first, pair[1], pair[0])


def slots_of(routes, experts, capacity):
    flat = routes.reshape(-1)
    onehot = (flat[:, None] == jnp.arange(experts, dtype=jnp.int32)[None, :]).astype(jnp.int32)
    before = jnp.cumsum(onehot, axis=0) - onehot
    slot = jnp.sum(before * onehot, axis=1)
    target = flat * capacity + slot
    return jnp.arange(experts * capacity, dtype=jnp.int32)[:, None] == target[None, :]


def per_device(tokens, cotangent, routes, route_weight, w_gate_up, w_down):
    tok_rows, width = tokens.shape
    experts = lax.axis_size("expert")
    dps = lax.axis_size("dp")
    top_count = routes.shape[1]
    capacity = min(tok_rows, 2 * tok_rows * top_count // experts)
    rows = experts * capacity
    hidden_units = w_gate_up.shape[2] // 2
    part = hidden_units // QUARTERS
    core = lax.axis_index("core")
    xh = lax.axis_index("xh")

    far_tokens = lax.ppermute(tokens, "xh", SWAP)

    blocks = w_gate_up[0].reshape(width, 2, XH, CORE, part).transpose(3, 2, 0, 1, 4)
    blocks = blocks.reshape(CORE, XH, width, 2 * part)
    own, theirs = pick(core, blocks)
    beside = lax.ppermute(theirs, "core", SWAP)
    near = jnp.stack([own, beside], axis=1)
    near_own, near_theirs = pick(xh, near)
    far = lax.ppermute(near_theirs, "xh", SWAP)
    w_mine = jnp.concatenate([near_own[0], far[0]], axis=0)
    w_beside = jnp.concatenate([near_own[1], far[1]], axis=0)

    matches = slots_of(routes, experts, capacity)
    select = jnp.sum(
        matches.reshape(rows, tok_rows, top_count).astype(F32), axis=2
    ).astype(BF)
    weights_slot = jnp.sum(jnp.where(matches, route_weight.reshape(1, -1), 0.0), axis=1)
    sent_grads = (dot(select, cotangent) * weights_slot[:, None]).astype(BF)
    sent_rows = dot(select, jnp.concatenate([tokens, far_tokens], axis=1)).astype(BF)
    sent = jnp.concatenate([sent_rows, sent_grads], axis=1)
    moved = exchange(sent.reshape(experts, capacity, 3 * width), "expert")
    moved = moved.reshape(rows, 3 * width)
    mine, slot_grads = moved[:, : 2 * width], moved[:, 2 * width :]
    beside_rows = lax.ppermute(mine, "core", SWAP)

    partial = (dot(mine, w_mine) + dot(beside_rows, w_beside)).astype(BF)
    moved = exchange(partial.reshape(Z, rows // Z, 2 * part), "z")
    gate_up = jnp.sum(moved.astype(F32), axis=0)
    hidden = (jax.nn.silu(gate_up[:, :part]) * gate_up[:, part:]).astype(BF)

    spread = exchange(jnp.broadcast_to(hidden[None], (XH * Z,) + hidden.shape), ("xh", "z"))
    hid_mine = spread.reshape(XH, rows, part)
    hid_beside = lax.ppermute(hid_mine, "core", SWAP)

    def grads_of(hid):
        return lax.dot_general(
            hid, slot_grads, (((1,), (0,)), ((), ())), preferred_element_type=F32
        ).astype(BF)

    def outs_of(hid, down):
        return lax.dot_general(
            hid, down, (((0, 2), (0, 1)), ((), ())), preferred_element_type=F32
        )

    grads = jnp.stack([grads_of(hid_mine), grads_of(hid_beside)])
    grads = jnp.stack(pick(core, grads), axis=1)
    moved = exchange(grads.reshape(dps, hidden_units // dps, width), "dp")
    down = w_down[0].reshape(XH, CORE, part, width).transpose(1, 0, 2, 3)
    down_mine, down_beside = pick(core, down)
    outputs = (outs_of(hid_mine, down_mine) + outs_of(hid_beside, down_beside)).astype(BF)
    grad_share = jnp.sum(moved.astype(F32), axis=0)
    return outputs, grad_share[None]


def solution(mesh):
    dps, experts = mesh.shape["dp"], mesh.shape["expert"]
    fine = Mesh(
        mesh.devices.reshape(dps, experts, XH, Z, CORE), ("dp", "expert", "xh", "z", "core")
    )
    tensor = ("xh", "z", "core")
    in_specs = (
        P(("dp", "expert"), tensor),
        P(("dp", "expert"), tensor),
        P(("dp", "expert"), None),
        P(("dp", "expert"), None),
        P("expert", tensor, None),
        P("expert", None, tensor),
    )
    out_specs = (P(("dp", "expert"), tensor), P("expert", "dp", tensor))
    return jax.shard_map(
        per_device, mesh=fine, in_specs=in_specs, out_specs=out_specs, check_vma=False
    )
```

time: 172 us -> 140 us (0.81)
  waiting for transfers between devices: 49.4 us -> 22.8 us
  starting transfers between devices: 56.2 us -> 44.3 us
  blocking collectives: 51.4 us -> 58.9 us
    all_to_all x4 -> x2, waiting for transfers between devices: 49.4 us -> 9.93 us  [exchange(): return lax.all_to_all(pieces, axes, split_axis=0, concat_axis=0, tiled=True)]
    all_to_all x4 -> x2, starting transfers between devices: 44.6 us -> 10.7 us  [exchange(): return lax.all_to_all(pieces, axes, split_axis=0, concat_axis=0, tiled=True)]
    ppermute x1 -> x5, starting transfers between devices: 11.6 us -> 33.6 us  [the longest x1 8.37 us: per_device(): beside = lax.ppermute(theirs, 'core', SWAP)]
    all_to_all x2, blocking collectives: 42.5 us -> 58.9 us  [exchange(): return lax.all_to_all(pieces, axes, split_axis=0, concat_axis=0, tiled=True)]
    ppermute x1 -> x5, waiting for transfers between devices: 0.01 us -> 12.9 us  [the longest x1 10.2 us: per_device(): far = lax.ppermute(near_theirs, 'xh', SWAP)]
    all_gather x1 -> x0, blocking collectives: 8.91 us -> none  [per_device(): pair = lax.all_gather(hidden, 'xh', axis=0)]
    dot_general x5 -> x8, matrix products: 4.93 us -> 3.53 us  [the longest x2 1.41 us: outs_of(): lax.dot_general(hid, down, (((0, 2), (0, 1)), ((), ())), preferred_elemen...]
  transfers between devices with their start and end apart: 5 -> 7, of which waited for: 4 -> 4; matrix products, arithmetic and copies ran while one was open for 3% -> 6% of each run, Pallas kernels for 0% -> 0%
where the time goes in v2:
time: 140 us; the launch traced here: 139 us
  blocking collectives  58.9 us (42%)
  starting transfers between devices  44.3 us (32%)
  waiting for transfers between devices  22.8 us (16%)
  local copies, waits for them, and re-layouts  5.85 us (4%)
  matrix products  3.53 us (3%)
  other arithmetic  2.77 us (2%)
    all_to_all x2, blocking collectives, exchange(): return lax.all_to_all(pieces, axes, split_axis=0, concat_axis=0, tiled=True)  58.9 us
    all_to_all x2, starting transfers between devices, exchange(): return lax.all_to_all(pieces, axes, split_axis=0, concat_axis=0, tiled=True)  10.7 us
    ppermute x1, waiting for transfers between devices, per_device(): far = lax.ppermute(near_theirs, 'xh', SWAP)  10.2 us
    all_to_all x2, waiting for transfers between devices, exchange(): return lax.all_to_all(pieces, axes, split_axis=0, concat_axis=0, tiled=True)  9.93 us
    ppermute x1, starting transfers between devices, per_device(): beside = lax.ppermute(theirs, 'core', SWAP)  8.37 us
    ppermute x1, starting transfers between devices, per_device(): far_tokens = lax.ppermute(tokens, 'xh', SWAP)  8.07 us
    ppermute x1, starting transfers between devices, per_device(): hid_beside = lax.ppermute(hid_mine, 'core', SWAP)  7.49 us
    ppermute x1, starting transfers between devices, per_device(): far = lax.ppermute(near_theirs, 'xh', SWAP)  5.41 us
  transfers between devices with their start and end apart: 7, of which 4 were waited for; matrix products, arithmetic and copies ran while one was open for 6% of the time, Pallas kernels for 0%

profile of v2, /device:TPU:1, one launch (start us, length us, event | category | flops | bytes accessed | tf_op | source)
XLA Modules:
  0.0 139.2 jit_solution(15064117786261664205)
XLA Ops:
  0.6 0.0 copy-start
  0.6 0.0 copy-start.2
  0.7 8.1 %collective-permute-start = (bf16[128,128]{1,0:T(8,128)(2,1)}, bf16[128,128]{1,0:T(8,128)(2,1)S(1)}, u32[]{:S(2)}, u32[]{:S(2)}) collective-permute-start(bf16[128,128]{1,0:T(8,128)(2,1)} %param.6), channel_id=1, source_target_pairs={{0,16},{16,0},{1,17},{17,1},{2,18},{18,2},{3,19},{19,3},{4,20},{20... | collective-permute-start | bytes 98312 | tf_op jit(solution)/shard_map/ppermute | solution.py:47
  8.7 0.8 copy.62
  9.5 0.1 eq.58
  9.7 0.1 eq.54
  9.8 0.6 reduce-window.6
  10.4 0.2 slice_reduce_fusion
  10.7 0.1 fusion.29
  10.8 0.1 reduce_sum.48
  10.9 0.8 copy.65
  11.7 0.1 broadcast_in_dim.27
  11.8 0.1 copy.64
  11.9 0.7 multiply_add_fusion.1
  12.6 0.1 convert_reduce_fusion.2
  12.7 0.1 select_reduce_fusion
  12.8 0.0 copy-done
  12.8 0.2 fusion.1
  13.1 1.5 %copy.67 = bf16[1,128,3072]{1,2,0:T(8,128)(2,1)S(1)} copy(bf16[1,128,3072]{2,1,0:T(8,128)(2,1)} %param.10) | data formatting | bytes 1572864 | tf_op args[4]
  14.6 0.0 collective-permute-done
  14.6 0.0 copy-done.2
  14.6 0.3 convolution_convert_fusion
  14.9 0.9 copy.66
  15.8 7.3 %all-to-all-start = ((bf16[8,64,384]{2,1,0:T(8,128)(2,1)}), bf16[8,64,384]{2,1,0:T(8,128)(2,1)S(1)}, u32[]{:S(2)}, u32[]{:S(2)}) async-start(bf16[8,64,384]{2,1,0:T(8,128)(2,1)} %bitcast.2), calls=%async_computation | async-start | bytes 786432 | tf_op jit(solution)/shard_map/all_to_all | solution.py:14
  23.1 0.1 broadcast_select_fusion.1
  23.2 8.4 %collective-permute-start.1 = (bf16[2,128,768]{1,2,0:T(8,128)(2,1)S(1)}, bf16[2,128,768]{1,2,0:T(8,128)(2,1)S(1)}, u32[]{:S(2)}, u32[]{:S(2)}) collective-permute-start(bf16[2,128,768]{1,2,0:T(8,128)(2,1)S(1)} %bitcast.90), channel_id=1, source_target_pairs={{0,1},{1,0},{2,3},{3,2},{4,5},{5,4},{6,7},{7,6},{8,9},{9,8},{10,11... | collective-permute-start | bytes 1179656 | tf_op jit(solution)/shard_map/ppermute | solution.py:52
  31.6 1.3 collective-permute-done.1
  32.9 0.1 fusion.3
  33.0 5.4 %collective-permute-start.2 = (bf16[2,128,768]{1,2,0:T(8,128)(2,1)S(1)}, bf16[2,128,768]{1,2,0:T(8,128)(2,1)S(1)}, u32[]{:S(2)}, u32[]{:S(2)}) collective-permute-start(bf16[2,128,768]{1,2,0:T(8,128)(2,1)S(1)} %fusion.3), channel_id=1, source_target_pairs={{0,16},{16,0},{1,17},{17,1},{2,18},{18,2},{3,19},{19,3},{4,20},{20... | collective-permute-start | bytes 1179656 | tf_op jit(solution)/shard_map/ppermute | solution.py:55
  38.4 0.1 bitcast_select_fusion.1
  38.5 0.0 all-to-all-done
  38.5 4.3 %collective-permute-start.3 = (bf16[512,256]{1,0:T(8,128)(2,1)S(1)}, bf16[512,256]{1,0:T(8,128)(2,1)S(1)}, u32[]{:S(2)}, u32[]{:S(2)}) collective-permute-start(bf16[512,256]{1,0:T(8,128)(2,1)S(1)} %slice.75), channel_id=1, source_target_pairs={{0,1},{1,0},{2,3},{3,2},{4,5},{5,4},{6,7},{7,6},{8,9},{9,8},{10,11... | collective-permute-start | bytes 786440 | tf_op jit(solution)/shard_map/ppermute | solution.py:70
  42.8 10.2 %collective-permute-done.2 = bf16[2,128,768]{1,2,0:T(8,128)(2,1)S(1)} collective-permute-done((bf16[2,128,768]{1,2,0:T(8,128)(2,1)S(1)}, bf16[2,128,768]{1,2,0:T(8,128)(2,1)S(1)}, u32[]{:S(2)}, u32[]{:S(2)}) %collective-permute-start.2) | collective-permute-done | bytes 393248 | tf_op jit(solution)/shard_map/ppermute | solution.py:55
  53.0 0.0 collective-permute-done.3
  53.0 0.4 fusion.8
  53.4 0.4 add_convert_fusion
  53.8 38.1 %all_to_all.20 = bf16[8,64,768]{2,1,0:T(8,128)(2,1)S(1)} all-to-all(bf16[8,64,768]{2,1,0:T(8,128)(2,1)S(1)} %bitcast.86), channel_id=1, replica_groups=mesh['dp'=4,'expert'=8,'xh'=2,'z'=8,'core'=2] {'z'}, dimensions={0} | all-to-all | bytes 1572864 | tf_op jit(solution)/shard_map/all_to_all | solution.py:14
  91.9 0.1 convert_reduce_fusion
  92.1 0.1 broadcast_in_dim.30
  92.2 20.8 %all_to_all.21 = bf16[16,64,384]{2,1,0:T(8,128)(2,1)S(1)} all-to-all(bf16[16,64,384]{2,1,0:T(8,128)(2,1)S(1)} %broadcast_in_dim.30), channel_id=1, replica_groups=mesh['dp'=4,'expert'=8,'xh'=2,'z'=8,'core'=2] {'xh','z'}, dimensions={0} | all-to-all | bytes 1572864 | tf_op jit(solution)/shard_map/all_to_all | solution.py:14
  112.9 7.5 %collective-permute-start.4 = (bf16[2,512,384]{2,1,0:T(8,128)(2,1)S(1)}, bf16[2,512,384]{2,1,0:T(8,128)(2,1)S(1)}, u32[]{:S(2)}, u32[]{:S(2)}) collective-permute-start(bf16[2,512,384]{2,1,0:T(8,128)(2,1)S(1)} %bitcast.82), channel_id=1, source_target_pairs={{0,1},{1,0},{2,3},{3,2},{4,5},{5,4},{6,7},{7,6},{8,9},{9,8},{10,11... | collective-permute-start | bytes 2359304 | tf_op jit(solution)/shard_map/ppermute | solution.py:79
  120.4 0.4 convolution_convert_fusion.2
  120.9 0.0 copy-start.1
  120.9 1.5 %collective-permute-done.4 = bf16[2,512,384]{2,1,0:T(8,128)(2,1)S(1)} collective-permute-done((bf16[2,512,384]{2,1,0:T(8,128)(2,1)S(1)}, bf16[2,512,384]{2,1,0:T(8,128)(2,1)S(1)}, u32[]{:S(2)}, u32[]{:S(2)}) %collective-permute-start.4) | collective-permute-done | bytes 786464 | tf_op jit(solution)/shard_map/ppermute | solution.py:79
  122.3 0.4 select_bitcast_fusion.1
  122.8 0.8 copy.77
  123.6 3.5 %all-to-all-start.3 = ((bf16[4,384,128]{2,1,0:T(8,128)(2,1)}), bf16[4,384,128]{2,1,0:T(8,128)(2,1)S(1)}, u32[]{:S(2)}, u32[]{:S(2)}) async-start(bf16[4,384,128]{2,1,0:T(8,128)(2,1)} %bitcast.29), calls=%async_computation.3 | async-start | bytes 786432 | tf_op jit(solution)/shard_map/all_to_all | solution.py:14
  127.0 0.0 copy-done.1
  127.1 0.4 convolution_bitcast_fusion.1
  127.5 1.0 fusion.2
  128.5 9.9 %all-to-all-done.3 = bf16[4,384,128]{2,1,0:T(8,128)(2,1)S(1)} async-done(((bf16[4,384,128]{2,1,0:T(8,128)(2,1)}), bf16[4,384,128]{2,1,0:T(8,128)(2,1)S(1)}, u32[]{:S(2)}, u32[]{:S(2)}) %all-to-all-start.3) | async-done | bytes 393248 | tf_op jit(solution)/shard_map/all_to_all | solution.py:14
  138.4 0.7 convert_reduce_fusion.1
  (13 shorter events, 0.3 us)
Async XLA Ops:
  0.6 12.2 %copy-start = (bf16[128,128]{1,0:T(8,128)(2,1)S(1)}, bf16[128,128]{1,0:T(8,128)(2,1)}, u32[]{:S(2)}) copy-start(bf16[128,128]{1,0:T(8,128)(2,1)} %param.7) | copy-start | bytes 98308
  0.6 13.9 %copy-start.2 = (bf16[128,128]{1,0:T(8,128)(2,1)S(1)}, bf16[128,128]{1,0:T(8,128)(2,1)}, u32[]{:S(2)}) copy-start(bf16[128,128]{1,0:T(8,128)(2,1)} %param.6) | copy-start | bytes 98308
  0.7 13.9 %collective-permute-start = (bf16[128,128]{1,0:T(8,128)(2,1)}, bf16[128,128]{1,0:T(8,128)(2,1)S(1)}, u32[]{:S(2)}, u32[]{:S(2)}) collective-permute-start(bf16[128,128]{1,0:T(8,128)(2,1)} %param.6), channel_id=1, source_target_pairs={{0,16},{16,0},{1,17},{17,1},{2,18},{18,2},{3,19},{19,3},{4,20},{20... | collective-permute-start | bytes 98312 | tf_op jit(solution)/shard_map/ppermute | solution.py:47
  15.8 22.6 %all-to-all-start = ((bf16[8,64,384]{2,1,0:T(8,128)(2,1)}), bf16[8,64,384]{2,1,0:T(8,128)(2,1)S(1)}, u32[]{:S(2)}, u32[]{:S(2)}) async-start(bf16[8,64,384]{2,1,0:T(8,128)(2,1)} %bitcast.2), calls=%async_computation | async-start | bytes 786432 | tf_op jit(solution)/shard_map/all_to_all | solution.py:14
  23.2 9.7 %collective-permute-start.1 = (bf16[2,128,768]{1,2,0:T(8,128)(2,1)S(1)}, bf16[2,128,768]{1,2,0:T(8,128)(2,1)S(1)}, u32[]{:S(2)}, u32[]{:S(2)}) collective-permute-start(bf16[2,128,768]{1,2,0:T(8,128)(2,1)S(1)} %bitcast.90), channel_id=1, source_target_pairs={{0,1},{1,0},{2,3},{3,2},{4,5},{5,4},{6,7},{7,6},{8,9},{9,8},{10,11... | collective-permute-start | bytes 1179656 | tf_op jit(solution)/shard_map/ppermute | solution.py:52
  33.0 20.0 %collective-permute-start.2 = (bf16[2,128,768]{1,2,0:T(8,128)(2,1)S(1)}, bf16[2,128,768]{1,2,0:T(8,128)(2,1)S(1)}, u32[]{:S(2)}, u32[]{:S(2)}) collective-permute-start(bf16[2,128,768]{1,2,0:T(8,128)(2,1)S(1)} %fusion.3), channel_id=1, source_target_pairs={{0,16},{16,0},{1,17},{17,1},{2,18},{18,2},{3,19},{19,3},{4,20},{20... | collective-permute-start | bytes 1179656 | tf_op jit(solution)/shard_map/ppermute | solution.py:55
  38.5 14.5 %collective-permute-start.3 = (bf16[512,256]{1,0:T(8,128)(2,1)S(1)}, bf16[512,256]{1,0:T(8,128)(2,1)S(1)}, u32[]{:S(2)}, u32[]{:S(2)}) collective-permute-start(bf16[512,256]{1,0:T(8,128)(2,1)S(1)} %slice.75), channel_id=1, source_target_pairs={{0,1},{1,0},{2,3},{3,2},{4,5},{5,4},{6,7},{7,6},{8,9},{9,8},{10,11... | collective-permute-start | bytes 786440 | tf_op jit(solution)/shard_map/ppermute | solution.py:70
  112.9 9.4 %collective-permute-start.4 = (bf16[2,512,384]{2,1,0:T(8,128)(2,1)S(1)}, bf16[2,512,384]{2,1,0:T(8,128)(2,1)S(1)}, u32[]{:S(2)}, u32[]{:S(2)}) collective-permute-start(bf16[2,512,384]{2,1,0:T(8,128)(2,1)S(1)} %bitcast.82), channel_id=1, source_target_pairs={{0,1},{1,0},{2,3},{3,2},{4,5},{5,4},{6,7},{7,6},{8,9},{9,8},{10,11... | collective-permute-start | bytes 2359304 | tf_op jit(solution)/shard_map/ppermute | solution.py:79
  120.9 6.2 %copy-start.1 = (bf16[1,1536,128]{2,1,0:T(8,128)(2,1)S(1)}, bf16[1,1536,128]{2,1,0:T(8,128)(2,1)}, u32[]{:S(2)}) copy-start(bf16[1,1536,128]{2,1,0:T(8,128)(2,1)} %param.11) | copy-start | bytes 1179652
  123.6 14.9 %all-to-all-start.3 = ((bf16[4,384,128]{2,1,0:T(8,128)(2,1)}), bf16[4,384,128]{2,1,0:T(8,128)(2,1)S(1)}, u32[]{:S(2)}, u32[]{:S(2)}) async-start(bf16[4,384,128]{2,1,0:T(8,128)(2,1)} %bitcast.29), calls=%async_computation.3 | async-start | bytes 786432 | tf_op jit(solution)/shard_map/all_to_all | solution.py:14

commit v3 on v2

--- a/solution.py
+++ b/solution.py
@@ -5,8 +5,9 @@
 
 BF = jnp.bfloat16
 F32 = jnp.float32
-XH, Z, CORE = 2, 8, 2
-QUARTERS = XH * CORE
+XH, ZH, ZL, CORE = 2, 4, 2, 2
+QUARTERS = ZL * CORE
+ROWS_AXES = ("xh", "zh")
 SWAP = [(0, 1), (1, 0)]
 
 
@@ -42,40 +43,43 @@
     hidden_units = w_gate_up.shape[2] // 2
     part = hidden_units // QUARTERS
     core = lax.axis_index("core")
-    xh = lax.axis_index("xh")
+    zl = lax.axis_index("zl")
 
-    far_tokens = lax.ppermute(tokens, "xh", SWAP)
+    far_tokens = lax.ppermute(tokens, "zl", SWAP)
 
-    blocks = w_gate_up[0].reshape(width, 2, XH, CORE, part).transpose(3, 2, 0, 1, 4)
-    blocks = blocks.reshape(CORE, XH, width, 2 * part)
-    own, theirs = pick(core, blocks)
-    beside = lax.ppermute(theirs, "core", SWAP)
-    near = jnp.stack([own, beside], axis=1)
-    near_own, near_theirs = pick(xh, near)
-    far = lax.ppermute(near_theirs, "xh", SWAP)
-    w_mine = jnp.concatenate([near_own[0], far[0]], axis=0)
-    w_beside = jnp.concatenate([near_own[1], far[1]], axis=0)
+    blocks = w_gate_up[0].reshape(width, 2, ZL, CORE, part).transpose(2, 3, 0, 1, 4)
+    blocks = blocks.reshape(ZL, CORE, width, 2 * part)
+    own, theirs = pick(zl, blocks)
+    far = lax.ppermute(theirs, "zl", SWAP)
+    own_mine, own_theirs = pick(core, own)
+    far_mine, far_theirs = pick(core, far)
+    w_mine = jnp.concatenate([own_mine, far_mine], axis=0)
+    w_beside = lax.ppermute(jnp.concatenate([own_theirs, far_theirs], axis=0), "core", SWAP)
 
     matches = slots_of(routes, experts, capacity)
     select = jnp.sum(
         matches.reshape(rows, tok_rows, top_count).astype(F32), axis=2
     ).astype(BF)
     weights_slot = jnp.sum(jnp.where(matches, route_weight.reshape(1, -1), 0.0), axis=1)
-    sent_grads = (dot(select, cotangent) * weights_slot[:, None]).astype(BF)
-    sent_rows = dot(select, jnp.concatenate([tokens, far_tokens], axis=1)).astype(BF)
-    sent = jnp.concatenate([sent_rows, sent_grads], axis=1)
+    sent = dot(select, jnp.concatenate([tokens, far_tokens, cotangent], axis=1))
+    is_token = jnp.arange(3 * width, dtype=jnp.int32)[None, :] < 2 * width
+    sent = (sent * jnp.where(is_token, 1.0, weights_slot[:, None])).astype(BF)
     moved = exchange(sent.reshape(experts, capacity, 3 * width), "expert")
     moved = moved.reshape(rows, 3 * width)
     mine, slot_grads = moved[:, : 2 * width], moved[:, 2 * width :]
     beside_rows = lax.ppermute(mine, "core", SWAP)
 
     partial = (dot(mine, w_mine) + dot(beside_rows, w_beside)).astype(BF)
-    moved = exchange(partial.reshape(Z, rows // Z, 2 * part), "z")
+    groups = XH * ZH
+    moved = exchange(partial.reshape(groups, rows // groups, 2 * part), ROWS_AXES)
     gate_up = jnp.sum(moved.astype(F32), axis=0)
     hidden = (jax.nn.silu(gate_up[:, :part]) * gate_up[:, part:]).astype(BF)
 
-    spread = exchange(jnp.broadcast_to(hidden[None], (XH * Z,) + hidden.shape), ("xh", "z"))
-    hid_mine = spread.reshape(XH, rows, part)
+    spread = exchange(
+        jnp.broadcast_to(hidden[None], (groups * ZL,) + hidden.shape), ROWS_AXES + ("zl",)
+    )
+    spread = spread.reshape(groups, ZL, rows // groups, part).transpose(1, 0, 2, 3)
+    hid_mine = spread.reshape(ZL, rows, part)
     hid_beside = lax.ppermute(hid_mine, "core", SWAP)
 
     def grads_of(hid):
@@ -91,7 +95,7 @@
     grads = jnp.stack([grads_of(hid_mine), grads_of(hid_beside)])
     grads = jnp.stack(pick(core, grads), axis=1)
     moved = exchange(grads.reshape(dps, hidden_units // dps, width), "dp")
-    down = w_down[0].reshape(XH, CORE, part, width).transpose(1, 0, 2, 3)
+    down = w_down[0].reshape(ZL, CORE, part, width).transpose(1, 0, 2, 3)
     down_mine, down_beside = pick(core, down)
     outputs = (outs_of(hid_mine, down_mine) + outs_of(hid_beside, down_beside)).astype(BF)
     grad_share = jnp.sum(moved.astype(F32), axis=0)
@@ -101,9 +105,10 @@
 def solution(mesh):
     dps, experts = mesh.shape["dp"], mesh.shape["expert"]
     fine = Mesh(
-        mesh.devices.reshape(dps, experts, XH, Z, CORE), ("dp", "expert", "xh", "z", "core")
+        mesh.devices.reshape(dps, experts, XH, ZH, ZL, CORE),
+        ("dp", "expert", "xh", "zh", "zl", "core"),
     )
-    tensor = ("xh", "z", "core")
+    tensor = ("xh", "zh", "zl", "core")
     in_specs = (
         P(("dp", "expert"), tensor),
         P(("dp", "expert"), tensor),

time: 140 us -> 137 us (0.979)
  waiting for transfers between devices: 22.8 us -> 12.1 us
  blocking collectives: 58.9 us -> 67.2 us
  local copies, waits for them, and re-layouts: 5.85 us -> 3.6 us
  starting transfers between devices: 44.3 us -> 46.1 us
    ppermute x3, waiting for transfers between devices: 11.4 us -> 0.01 us  [the longest x1 0.01 us: per_device(): far_tokens = lax.ppermute(tokens, 'zl', SWAP)]
    all_to_all x2, blocking collectives: 58.9 us -> 67.2 us  [exchange(): return lax.all_to_all(pieces, axes, split_axis=0, concat_axis=0, tiled=True)]
    ppermute x1, starting transfers between devices: 4.26 us -> 11.5 us  [per_device(): beside_rows = lax.ppermute(mine, 'core', SWAP)]
    ppermute x3, starting transfers between devices: 21.9 us -> 18.1 us  [the longest x1 10.4 us: per_device(): lax.ppermute(jnp.concatenate([own_theirs, far_theirs], axis=0), 'core', S...]
    ppermute x1, starting transfers between devices: 7.49 us -> 4.92 us  [per_device(): hid_beside = lax.ppermute(hid_mine, 'core', SWAP)]
    unnamed x9 -> x13, local copies, waits for them, and re-layouts: 3.1 us -> 1.76 us
  transfers between devices with their start and end apart: 7 -> 7, of which waited for: 4 -> 4; matrix products, arithmetic and copies ran while one was open for 6% -> 5% of each run, Pallas kernels for 0% -> 0%
where the time goes in v3:
time: 137 us; the launch traced here: 136 us
  blocking collectives  67.2 us (49%)
  starting transfers between devices  46.1 us (34%)
  waiting for transfers between devices  12.1 us (9%)
  matrix products  4.05 us (3%)
  local copies, waits for them, and re-layouts  3.6 us (3%)
  other arithmetic  2.04 us (1%)
    all_to_all x2, blocking collectives, exchange(): return lax.all_to_all(pieces, axes, split_axis=0, concat_axis=0, tiled=True)  67.2 us
    all_to_all x2, starting transfers between devices, exchange(): return lax.all_to_all(pieces, axes, split_axis=0, concat_axis=0, tiled=True)  11.6 us
    ppermute x1, starting transfers between devices, per_device(): beside_rows = lax.ppermute(mine, 'core', SWAP)  11.5 us
    ppermute x1, starting transfers between devices, per_device(): lax.ppermute(jnp.concatenate([own_theirs, far_theirs], axis=0), 'core', S...  10.4 us
    all_to_all x2, waiting for transfers between devices, exchange(): return lax.all_to_all(pieces, axes, split_axis=0, concat_axis=0, tiled=True)  9.93 us
    ppermute x1, starting transfers between devices, per_device(): far_tokens = lax.ppermute(tokens, 'zl', SWAP)  5.74 us
    ppermute x1, starting transfers between devices, per_device(): hid_beside = lax.ppermute(hid_mine, 'core', SWAP)  4.92 us
  transfers between devices with their start and end apart: 7, of which 4 were waited for; matrix products, arithmetic and copies ran while one was open for 5% of the time, Pallas kernels for 0%

profile of v3, /device:TPU:1, one launch (start us, length us, event | category | flops | bytes accessed | tf_op | source)
XLA Modules:
  0.0 136.0 jit_solution(13009782246967514319)
XLA Ops:
  0.6 5.7 %collective-permute-start = (bf16[128,128]{1,0:T(8,128)(2,1)}, bf16[128,128]{1,0:T(8,128)(2,1)S(1)}, u32[]{:S(2)}, u32[]{:S(2)}) collective-permute-start(bf16[128,128]{1,0:T(8,128)(2,1)} %param.6), channel_id=1, source_target_pairs={{0,2},{2,0},{1,3},{3,1},{4,6},{6,4},{5,7},{7,5},{8,10},{10,8},{9,1... | collective-permute-start | bytes 98312 | tf_op jit(solution)/shard_map/ppermute | solution.py:48
  6.4 1.5 %copy.51 = bf16[1,128,3072]{1,2,0:T(8,128)(2,1)S(1)} copy(bf16[1,128,3072]{2,1,0:T(8,128)(2,1)} %param.10) | data formatting | bytes 1572864 | tf_op args[4]
  7.9 0.0 copy-start.1
  7.9 0.0 copy-start.2
  7.9 0.0 copy-start.3
  7.9 0.0 copy-start.4
  7.9 0.1 broadcast_select_fusion.1
  8.0 1.9 %collective-permute-start.1 = (bf16[2,128,768]{1,2,0:T(8,128)(2,1)S(1)}, bf16[2,128,768]{1,2,0:T(8,128)(2,1)S(1)}, u32[]{:S(2)}, u32[]{:S(2)}) collective-permute-start(bf16[2,128,768]{1,2,0:T(8,128)(2,1)S(1)} %bitcast.75), channel_id=1, source_target_pairs={{0,2},{2,0},{1,3},{3,1},{4,6},{6,4},{5,7},{7,5},{8,10},{10,8},{9,1... | collective-permute-start | bytes 1179656 | tf_op jit(solution)/shard_map/ppermute | solution.py:53
  10.0 0.0 copy-done.1
  10.0 0.1 copy.47
  10.1 0.1 eq.59
  10.2 0.1 eq.55
  10.4 0.6 reduce-window.6
  11.0 0.2 slice_reduce_fusion
  11.2 0.1 fusion.25
  11.3 0.1 reduce_sum.48
  11.5 0.0 copy-done.2
  11.5 0.1 copy.50
  11.6 0.1 broadcast_in_dim.50
  11.8 0.1 copy.49
  11.8 0.1 convert_reduce_fusion.2
  11.9 0.1 select_reduce_fusion
  12.1 0.0 collective-permute-done
  12.1 0.0 copy-done.3
  12.1 0.0 copy-done.4
  12.1 1.0 fusion
  13.1 7.3 %all-to-all-start = ((bf16[8,64,384]{2,1,0:T(8,128)(2,1)}), bf16[8,64,384]{2,1,0:T(8,128)(2,1)S(1)}, u32[]{:S(2)}, u32[]{:S(2)}) async-start(bf16[8,64,384]{2,1,0:T(8,128)(2,1)} %bitcast.2), calls=%async_computation | async-start | bytes 786432 | tf_op jit(solution)/shard_map/all_to_all | solution.py:15
  20.4 0.0 collective-permute-done.1
  20.5 10.4 %collective-permute-start.3 = (bf16[256,768]{0,1:T(8,128)(2,1)S(1)}, bf16[256,768]{0,1:T(8,128)(2,1)S(1)}, u32[]{:S(2)}, u32[]{:S(2)}) collective-permute-start(bf16[256,768]{0,1:T(8,128)(2,1)S(1)} %pad_maximum_fusion), channel_id=1, source_target_pairs={{0,1},{1,0},{2,3},{3,2},{4,5},{5,4},{6,7},{7,6},{8,9},{9,8},{10,11... | collective-permute-start | bytes 1179656 | tf_op jit(solution)/shard_map/ppermute | solution.py:57
  31.0 0.2 all-to-all-done
  31.1 11.5 %collective-permute-start.2 = (bf16[512,256]{1,0:T(8,128)(2,1)S(1)}, bf16[512,256]{1,0:T(8,128)(2,1)S(1)}, u32[]{:S(2)}, u32[]{:S(2)}) collective-permute-start(bf16[512,256]{1,0:T(8,128)(2,1)S(1)} %slice.69), channel_id=1, source_target_pairs={{0,1},{1,0},{2,3},{3,2},{4,5},{5,4},{6,7},{7,6},{8,9},{9,8},{10,11... | collective-permute-start | bytes 786440 | tf_op jit(solution)/shard_map/ppermute | solution.py:70
  42.7 0.4 fusion.3
  43.1 0.0 collective-permute-done.3
  43.1 0.7 collective-permute-done.2
  43.8 0.4 add_convert_fusion
  44.2 35.0 %all_to_all.20 = bf16[8,64,768]{2,1,0:T(8,128)(2,1)S(1)} all-to-all(bf16[8,64,768]{2,1,0:T(8,128)(2,1)S(1)} %bitcast.71), channel_id=1, replica_groups=mesh['dp'=4,'expert'=8,'xh'=2,'zh'=4,'zl'=2,'core'=2] {'xh','zh'}, dimensions={0} | all-to-all | bytes 1572864 | tf_op jit(solution)/shard_map/all_to_all | solution.py:15
  79.2 0.1 convert_reduce_fusion
  79.3 0.1 broadcast_in_dim.54
  79.4 32.2 %all_to_all.21 = bf16[16,64,384]{2,1,0:T(8,128)(2,1)S(1)} all-to-all(bf16[16,64,384]{2,1,0:T(8,128)(2,1)S(1)} %broadcast_in_dim.54), channel_id=1, replica_groups=mesh['dp'=4,'expert'=8,'xh'=2,'zh'=4,'zl'=2,'core'=2] {'xh','zh','zl'}, dimensions={0} | all-to-all | bytes 1572864 | tf_op jit(solution)/shard_map/all_to_all | solution.py:15
  111.6 0.1 copy.53
  111.7 4.9 %collective-permute-start.4 = (bf16[2,512,384]{2,1,0:T(8,128)(2,1)S(1)}, bf16[2,512,384]{2,1,0:T(8,128)(2,1)S(1)}, u32[]{:S(2)}, u32[]{:S(2)}) collective-permute-start(bf16[2,512,384]{2,1,0:T(8,128)(2,1)S(1)} %bitcast.66), channel_id=1, source_target_pairs={{0,1},{1,0},{2,3},{3,2},{4,5},{5,4},{6,7},{7,6},{8,9},{9,8},{10,11... | collective-permute-start | bytes 2359304 | tf_op jit(solution)/shard_map/ppermute | solution.py:83
  116.6 0.4 convolution_convert_fusion.1
  117.0 0.0 copy-start
  117.1 1.5 %collective-permute-done.4 = bf16[2,512,384]{2,1,0:T(8,128)(2,1)S(1)} collective-permute-done((bf16[2,512,384]{2,1,0:T(8,128)(2,1)S(1)}, bf16[2,512,384]{2,1,0:T(8,128)(2,1)S(1)}, u32[]{:S(2)}, u32[]{:S(2)}) %collective-permute-start.4) | collective-permute-done | bytes 786464 | tf_op jit(solution)/shard_map/ppermute | solution.py:83
  118.5 0.4 select_bitcast_fusion.1
  119.0 0.8 copy.57
  119.7 4.3 %all-to-all-start.3 = ((bf16[4,384,128]{2,1,0:T(8,128)(2,1)}), bf16[4,384,128]{2,1,0:T(8,128)(2,1)S(1)}, u32[]{:S(2)}, u32[]{:S(2)}) async-start(bf16[4,384,128]{2,1,0:T(8,128)(2,1)} %bitcast.25), calls=%async_computation.3 | async-start | bytes 786432 | tf_op jit(solution)/shard_map/all_to_all | solution.py:15
  124.0 0.0 copy-done
  124.1 0.4 convolution_bitcast_fusion.1
  124.5 1.0 fusion.2
  125.5 9.8 %all-to-all-done.3 = bf16[4,384,128]{2,1,0:T(8,128)(2,1)S(1)} async-done(((bf16[4,384,128]{2,1,0:T(8,128)(2,1)}), bf16[4,384,128]{2,1,0:T(8,128)(2,1)S(1)}, u32[]{:S(2)}, u32[]{:S(2)}) %all-to-all-start.3) | async-done | bytes 393248 | tf_op jit(solution)/shard_map/all_to_all | solution.py:15
  135.3 0.7 convert_reduce_fusion.1
  (14 shorter events, 0.3 us)
Async XLA Ops:
  0.6 11.5 %collective-permute-start = (bf16[128,128]{1,0:T(8,128)(2,1)}, bf16[128,128]{1,0:T(8,128)(2,1)S(1)}, u32[]{:S(2)}, u32[]{:S(2)}) collective-permute-start(bf16[128,128]{1,0:T(8,128)(2,1)} %param.6), channel_id=1, source_target_pairs={{0,2},{2,0},{1,3},{3,1},{4,6},{6,4},{5,7},{7,5},{8,10},{10,8},{9,1... | collective-permute-start | bytes 98312 | tf_op jit(solution)/shard_map/ppermute | solution.py:48
  7.9 2.1 %copy-start.1 = (s32[128,2]{0,1:T(2,128)S(1)}, s32[128,2]{0,1:T(2,128)}, u32[]{:S(2)}) copy-start(s32[128,2]{0,1:T(2,128)} %param.8) | copy-start | bytes 3076
  7.9 3.6 %copy-start.2 = (f32[128,2]{0,1:T(2,128)S(1)}, f32[128,2]{0,1:T(2,128)}, u32[]{:S(2)}) copy-start(f32[128,2]{0,1:T(2,128)} %param.9) | copy-start | bytes 3076
  7.9 4.2 %copy-start.3 = (bf16[128,128]{1,0:T(8,128)(2,1)S(1)}, bf16[128,128]{1,0:T(8,128)(2,1)}, u32[]{:S(2)}) copy-start(bf16[128,128]{1,0:T(8,128)(2,1)} %param.7) | copy-start | bytes 98308
  7.9 4.2 %copy-start.4 = (bf16[128,128]{1,0:T(8,128)(2,1)S(1)}, bf16[128,128]{1,0:T(8,128)(2,1)}, u32[]{:S(2)}) copy-start(bf16[128,128]{1,0:T(8,128)(2,1)} %param.6) | copy-start | bytes 98308
  8.0 12.4 %collective-permute-start.1 = (bf16[2,128,768]{1,2,0:T(8,128)(2,1)S(1)}, bf16[2,128,768]{1,2,0:T(8,128)(2,1)S(1)}, u32[]{:S(2)}, u32[]{:S(2)}) collective-permute-start(bf16[2,128,768]{1,2,0:T(8,128)(2,1)S(1)} %bitcast.75), channel_id=1, source_target_pairs={{0,2},{2,0},{1,3},{3,1},{4,6},{6,4},{5,7},{7,5},{8,10},{10,8},{9,1... | collective-permute-start | bytes 1179656 | tf_op jit(solution)/shard_map/ppermute | solution.py:53
  13.1 18.0 %all-to-all-start = ((bf16[8,64,384]{2,1,0:T(8,128)(2,1)}), bf16[8,64,384]{2,1,0:T(8,128)(2,1)S(1)}, u32[]{:S(2)}, u32[]{:S(2)}) async-start(bf16[8,64,384]{2,1,0:T(8,128)(2,1)} %bitcast.2), calls=%async_computation | async-start | bytes 786432 | tf_op jit(solution)/shard_map/all_to_all | solution.py:15
  20.5 22.5 %collective-permute-start.3 = (bf16[256,768]{0,1:T(8,128)(2,1)S(1)}, bf16[256,768]{0,1:T(8,128)(2,1)S(1)}, u32[]{:S(2)}, u32[]{:S(2)}) collective-permute-start(bf16[256,768]{0,1:T(8,128)(2,1)S(1)} %pad_maximum_fusion), channel_id=1, source_target_pairs={{0,1},{1,0},{2,3},{3,2},{4,5},{5,4},{6,7},{7,6},{8,9},{9,8},{10,11... | collective-permute-start | bytes 1179656 | tf_op jit(solution)/shard_map/ppermute | solution.py:57
  31.1 12.6 %collective-permute-start.2 = (bf16[512,256]{1,0:T(8,128)(2,1)S(1)}, bf16[512,256]{1,0:T(8,128)(2,1)S(1)}, u32[]{:S(2)}, u32[]{:S(2)}) collective-permute-start(bf16[512,256]{1,0:T(8,128)(2,1)S(1)} %slice.69), channel_id=1, source_target_pairs={{0,1},{1,0},{2,3},{3,2},{4,5},{5,4},{6,7},{7,6},{8,9},{9,8},{10,11... | collective-permute-start | bytes 786440 | tf_op jit(solution)/shard_map/ppermute | solution.py:70
  111.7 6.8 %collective-permute-start.4 = (bf16[2,512,384]{2,1,0:T(8,128)(2,1)S(1)}, bf16[2,512,384]{2,1,0:T(8,128)(2,1)S(1)}, u32[]{:S(2)}, u32[]{:S(2)}) collective-permute-start(bf16[2,512,384]{2,1,0:T(8,128)(2,1)S(1)} %bitcast.66), channel_id=1, source_target_pairs={{0,1},{1,0},{2,3},{3,2},{4,5},{5,4},{6,7},{7,6},{8,9},{9,8},{10,11... | collective-permute-start | bytes 2359304 | tf_op jit(solution)/shard_map/ppermute | solution.py:83
  117.0 7.0 %copy-start = (bf16[1,1536,128]{2,1,0:T(8,128)(2,1)S(1)}, bf16[1,1536,128]{2,1,0:T(8,128)(2,1)}, u32[]{:S(2)}) copy-start(bf16[1,1536,128]{2,1,0:T(8,128)(2,1)} %param.11) | copy-start | bytes 1179652
  119.7 15.5 %all-to-all-start.3 = ((bf16[4,384,128]{2,1,0:T(8,128)(2,1)}), bf16[4,384,128]{2,1,0:T(8,128)(2,1)S(1)}, u32[]{:S(2)}, u32[]{:S(2)}) async-start(bf16[4,384,128]{2,1,0:T(8,128)(2,1)} %bitcast.25), calls=%async_computation.3 | async-start | bytes 786432 | tf_op jit(solution)/shard_map/all_to_all | solution.py:15

commit v4 on v2

v4 whole, which is shorter than its diff:
```python
import jax
import jax.numpy as jnp
from jax import lax
from jax.sharding import Mesh, PartitionSpec as P

BF = jnp.bfloat16
F32 = jnp.float32
XH, Z, CORE = 2, 8, 2
QUARTERS = XH * CORE
SWAP = [(0, 1), (1, 0)]


def exchange(pieces, axes):
    return lax.all_to_all(pieces, axes, split_axis=0, concat_axis=0, tiled=True)


def dot(a, b):
    return jnp.dot(a, b, preferred_element_type=F32)


def pick(index, pair):
    first = index == 0
    return jnp.where(first, pair[0], pair[1]), jnp.where(first, pair[1], pair[0])


def slots_of(routes, experts, capacity):
    flat = routes.reshape(-1)
    onehot = (flat[:, None] == jnp.arange(experts, dtype=jnp.int32)[None, :]).astype(jnp.int32)
    before = jnp.cumsum(onehot, axis=0) - onehot
    slot = jnp.sum(before * onehot, axis=1)
    target = flat * capacity + slot
    return jnp.arange(experts * capacity, dtype=jnp.int32)[:, None] == target[None, :]


def after(index, array):
    return index + jnp.minimum(jnp.abs(array[0, 0]).astype(jnp.int32), 0)


def to_quarters(blocks, xh, core):
    near, sent = pick(xh, blocks)
    far = lax.ppermute(sent, "xh", SWAP)
    near_mine, near_sent = pick(core, near)
    far_mine, far_sent = pick(core, far)
    mine = jnp.stack([near_mine, far_mine])
    beside = lax.ppermute(jnp.stack([near_sent, far_sent]), "core", SWAP)
    return mine, beside


def per_device(tokens, cotangent, routes, route_weight, w_gate_up, w_down):
    tok_rows, width = tokens.shape
    experts = lax.axis_size("expert")
    dps = lax.axis_size("dp")
    top_count = routes.shape[1]
    capacity = min(tok_rows, 2 * tok_rows * top_count // experts)
    rows = experts * capacity
    hidden_units = w_gate_up.shape[2] // 2
    part = hidden_units // QUARTERS
    step = part // dps
    core = lax.axis_index("core")
    xh = lax.axis_index("xh")

    far_tokens = lax.ppermute(tokens, "xh", SWAP)

    matches = slots_of(routes, experts, capacity)
    select = jnp.sum(
        matches.reshape(rows, tok_rows, top_count).astype(F32), axis=2
    ).astype(BF)
    w = w_gate_up[0].reshape(width, 2, dps, XH, CORE, step).transpose(3, 4, 0, 1, 2, 5)
    w_mine, w_beside = to_quarters(
        w.reshape(XH, CORE, width, 2 * part), after(xh, far_tokens), core
    )

    weights_slot = jnp.sum(jnp.where(matches, route_weight.reshape(1, -1), 0.0), axis=1)
    sent = dot(select, jnp.concatenate([tokens, far_tokens, cotangent], axis=1))
    is_token = jnp.arange(3 * width, dtype=jnp.int32)[None, :] < 2 * width
    sent = (sent * jnp.where(is_token, 1.0, weights_slot[:, None])).astype(BF)
    mine = exchange(sent.reshape(experts, capacity, 3 * width), "expert")
    mine = mine.reshape(rows, 3 * width)
    beside = lax.ppermute(mine, "core", SWAP)

    partial = dot(mine[:, : 2 * width], w_mine.reshape(2 * width, 2 * part))
    partial += dot(beside[:, : 2 * width], w_beside.reshape(2 * width, 2 * part))
    moved = exchange(partial.astype(BF).reshape(Z, rows // Z, 2 * part), "z")
    gate_up = jnp.sum(moved.astype(F32), axis=0)
    hidden = (jax.nn.silu(gate_up[:, :part]) * gate_up[:, part:]).astype(BF)
    hidden = exchange(jnp.broadcast_to(hidden[None], (Z,) + hidden.shape), "z")
    hidden = hidden.reshape(rows, part)

    near_grads = jnp.stack([mine[:, 2 * width :], beside[:, 2 * width :]])
    far_grads = lax.ppermute(near_grads, "xh", SWAP)
    by_xh = pick(after(xh, gate_up), jnp.stack([near_grads, far_grads]))
    slot_grads = [g for pair in by_xh for g in pick(core, pair)]
    grads = [
        lax.dot_general(
            hidden, g, (((0,), (0,)), ((), ())), preferred_element_type=F32
        ).astype(BF)
        for g in slot_grads
    ]
    grads = jnp.stack([g.reshape(dps, step, width) for g in grads], axis=1)
    moved = exchange(grads.reshape(dps * QUARTERS, step, width), ("dp", "xh", "core"))
    moved = moved.reshape(dps, QUARTERS * step, width)
    grad_share = jnp.sum(moved.astype(F32), axis=0)

    down = w_down[0].reshape(dps, XH, CORE, step, width).transpose(1, 2, 0, 3, 4)
    down_mine, down_beside = to_quarters(
        down.reshape(XH, CORE, part, width), after(xh, mine), after(core, gate_up)
    )
    terms = [dot(hidden, d) for d in (down_beside[0], down_beside[1])]
    came = lax.ppermute(jnp.stack(terms), "core", SWAP)
    far_sum = dot(hidden, down_mine[1]) + came[1]
    near_sum = dot(hidden, down_mine[0]) + came[0]
    outputs = near_sum + lax.ppermute(far_sum.astype(BF), "xh", SWAP).astype(F32)
    return outputs.astype(BF), grad_share[None]


def solution(mesh):
    dps, experts = mesh.shape["dp"], mesh.shape["expert"]
    fine = Mesh(
        mesh.devices.reshape(dps, experts, XH, Z, CORE), ("dp", "expert", "xh", "z", "core")
    )
    tensor = ("xh", "z", "core")
    in_specs = (
        P(("dp", "expert"), tensor),
        P(("dp", "expert"), tensor),
        P(("dp", "expert"), None),
        P(("dp", "expert"), None),
        P("expert", tensor, None),
        P("expert", None, tensor),
    )
    out_specs = (P(("dp", "expert"), tensor), P("expert", "dp", tensor))
    return jax.shard_map(
        per_device, mesh=fine, in_specs=in_specs, out_specs=out_specs, check_vma=False
    )
```

time: 140 us -> 140 us (level)
  blocking collectives: 58.9 us -> 0 us
  starting transfers between devices: 44.3 us -> 73.1 us
  waiting for transfers between devices: 22.8 us -> 46.2 us
  between operations: 0.94 us -> 3.08 us
  other arithmetic: 2.77 us -> 4.42 us
    all_to_all x2 -> x0, blocking collectives: 58.9 us -> none  [exchange(): return lax.all_to_all(pieces, axes, split_axis=0, concat_axis=0, tiled=True)]
    all_to_all x2 -> x4, starting transfers between devices: 10.7 us -> 27.6 us  [exchange(): return lax.all_to_all(pieces, axes, split_axis=0, concat_axis=0, tiled=True)]
    all_to_all x2 -> x4, waiting for transfers between devices: 9.93 us -> 25.6 us  [exchange(): return lax.all_to_all(pieces, axes, split_axis=0, concat_axis=0, tiled=True)]
    ppermute x4 -> x8, starting transfers between devices: 25.5 us -> 37.7 us  [the longest x2 9.2 us: to_quarters(): beside = lax.ppermute(jnp.stack([near_sent, far_sent]), 'core', SWAP)]
    ppermute x4 -> x8, waiting for transfers between devices: 12.9 us -> 20.6 us  [the longest x1 10.6 us: per_device(): lax.ppermute(far_sum.astype(BF), 'xh', SWAP).astype(F32)]
    dot_general x4 -> x7, matrix products: 1.29 us -> 3.71 us  [dot(): return jnp.dot(a, b, preferred_element_type=F32)]
    slice x2 -> x4, local copies, waits for them, and re-layouts: 0.23 us -> 1.75 us  [the longest x3 1.54 us: after(): return index + jnp.minimum(jnp.abs(array[0, 0]).astype(jnp.int32), 0)]
  transfers between devices with their start and end apart: 7 -> 13, of which waited for: 4 -> 5; matrix products, arithmetic and copies ran while one was open for 6% -> 9% of each run, Pallas kernels for 0% -> 0%
where the time goes in v4:
time: 140 us; the launch traced here: 138 us
  starting transfers between devices  73.1 us (52%)
  waiting for transfers between devices  46.2 us (33%)
  local copies, waits for them, and re-layouts  6.67 us (5%)
  matrix products  4.93 us (4%)
  other arithmetic  4.42 us (3%)
  between operations  3.08 us (2%)
    all_to_all x4, starting transfers between devices, exchange(): return lax.all_to_all(pieces, axes, split_axis=0, concat_axis=0, tiled=True)  27.6 us
    all_to_all x4, waiting for transfers between devices, exchange(): return lax.all_to_all(pieces, axes, split_axis=0, concat_axis=0, tiled=True)  25.6 us
    ppermute x1, waiting for transfers between devices, per_device(): lax.ppermute(far_sum.astype(BF), 'xh', SWAP).astype(F32)  10.6 us
    ppermute x2, waiting for transfers between devices, to_quarters(): far = lax.ppermute(sent, 'xh', SWAP)  9.41 us
    ppermute x2, starting transfers between devices, to_quarters(): beside = lax.ppermute(jnp.stack([near_sent, far_sent]), 'core', SWAP)  9.2 us
    ppermute x2, starting transfers between devices, to_quarters(): far = lax.ppermute(sent, 'xh', SWAP)  8.61 us
    ppermute x1, starting transfers between devices, per_device(): far_tokens = lax.ppermute(tokens, 'xh', SWAP)  7.94 us
    ppermute x1, starting transfers between devices, per_device(): lax.ppermute(far_sum.astype(BF), 'xh', SWAP).astype(F32)  7.2 us
  transfers between devices with their start and end apart: 13, of which 5 were waited for; matrix products, arithmetic and copies ran while one was open for 9% of the time, Pallas kernels for 0%

profile of v4, /device:TPU:1, one launch (start us, length us, event | category | flops | bytes accessed | tf_op | source)
XLA Modules:
  0.0 138.4 jit_solution(140100792638615765)
XLA Ops:
  0.6 7.9 %collective-permute-start = (bf16[128,128]{1,0:T(8,128)(2,1)}, bf16[128,128]{1,0:T(8,128)(2,1)S(1)}, u32[]{:S(2)}, u32[]{:S(2)}) collective-permute-start(bf16[128,128]{1,0:T(8,128)(2,1)} %param.6), channel_id=1, source_target_pairs={{0,16},{16,0},{1,17},{17,1},{2,18},{18,2},{3,19},{19,3},{4,20},{20... | collective-permute-start | bytes 98312 | tf_op jit(solution)/shard_map/ppermute | solution.py:62
  8.6 0.8 copy.49
  9.4 0.1 eq.69
  9.5 0.1 eq.65
  9.7 0.6 reduce-window.6
  10.2 0.2 slice_reduce_fusion
  10.5 0.1 fusion.41
  10.6 0.1 reduce_sum.48
  10.8 0.8 copy.52
  11.5 0.1 broadcast_in_dim.50
  11.7 0.1 copy.51
  11.7 0.7 multiply_add_fusion.1
  12.4 0.1 convert_reduce_fusion.2
  12.5 0.1 select_reduce_fusion
  12.7 1.5 %copy.53 = bf16[1,128,3072]{1,2,0:T(8,128)(2,1)S(1)} copy(bf16[1,128,3072]{2,1,0:T(8,128)(2,1)} %param.10) | data formatting | bytes 1572864 | tf_op args[4]
  14.2 0.0 copy-start.1
  14.2 0.0 copy-start.2
  14.2 0.0 collective-permute-done
  14.2 0.5 slice.151
  15.4 0.1 broadcast_select_fusion.1
  15.5 3.6 %collective-permute-start.1 = (bf16[2,128,768]{1,2,0:T(8,128)(2,1)S(1)}, bf16[2,128,768]{1,2,0:T(8,128)(2,1)S(1)}, u32[]{:S(2)}, u32[]{:S(2)}) collective-permute-start(bf16[2,128,768]{1,2,0:T(8,128)(2,1)S(1)} %bitcast.118), channel_id=1, source_target_pairs={{0,16},{16,0},{1,17},{17,1},{2,18},{18,2},{3,19},{19,3},{4,20},{20... | collective-permute-start | bytes 1179656 | tf_op jit(solution)/shard_map/ppermute | solution.py:41
  19.2 1.0 fusion
  20.2 7.1 %all-to-all-start = ((bf16[8,64,384]{2,1,0:T(8,128)(2,1)}), bf16[8,64,384]{2,1,0:T(8,128)(2,1)S(1)}, u32[]{:S(2)}, u32[]{:S(2)}) async-start(bf16[8,64,384]{2,1,0:T(8,128)(2,1)} %bitcast.2), calls=%async_computation | async-start | bytes 786432 | tf_op jit(solution)/shard_map/all_to_all | solution.py:14
  27.3 9.4 %collective-permute-done.1 = bf16[2,128,768]{1,2,0:T(8,128)(2,1)S(1)} collective-permute-done((bf16[2,128,768]{1,2,0:T(8,128)(2,1)S(1)}, bf16[2,128,768]{1,2,0:T(8,128)(2,1)S(1)}, u32[]{:S(2)}, u32[]{:S(2)}) %collective-permute-start.1) | collective-permute-done | bytes 393248 | tf_op jit(solution)/shard_map/ppermute | solution.py:41
  36.8 6.8 %collective-permute-start.3 = (bf16[2,128,768]{1,2,0:T(8,128)(2,1)S(1)}, bf16[2,128,768]{1,2,0:T(8,128)(2,1)S(1)}, u32[]{:S(2)}, u32[]{:S(2)}) collective-permute-start(bf16[2,128,768]{1,2,0:T(8,128)(2,1)S(1)} %pad_maximum_fusion.2), channel_id=1, source_target_pairs={{0,1},{1,0},{2,3},{3,2},{4,5},{5,4},{6,7},{7,6},{8,9},{9,8},{10,11... | collective-permute-start | bytes 1179656 | tf_op jit(solution)/shard_map/ppermute | solution.py:45
  43.7 0.0 all-to-all-done
  43.7 6.0 %collective-permute-start.2 = (bf16[512,384]{1,0:T(8,128)(2,1)S(1)}, bf16[512,384]{1,0:T(8,128)(2,1)S(1)}, u32[]{:S(2)}, u32[]{:S(2)}) collective-permute-start(bf16[512,384]{1,0:T(8,128)(2,1)S(1)} %bitcast.109), channel_id=1, source_target_pairs={{0,1},{1,0},{2,3},{3,2},{4,5},{5,4},{6,7},{7,6},{8,9},{9,8},{10,11... | collective-permute-start | bytes 1179656 | tf_op jit(solution)/shard_map/ppermute | solution.py:79
  49.7 0.2 copy.55
  49.9 0.4 fusion.6
  50.3 0.0 collective-permute-done.3
  50.3 0.2 copy.56
  50.5 0.5 collective-permute-done.2
  51.0 1.3 add_convert_fusion
  52.3 12.3 %all-to-all-start.1 = ((bf16[8,64,768]{2,1,0:T(8,128)(2,1)}), bf16[8,64,768]{2,1,0:T(8,128)(2,1)S(1)}, u32[]{:S(2)}, u32[]{:S(2)}) async-start(bf16[8,64,768]{2,1,0:T(8,128)(2,1)} %bitcast.13), calls=%async_computation.1 | async-start | bytes 1572864 | tf_op jit(solution)/shard_map/all_to_all | solution.py:14
  64.6 0.5 slice.162
  65.9 5.0 %collective-permute-start.4 = (bf16[2,384,128]{2,1,0:T(8,128)(2,1)S(1)}, bf16[2,384,128]{2,1,0:T(8,128)(2,1)S(1)}, u32[]{:S(2)}, u32[]{:S(2)}) collective-permute-start(bf16[2,384,128]{2,1,0:T(8,128)(2,1)S(1)} %bitcast.122), channel_id=1, source_target_pairs={{0,16},{16,0},{1,17},{17,1},{2,18},{18,2},{3,19},{19,3},{4,20},{20... | collective-permute-start | bytes 589832 | tf_op jit(solution)/shard_map/ppermute | solution.py:41
  70.9 4.2 %collective-permute-start.8 = (bf16[2,512,128]{2,1,0:T(8,128)(2,1)S(1)}, bf16[2,512,128]{2,1,0:T(8,128)(2,1)S(1)}, u32[]{:S(2)}, u32[]{:S(2)}) collective-permute-start(bf16[2,512,128]{2,1,0:T(8,128)(2,1)S(1)} %pad_maximum_fusion.4), channel_id=1, source_target_pairs={{0,16},{16,0},{1,17},{17,1},{2,18},{18,2},{3,19},{19,3},{4,20},{20... | collective-permute-start | bytes 786440 | tf_op jit(solution)/shard_map/ppermute | solution.py:90
  75.1 13.1 %all-to-all-done.1 = bf16[8,64,768]{2,1,0:T(8,128)(2,1)S(1)} async-done(((bf16[8,64,768]{2,1,0:T(8,128)(2,1)}), bf16[8,64,768]{2,1,0:T(8,128)(2,1)S(1)}, u32[]{:S(2)}, u32[]{:S(2)}) %all-to-all-start.1) | async-done | bytes 786464 | tf_op jit(solution)/shard_map/all_to_all | solution.py:14
  88.2 0.1 convert_reduce_fusion
  88.3 0.5 slice.161
  89.5 0.8 broadcast_in_dim.54
  90.3 3.5 %all-to-all-start.2 = ((bf16[8,64,384]{2,1,0:T(8,128)(2,1)}), bf16[8,64,384]{2,1,0:T(8,128)(2,1)S(1)}, u32[]{:S(2)}, u32[]{:S(2)}) async-start(bf16[8,64,384]{2,1,0:T(8,128)(2,1)} %broadcast_in_dim.54), calls=%async_computation.2 | async-start | bytes 786432 | tf_op jit(solution)/shard_map/all_to_all | solution.py:14
  93.8 0.0 collective-permute-done.4
  93.9 2.4 %collective-permute-start.5 = (bf16[2,384,128]{2,1,0:T(8,128)(2,1)S(1)}, bf16[2,384,128]{2,1,0:T(8,128)(2,1)S(1)}, u32[]{:S(2)}, u32[]{:S(2)}) collective-permute-start(bf16[2,384,128]{2,1,0:T(8,128)(2,1)S(1)} %pad_maximum_fusion.5), channel_id=1, source_target_pairs={{0,1},{1,0},{2,3},{3,2},{4,5},{5,4},{6,7},{7,6},{8,9},{9,8},{10,11... | collective-permute-start | bytes 589832 | tf_op jit(solution)/shard_map/ppermute | solution.py:45
  96.3 0.0 collective-permute-done.8
  96.4 12.5 %all-to-all-done.2 = bf16[8,64,384]{2,1,0:T(8,128)(2,1)S(1)} async-done(((bf16[8,64,384]{2,1,0:T(8,128)(2,1)}), bf16[8,64,384]{2,1,0:T(8,128)(2,1)S(1)}, u32[]{:S(2)}, u32[]{:S(2)}) %all-to-all-start.2) | async-done | bytes 393248 | tf_op jit(solution)/shard_map/all_to_all | solution.py:14
  108.9 0.3 convolution_convert_fusion.3
  109.2 0.3 convolution_convert_fusion.2
  109.5 0.0 collective-permute-done.5
  109.5 0.3 convolution_bitcast_fusion.1
  109.8 0.3 convolution_bitcast_fusion
  110.1 2.4 %collective-permute-start.6 = (f32[2,512,128]{2,1,0:T(8,128)S(1)}, f32[2,512,128]{2,1,0:T(8,128)S(1)}, u32[]{:S(2)}, u32[]{:S(2)}) collective-permute-start(f32[2,512,128]{2,1,0:T(8,128)S(1)} %pad_maximum_fusion), channel_id=1, source_target_pairs={{0,1},{1,0},{2,3},{3,2},{4,5},{5,4},{6,7},{7,6},{8,9},{9,8},{10,11... | collective-permute-start | bytes 1572872 | tf_op jit(solution)/shard_map/ppermute | solution.py:109
  112.5 0.3 convolution_convert_fusion.1
  112.8 0.3 convolution_convert_fusion
  113.1 0.8 pad_maximum_fusion.3
  113.9 4.7 %all-to-all-start.3 = ((bf16[16,96,128]{2,1,0:T(8,128)(2,1)}), bf16[16,96,128]{2,1,0:T(8,128)(2,1)S(1)}, u32[]{:S(2)}, u32[]{:S(2)}) async-start(bf16[16,96,128]{2,1,0:T(8,128)(2,1)} %bitcast.44), calls=%async_computation.3 | async-start | bytes 786432 | tf_op jit(solution)/shard_map/all_to_all | solution.py:14
  118.6 0.0 collective-permute-done.6
  118.6 0.3 fusion.1
  118.9 7.2 %collective-permute-start.7 = (bf16[512,128]{1,0:T(8,128)(2,1)S(1)}, bf16[512,128]{1,0:T(8,128)(2,1)S(1)}, u32[]{:S(2)}, u32[]{:S(2)}) collective-permute-start(bf16[512,128]{1,0:T(8,128)(2,1)S(1)} %fusion.1), channel_id=1, source_target_pairs={{0,16},{16,0},{1,17},{17,1},{2,18},{18,2},{3,19},{19,3},{4,20},{20... | collective-permute-start | bytes 393224 | tf_op jit(solution)/shard_map/ppermute | solution.py:112
  126.1 0.3 fusion.44
  126.4 10.6 %collective-permute-done.7 = bf16[512,128]{1,0:T(8,128)(2,1)S(1)} collective-permute-done((bf16[512,128]{1,0:T(8,128)(2,1)S(1)}, bf16[512,128]{1,0:T(8,128)(2,1)S(1)}, u32[]{:S(2)}, u32[]{:S(2)}) %collective-permute-start.7) | collective-permute-done | bytes 131104 | tf_op jit(solution)/shard_map/ppermute | solution.py:112
  137.0 0.7 fusion.4
  137.7 0.0 all-to-all-done.3
  137.7 0.7 convert_reduce_fusion.1
  (25 shorter events, 0.5 us)
Async XLA Ops:
  0.6 13.6 %collective-permute-start = (bf16[128,128]{1,0:T(8,128)(2,1)}, bf16[128,128]{1,0:T(8,128)(2,1)S(1)}, u32[]{:S(2)}, u32[]{:S(2)}) collective-permute-start(bf16[128,128]{1,0:T(8,128)(2,1)} %param.6), channel_id=1, source_target_pairs={{0,16},{16,0},{1,17},{17,1},{2,18},{18,2},{3,19},{19,3},{4,20},{20... | collective-permute-start | bytes 98312 | tf_op jit(solution)/shard_map/ppermute | solution.py:62
  14.2 5.0 %copy-start.1 = (bf16[128,128]{1,0:T(8,128)(2,1)S(1)}, bf16[128,128]{1,0:T(8,128)(2,1)}, u32[]{:S(2)}) copy-start(bf16[128,128]{1,0:T(8,128)(2,1)} %param.6) | copy-start | bytes 98308
  14.2 5.0 %copy-start.2 = (bf16[128,128]{1,0:T(8,128)(2,1)S(1)}, bf16[128,128]{1,0:T(8,128)(2,1)}, u32[]{:S(2)}) copy-start(bf16[128,128]{1,0:T(8,128)(2,1)} %param.7) | copy-start | bytes 98308
  15.5 21.2 %collective-permute-start.1 = (bf16[2,128,768]{1,2,0:T(8,128)(2,1)S(1)}, bf16[2,128,768]{1,2,0:T(8,128)(2,1)S(1)}, u32[]{:S(2)}, u32[]{:S(2)}) collective-permute-start(bf16[2,128,768]{1,2,0:T(8,128)(2,1)S(1)} %bitcast.118), channel_id=1, source_target_pairs={{0,16},{16,0},{1,17},{17,1},{2,18},{18,2},{3,19},{19,3},{4,20},{20... | collective-permute-start | bytes 1179656 | tf_op jit(solution)/shard_map/ppermute | solution.py:41
  20.2 23.5 %all-to-all-start = ((bf16[8,64,384]{2,1,0:T(8,128)(2,1)}), bf16[8,64,384]{2,1,0:T(8,128)(2,1)S(1)}, u32[]{:S(2)}, u32[]{:S(2)}) async-start(bf16[8,64,384]{2,1,0:T(8,128)(2,1)} %bitcast.2), calls=%async_computation | async-start | bytes 786432 | tf_op jit(solution)/shard_map/all_to_all | solution.py:14
  36.8 13.5 %collective-permute-start.3 = (bf16[2,128,768]{1,2,0:T(8,128)(2,1)S(1)}, bf16[2,128,768]{1,2,0:T(8,128)(2,1)S(1)}, u32[]{:S(2)}, u32[]{:S(2)}) collective-permute-start(bf16[2,128,768]{1,2,0:T(8,128)(2,1)S(1)} %pad_maximum_fusion.2), channel_id=1, source_target_pairs={{0,1},{1,0},{2,3},{3,2},{4,5},{5,4},{6,7},{7,6},{8,9},{9,8},{10,11... | collective-permute-start | bytes 1179656 | tf_op jit(solution)/shard_map/ppermute | solution.py:45
  43.7 7.4 %collective-permute-start.2 = (bf16[512,384]{1,0:T(8,128)(2,1)S(1)}, bf16[512,384]{1,0:T(8,128)(2,1)S(1)}, u32[]{:S(2)}, u32[]{:S(2)}) collective-permute-start(bf16[512,384]{1,0:T(8,128)(2,1)S(1)} %bitcast.109), channel_id=1, source_target_pairs={{0,1},{1,0},{2,3},{3,2},{4,5},{5,4},{6,7},{7,6},{8,9},{9,8},{10,11... | collective-permute-start | bytes 1179656 | tf_op jit(solution)/shard_map/ppermute | solution.py:79
  51.0 14.8 %copy-start = (bf16[1,1536,128]{2,1,0:T(8,128)(2,1)S(1)}, bf16[1,1536,128]{2,1,0:T(8,128)(2,1)}, u32[]{:S(2)}) copy-start(bf16[1,1536,128]{2,1,0:T(8,128)(2,1)} %param.11) | copy-start | bytes 1179652
  52.3 35.9 %all-to-all-start.1 = ((bf16[8,64,768]{2,1,0:T(8,128)(2,1)}), bf16[8,64,768]{2,1,0:T(8,128)(2,1)S(1)}, u32[]{:S(2)}, u32[]{:S(2)}) async-start(bf16[8,64,768]{2,1,0:T(8,128)(2,1)} %bitcast.13), calls=%async_computation.1 | async-start | bytes 1572864 | tf_op jit(solution)/shard_map/all_to_all | solution.py:14
  65.9 28.0 %collective-permute-start.4 = (bf16[2,384,128]{2,1,0:T(8,128)(2,1)S(1)}, bf16[2,384,128]{2,1,0:T(8,128)(2,1)S(1)}, u32[]{:S(2)}, u32[]{:S(2)}) collective-permute-start(bf16[2,384,128]{2,1,0:T(8,128)(2,1)S(1)} %bitcast.122), channel_id=1, source_target_pairs={{0,16},{16,0},{1,17},{17,1},{2,18},{18,2},{3,19},{19,3},{4,20},{20... | collective-permute-start | bytes 589832 | tf_op jit(solution)/shard_map/ppermute | solution.py:41
  70.9 25.4 %collective-permute-start.8 = (bf16[2,512,128]{2,1,0:T(8,128)(2,1)S(1)}, bf16[2,512,128]{2,1,0:T(8,128)(2,1)S(1)}, u32[]{:S(2)}, u32[]{:S(2)}) collective-permute-start(bf16[2,512,128]{2,1,0:T(8,128)(2,1)S(1)} %pad_maximum_fusion.4), channel_id=1, source_target_pairs={{0,16},{16,0},{1,17},{17,1},{2,18},{18,2},{3,19},{19,3},{4,20},{20... | collective-permute-start | bytes 786440 | tf_op jit(solution)/shard_map/ppermute | solution.py:90
  90.3 18.5 %all-to-all-start.2 = ((bf16[8,64,384]{2,1,0:T(8,128)(2,1)}), bf16[8,64,384]{2,1,0:T(8,128)(2,1)S(1)}, u32[]{:S(2)}, u32[]{:S(2)}) async-start(bf16[8,64,384]{2,1,0:T(8,128)(2,1)} %broadcast_in_dim.54), calls=%async_computation.2 | async-start | bytes 786432 | tf_op jit(solution)/shard_map/all_to_all | solution.py:14
  93.9 15.6 %collective-permute-start.5 = (bf16[2,384,128]{2,1,0:T(8,128)(2,1)S(1)}, bf16[2,384,128]{2,1,0:T(8,128)(2,1)S(1)}, u32[]{:S(2)}, u32[]{:S(2)}) collective-permute-start(bf16[2,384,128]{2,1,0:T(8,128)(2,1)S(1)} %pad_maximum_fusion.5), channel_id=1, source_target_pairs={{0,1},{1,0},{2,3},{3,2},{4,5},{5,4},{6,7},{7,6},{8,9},{9,8},{10,11... | collective-permute-start | bytes 589832 | tf_op jit(solution)/shard_map/ppermute | solution.py:45
  110.1 8.5 %collective-permute-start.6 = (f32[2,512,128]{2,1,0:T(8,128)S(1)}, f32[2,512,128]{2,1,0:T(8,128)S(1)}, u32[]{:S(2)}, u32[]{:S(2)}) collective-permute-start(f32[2,512,128]{2,1,0:T(8,128)S(1)} %pad_maximum_fusion), channel_id=1, source_target_pairs={{0,1},{1,0},{2,3},{3,2},{4,5},{5,4},{6,7},{7,6},{8,9},{9,8},{10,11... | collective-permute-start | bytes 1572872 | tf_op jit(solution)/shard_map/ppermute | solution.py:109
  113.9 23.8 %all-to-all-start.3 = ((bf16[16,96,128]{2,1,0:T(8,128)(2,1)}), bf16[16,96,128]{2,1,0:T(8,128)(2,1)S(1)}, u32[]{:S(2)}, u32[]{:S(2)}) async-start(bf16[16,96,128]{2,1,0:T(8,128)(2,1)} %bitcast.44), calls=%async_computation.3 | async-start | bytes 786432 | tf_op jit(solution)/shard_map/all_to_all | solution.py:14
  118.9 18.1 %collective-permute-start.7 = (bf16[512,128]{1,0:T(8,128)(2,1)S(1)}, bf16[512,128]{1,0:T(8,128)(2,1)S(1)}, u32[]{:S(2)}, u32[]{:S(2)}) collective-permute-start(bf16[512,128]{1,0:T(8,128)(2,1)S(1)} %fusion.1), channel_id=1, source_target_pairs={{0,16},{16,0},{1,17},{17,1},{2,18},{18,2},{3,19},{19,3},{4,20},{20... | collective-permute-start | bytes 393224 | tf_op jit(solution)/shard_map/ppermute | solution.py:112

commit v5 on v4

--- a/solution.py
+++ b/solution.py
@@ -32,10 +32,6 @@
     return jnp.arange(experts * capacity, dtype=jnp.int32)[:, None] == target[None, :]
 
 
-def after(index, array):
-    return index + jnp.minimum(jnp.abs(array[0, 0]).astype(jnp.int32), 0)
-
-
 def to_quarters(blocks, xh, core):
     near, sent = pick(xh, blocks)
     far = lax.ppermute(sent, "xh", SWAP)
@@ -67,7 +63,7 @@
     ).astype(BF)
     w = w_gate_up[0].reshape(width, 2, dps, XH, CORE, step).transpose(3, 4, 0, 1, 2, 5)
     w_mine, w_beside = to_quarters(
-        w.reshape(XH, CORE, width, 2 * part), after(xh, far_tokens), core
+        w.reshape(XH, CORE, width, 2 * part), xh, core
     )
 
     weights_slot = jnp.sum(jnp.where(matches, route_weight.reshape(1, -1), 0.0), axis=1)
@@ -83,33 +79,31 @@
     moved = exchange(partial.astype(BF).reshape(Z, rows // Z, 2 * part), "z")
     gate_up = jnp.sum(moved.astype(F32), axis=0)
     hidden = (jax.nn.silu(gate_up[:, :part]) * gate_up[:, part:]).astype(BF)
-    hidden = exchange(jnp.broadcast_to(hidden[None], (Z,) + hidden.shape), "z")
-    hidden = hidden.reshape(rows, part)
+    hidden = exchange(jnp.broadcast_to(hidden[None], (XH * Z,) + hidden.shape), ("xh", "z"))
+    hidden = hidden.reshape(XH, rows, part)
 
-    near_grads = jnp.stack([mine[:, 2 * width :], beside[:, 2 * width :]])
-    far_grads = lax.ppermute(near_grads, "xh", SWAP)
-    by_xh = pick(after(xh, gate_up), jnp.stack([near_grads, far_grads]))
-    slot_grads = [g for pair in by_xh for g in pick(core, pair)]
-    grads = [
-        lax.dot_general(
-            hidden, g, (((0,), (0,)), ((), ())), preferred_element_type=F32
-        ).astype(BF)
-        for g in slot_grads
-    ]
-    grads = jnp.stack([g.reshape(dps, step, width) for g in grads], axis=1)
-    moved = exchange(grads.reshape(dps * QUARTERS, step, width), ("dp", "xh", "core"))
-    moved = moved.reshape(dps, QUARTERS * step, width)
-    grad_share = jnp.sum(moved.astype(F32), axis=0)
+    slot_grads = pick(core, jnp.stack([mine[:, 2 * width :], beside[:, 2 * width :]]))
 
-    down = w_down[0].reshape(dps, XH, CORE, step, width).transpose(1, 2, 0, 3, 4)
-    down_mine, down_beside = to_quarters(
-        down.reshape(XH, CORE, part, width), after(xh, mine), after(core, gate_up)
+    def grads_of(half, g):
+        out = lax.dot_general(half, g, (((0,), (0,)), ((), ())), preferred_element_type=F32)
+        return out.astype(BF).reshape(dps, step, width)
+
+    grads = jnp.stack(
+        [jnp.stack([grads_of(hidden[h], g) for h in range(XH)], axis=1) for g in slot_grads],
+        axis=1,
     )
-    terms = [dot(hidden, d) for d in (down_beside[0], down_beside[1])]
-    came = lax.ppermute(jnp.stack(terms), "core", SWAP)
-    far_sum = dot(hidden, down_mine[1]) + came[1]
-    near_sum = dot(hidden, down_mine[0]) + came[0]
-    outputs = near_sum + lax.ppermute(far_sum.astype(BF), "xh", SWAP).astype(F32)
+    moved = exchange(grads.reshape(dps * CORE, XH * step, width), ("dp", "core"))
+    moved = jnp.sum(moved.reshape(dps, CORE, XH, step, width).astype(F32), axis=0)
+    grad_share = moved.transpose(1, 0, 2, 3).reshape(QUARTERS * step, width)
+
+    down = w_down[0].reshape(dps, XH, CORE, step, width).transpose(2, 1, 0, 3, 4)
+    down_mine, down_sent = pick(core, down.reshape(CORE, XH, part, width))
+    down_beside = lax.ppermute(down_sent, "core", SWAP)
+
+    def terms(down):
+        return dot(hidden[0], down[0]) + dot(hidden[1], down[1])
+
+    outputs = terms(down_mine) + lax.ppermute(terms(down_beside), "core", SWAP)
     return outputs.astype(BF), grad_share[None]
 
 

time: 140 us -> 134 us (0.957)
  blocking collectives: 0 us -> 32.3 us
  waiting for transfers between devices: 46.2 us -> 26.6 us
  starting transfers between devices: 73.1 us -> 61.9 us
  between operations: 3.08 us -> 1.04 us
  local copies, waits for them, and re-layouts: 6.67 us -> 4.76 us
  other arithmetic: 4.42 us -> 2.89 us
    all_to_all x0 -> x1, blocking collectives: none -> 32.3 us  [exchange(): return lax.all_to_all(pieces, axes, split_axis=0, concat_axis=0, tiled=True)]
    ppermute x3 -> x2, waiting for transfers between devices: 10.6 us -> 0.97 us  [the longest x1 0.96 us: per_device(): outputs = terms(down_mine) + lax.ppermute(terms(down_beside), 'core', SWAP)]
    ppermute x3 -> x2, starting transfers between devices: 13.8 us -> 5.44 us  [the longest x1 3.52 us: per_device(): down_beside = lax.ppermute(down_sent, 'core', SWAP)]
    ppermute x2 -> x1, starting transfers between devices: 8.61 us -> 1.92 us  [to_quarters(): far = lax.ppermute(sent, 'xh', SWAP)]
    ppermute x2 -> x1, waiting for transfers between devices: 9.41 us -> 3.42 us  [to_quarters(): far = lax.ppermute(sent, 'xh', SWAP)]
    all_to_all x4 -> x3, waiting for transfers between devices: 25.6 us -> 21.7 us  [exchange(): return lax.all_to_all(pieces, axes, split_axis=0, concat_axis=0, tiled=True)]
    ppermute x2 -> x1, starting transfers between devices: 9.2 us -> 12.1 us  [to_quarters(): beside = lax.ppermute(jnp.stack([near_sent, far_sent]), 'core', SWAP)]
    ppermute x1, starting transfers between devices: 6.03 us -> 8.09 us  [per_device(): beside = lax.ppermute(mine, 'core', SWAP)]
  transfers between devices with their start and end apart: 13 -> 9, of which waited for: 5 -> 5; matrix products, arithmetic and copies ran while one was open for 9% -> 7% of each run, Pallas kernels for 0% -> 0%
where the time goes in v5:
time: 134 us
  starting transfers between devices  61.9 us (46%)
  blocking collectives  32.3 us (24%)
  waiting for transfers between devices  26.6 us (20%)
  local copies, waits for them, and re-layouts  4.76 us (4%)
  matrix products  4.01 us (3%)
  other arithmetic  2.89 us (2%)
    all_to_all x1, blocking collectives, exchange(): return lax.all_to_all(pieces, axes, split_axis=0, concat_axis=0, tiled=True)  32.3 us
    all_to_all x3, starting transfers between devices, exchange(): return lax.all_to_all(pieces, axes, split_axis=0, concat_axis=0, tiled=True)  26.4 us
    all_to_all x3, waiting for transfers between devices, exchange(): return lax.all_to_all(pieces, axes, split_axis=0, concat_axis=0, tiled=True)  21.7 us
    ppermute x1, starting transfers between devices, to_quarters(): beside = lax.ppermute(jnp.stack([near_sent, far_sent]), 'core', SWAP)  12.1 us
    ppermute x1, starting transfers between devices, per_device(): beside = lax.ppermute(mine, 'core', SWAP)  8.09 us
    ppermute x1, starting transfers between devices, per_device(): far_tokens = lax.ppermute(tokens, 'xh', SWAP)  7.94 us
    ppermute x1, starting transfers between devices, per_device(): down_beside = lax.ppermute(down_sent, 'core', SWAP)  3.52 us
    ppermute x1, waiting for transfers between devices, to_quarters(): far = lax.ppermute(sent, 'xh', SWAP)  3.42 us
  transfers between devices with their start and end apart: 9, of which 5 were waited for; matrix products, arithmetic and copies ran while one was open for 7% of the time, Pallas kernels for 0%

profile of v5, /device:TPU:1, one launch (start us, length us, event | category | flops | bytes accessed | tf_op | source)
XLA Modules:
  0.0 133.5 jit_solution(1425490339255310450)
XLA Ops:
  0.6 7.9 %collective-permute-start = (bf16[128,128]{1,0:T(8,128)(2,1)}, bf16[128,128]{1,0:T(8,128)(2,1)S(1)}, u32[]{:S(2)}, u32[]{:S(2)}) collective-permute-start(bf16[128,128]{1,0:T(8,128)(2,1)} %param.6), channel_id=1, source_target_pairs={{0,16},{16,0},{1,17},{17,1},{2,18},{18,2},{3,19},{19,3},{4,20},{20... | collective-permute-start | bytes 98312 | tf_op jit(solution)/shard_map/ppermute | solution.py:58
  8.6 1.5 %copy.83 = bf16[1,128,3072]{1,2,0:T(8,128)(2,1)S(1)} copy(bf16[1,128,3072]{2,1,0:T(8,128)(2,1)} %param.10) | data formatting | bytes 1572864 | tf_op args[4]
  10.1 0.0 copy-start.1
  10.1 0.0 copy-start.2
  10.1 0.0 copy-start.3
  10.1 0.0 copy-start.4
  10.2 0.1 broadcast_select_fusion.1
  10.3 1.9 %collective-permute-start.1 = (bf16[2,128,768]{1,2,0:T(8,128)(2,1)S(1)}, bf16[2,128,768]{1,2,0:T(8,128)(2,1)S(1)}, u32[]{:S(2)}, u32[]{:S(2)}) collective-permute-start(bf16[2,128,768]{1,2,0:T(8,128)(2,1)S(1)} %bitcast.89), channel_id=1, source_target_pairs={{0,16},{16,0},{1,17},{17,1},{2,18},{18,2},{3,19},{19,3},{4,20},{20... | collective-permute-start | bytes 1179656 | tf_op jit(solution)/shard_map/ppermute | solution.py:37
  12.2 0.0 copy-done.1
  12.2 0.1 copy.79
  12.3 0.1 eq.59
  12.4 0.1 eq.55
  12.6 0.6 reduce-window.6
  13.2 0.2 slice_reduce_fusion
  13.4 0.1 fusion.13
  13.5 0.1 reduce_sum.48
  13.7 0.0 copy-done.2
  13.7 0.1 copy.82
  13.8 0.1 broadcast_in_dim.47
  14.0 0.1 copy.81
  14.0 0.1 convert_reduce_fusion.2
  14.1 0.1 select_reduce_fusion
  14.3 0.0 collective-permute-done
  14.3 0.0 copy-done.3
  14.3 0.0 copy-done.4
  14.3 1.0 fusion
  15.3 7.4 %all-to-all-start = ((bf16[8,64,384]{2,1,0:T(8,128)(2,1)}), bf16[8,64,384]{2,1,0:T(8,128)(2,1)S(1)}, u32[]{:S(2)}, u32[]{:S(2)}) async-start(bf16[8,64,384]{2,1,0:T(8,128)(2,1)} %bitcast.2), calls=%async_computation | async-start | bytes 786432 | tf_op jit(solution)/shard_map/all_to_all | solution.py:14
  22.8 3.4 %collective-permute-done.1 = bf16[2,128,768]{1,2,0:T(8,128)(2,1)S(1)} collective-permute-done((bf16[2,128,768]{1,2,0:T(8,128)(2,1)S(1)}, bf16[2,128,768]{1,2,0:T(8,128)(2,1)S(1)}, u32[]{:S(2)}, u32[]{:S(2)}) %collective-permute-start.1) | collective-permute-done | bytes 393248 | tf_op jit(solution)/shard_map/ppermute | solution.py:37
  26.3 12.1 %collective-permute-start.3 = (bf16[2,128,768]{1,2,0:T(8,128)(2,1)S(1)}, bf16[2,128,768]{1,2,0:T(8,128)(2,1)S(1)}, u32[]{:S(2)}, u32[]{:S(2)}) collective-permute-start(bf16[2,128,768]{1,2,0:T(8,128)(2,1)S(1)} %pad_maximum_fusion.1), channel_id=1, source_target_pairs={{0,1},{1,0},{2,3},{3,2},{4,5},{5,4},{6,7},{7,6},{8,9},{9,8},{10,11... | collective-permute-start | bytes 1179656 | tf_op jit(solution)/shard_map/ppermute | solution.py:41
  38.4 0.0 all-to-all-done
  38.4 8.1 %collective-permute-start.2 = (bf16[512,384]{1,0:T(8,128)(2,1)S(1)}, bf16[512,384]{1,0:T(8,128)(2,1)S(1)}, u32[]{:S(2)}, u32[]{:S(2)}) collective-permute-start(bf16[512,384]{1,0:T(8,128)(2,1)S(1)} %bitcast.80), channel_id=1, source_target_pairs={{0,1},{1,0},{2,3},{3,2},{4,5},{5,4},{6,7},{7,6},{8,9},{9,8},{10,11... | collective-permute-start | bytes 1179656 | tf_op jit(solution)/shard_map/ppermute | solution.py:75
  46.6 0.2 copy.85
  46.7 0.4 fusion.2
  47.1 0.0 collective-permute-done.3
  47.1 0.2 copy.86
  47.3 0.5 collective-permute-done.2
  47.8 0.4 add_convert_fusion
  48.2 32.3 %all_to_all.20 = bf16[8,64,768]{2,1,0:T(8,128)(2,1)S(1)} all-to-all(bf16[8,64,768]{2,1,0:T(8,128)(2,1)S(1)} %bitcast.76), channel_id=1, replica_groups=mesh['dp'=4,'expert'=8,'xh'=2,'z'=8,'core'=2] {'z'}, dimensions={0} | all-to-all | bytes 1572864 | tf_op jit(solution)/shard_map/all_to_all | solution.py:14
  80.5 0.1 convert_reduce_fusion
  80.6 0.0 copy-start
  80.7 1.0 broadcast_in_dim.51
  81.7 7.0 %all-to-all-start.2 = ((bf16[16,64,384]{2,1,0:T(8,128)(2,1)}), bf16[16,64,384]{2,1,0:T(8,128)(2,1)S(1)}, u32[]{:S(2)}, u32[]{:S(2)}) async-start(bf16[16,64,384]{2,1,0:T(8,128)(2,1)} %broadcast_in_dim.51), calls=%async_computation.2 | async-start | bytes 1572864 | tf_op jit(solution)/shard_map/all_to_all | solution.py:14
  88.7 0.0 copy-done
  88.7 3.5 %collective-permute-start.4 = (bf16[2,384,128]{2,1,0:T(8,128)(2,1)S(1)}, bf16[2,384,128]{2,1,0:T(8,128)(2,1)S(1)}, u32[]{:S(2)}, u32[]{:S(2)}) collective-permute-start(bf16[2,384,128]{2,1,0:T(8,128)(2,1)S(1)} %bitcast.93), channel_id=1, source_target_pairs={{0,1},{1,0},{2,3},{3,2},{4,5},{5,4},{6,7},{7,6},{8,9},{9,8},{10,11... | collective-permute-start | bytes 589832 | tf_op jit(solution)/shard_map/ppermute | solution.py:101
  92.3 14.7 %all-to-all-done.2 = bf16[16,64,384]{2,1,0:T(8,128)(2,1)S(1)} async-done(((bf16[16,64,384]{2,1,0:T(8,128)(2,1)}), bf16[16,64,384]{2,1,0:T(8,128)(2,1)S(1)}, u32[]{:S(2)}, u32[]{:S(2)}) %all-to-all-start.2) | async-done | bytes 786464 | tf_op jit(solution)/shard_map/all_to_all | solution.py:14
  107.0 0.1 fusion.16
  107.1 0.3 convolution_convert_fusion.1
  107.4 0.3 convolution_convert_fusion.3
  107.7 0.3 convolution_convert_fusion
  108.0 0.3 convolution_convert_fusion.2
  108.4 0.8 pad_maximum_fusion.2
  109.2 11.9 %all-to-all-start.3 = ((bf16[8,192,128]{2,1,0:T(8,128)(2,1)}), bf16[8,192,128]{2,1,0:T(8,128)(2,1)S(1)}, u32[]{:S(2)}, u32[]{:S(2)}) async-start(bf16[8,192,128]{2,1,0:T(8,128)(2,1)} %bitcast.33), calls=%async_computation.3 | async-start | bytes 786432 | tf_op jit(solution)/shard_map/all_to_all | solution.py:14
  121.1 0.0 collective-permute-done.4
  121.1 0.3 fusion.5
  121.4 0.3 convolution_add_fusion
  121.6 1.9 %collective-permute-start.5 = (f32[512,128]{1,0:T(8,128)S(1)}, f32[512,128]{1,0:T(8,128)S(1)}, u32[]{:S(2)}, u32[]{:S(2)}) collective-permute-start(f32[512,128]{1,0:T(8,128)S(1)} %convolution_add_fusion), channel_id=1, source_target_pairs={{0,1},{1,0},{2,3},{3,2},{4,5},{5,4},{6,7},{7,6},{8,9},{9,8},{10,11... | collective-permute-start | bytes 786440 | tf_op jit(solution)/shard_map/ppermute | solution.py:106
  123.6 0.3 fusion.18
  123.8 0.3 convolution_add_fusion.1
  124.1 1.0 collective-permute-done.5
  125.1 0.7 add_convert_fusion.1
  125.8 7.0 %all-to-all-done.3 = bf16[8,192,128]{2,1,0:T(8,128)(2,1)S(1)} async-done(((bf16[8,192,128]{2,1,0:T(8,128)(2,1)}), bf16[8,192,128]{2,1,0:T(8,128)(2,1)S(1)}, u32[]{:S(2)}, u32[]{:S(2)}) %all-to-all-start.3) | async-done | bytes 393248 | tf_op jit(solution)/shard_map/all_to_all | solution.py:14
  132.8 0.1 convert_reduce_fusion.1
  132.8 0.7 copy.92
  (16 shorter events, 0.4 us)
Async XLA Ops:
  0.6 13.6 %collective-permute-start = (bf16[128,128]{1,0:T(8,128)(2,1)}, bf16[128,128]{1,0:T(8,128)(2,1)S(1)}, u32[]{:S(2)}, u32[]{:S(2)}) collective-permute-start(bf16[128,128]{1,0:T(8,128)(2,1)} %param.6), channel_id=1, source_target_pairs={{0,16},{16,0},{1,17},{17,1},{2,18},{18,2},{3,19},{19,3},{4,20},{20... | collective-permute-start | bytes 98312 | tf_op jit(solution)/shard_map/ppermute | solution.py:58
  10.1 2.1 %copy-start.1 = (s32[128,2]{0,1:T(2,128)S(1)}, s32[128,2]{0,1:T(2,128)}, u32[]{:S(2)}) copy-start(s32[128,2]{0,1:T(2,128)} %param.8) | copy-start | bytes 3076
  10.1 3.6 %copy-start.2 = (f32[128,2]{0,1:T(2,128)S(1)}, f32[128,2]{0,1:T(2,128)}, u32[]{:S(2)}) copy-start(f32[128,2]{0,1:T(2,128)} %param.9) | copy-start | bytes 3076
  10.1 4.2 %copy-start.3 = (bf16[128,128]{1,0:T(8,128)(2,1)S(1)}, bf16[128,128]{1,0:T(8,128)(2,1)}, u32[]{:S(2)}) copy-start(bf16[128,128]{1,0:T(8,128)(2,1)} %param.7) | copy-start | bytes 98308
  10.1 4.2 %copy-start.4 = (bf16[128,128]{1,0:T(8,128)(2,1)S(1)}, bf16[128,128]{1,0:T(8,128)(2,1)}, u32[]{:S(2)}) copy-start(bf16[128,128]{1,0:T(8,128)(2,1)} %param.6) | copy-start | bytes 98308
  10.3 15.9 %collective-permute-start.1 = (bf16[2,128,768]{1,2,0:T(8,128)(2,1)S(1)}, bf16[2,128,768]{1,2,0:T(8,128)(2,1)S(1)}, u32[]{:S(2)}, u32[]{:S(2)}) collective-permute-start(bf16[2,128,768]{1,2,0:T(8,128)(2,1)S(1)} %bitcast.89), channel_id=1, source_target_pairs={{0,16},{16,0},{1,17},{17,1},{2,18},{18,2},{3,19},{19,3},{4,20},{20... | collective-permute-start | bytes 1179656 | tf_op jit(solution)/shard_map/ppermute | solution.py:37
  15.3 23.1 %all-to-all-start = ((bf16[8,64,384]{2,1,0:T(8,128)(2,1)}), bf16[8,64,384]{2,1,0:T(8,128)(2,1)S(1)}, u32[]{:S(2)}, u32[]{:S(2)}) async-start(bf16[8,64,384]{2,1,0:T(8,128)(2,1)} %bitcast.2), calls=%async_computation | async-start | bytes 786432 | tf_op jit(solution)/shard_map/all_to_all | solution.py:14
  26.3 20.8 %collective-permute-start.3 = (bf16[2,128,768]{1,2,0:T(8,128)(2,1)S(1)}, bf16[2,128,768]{1,2,0:T(8,128)(2,1)S(1)}, u32[]{:S(2)}, u32[]{:S(2)}) collective-permute-start(bf16[2,128,768]{1,2,0:T(8,128)(2,1)S(1)} %pad_maximum_fusion.1), channel_id=1, source_target_pairs={{0,1},{1,0},{2,3},{3,2},{4,5},{5,4},{6,7},{7,6},{8,9},{9,8},{10,11... | collective-permute-start | bytes 1179656 | tf_op jit(solution)/shard_map/ppermute | solution.py:41
  38.4 9.4 %collective-permute-start.2 = (bf16[512,384]{1,0:T(8,128)(2,1)S(1)}, bf16[512,384]{1,0:T(8,128)(2,1)S(1)}, u32[]{:S(2)}, u32[]{:S(2)}) collective-permute-start(bf16[512,384]{1,0:T(8,128)(2,1)S(1)} %bitcast.80), channel_id=1, source_target_pairs={{0,1},{1,0},{2,3},{3,2},{4,5},{5,4},{6,7},{7,6},{8,9},{9,8},{10,11... | collective-permute-start | bytes 1179656 | tf_op jit(solution)/shard_map/ppermute | solution.py:75
  80.6 8.1 %copy-start = (bf16[1,1536,128]{2,1,0:T(8,128)(2,1)S(1)}, bf16[1,1536,128]{2,1,0:T(8,128)(2,1)}, u32[]{:S(2)}) copy-start(bf16[1,1536,128]{2,1,0:T(8,128)(2,1)} %param.11) | copy-start | bytes 1179652
  81.7 25.3 %all-to-all-start.2 = ((bf16[16,64,384]{2,1,0:T(8,128)(2,1)}), bf16[16,64,384]{2,1,0:T(8,128)(2,1)S(1)}, u32[]{:S(2)}, u32[]{:S(2)}) async-start(bf16[16,64,384]{2,1,0:T(8,128)(2,1)} %broadcast_in_dim.51), calls=%async_computation.2 | async-start | bytes 1572864 | tf_op jit(solution)/shard_map/all_to_all | solution.py:14
  88.7 32.4 %collective-permute-start.4 = (bf16[2,384,128]{2,1,0:T(8,128)(2,1)S(1)}, bf16[2,384,128]{2,1,0:T(8,128)(2,1)S(1)}, u32[]{:S(2)}, u32[]{:S(2)}) collective-permute-start(bf16[2,384,128]{2,1,0:T(8,128)(2,1)S(1)} %bitcast.93), channel_id=1, source_target_pairs={{0,1},{1,0},{2,3},{3,2},{4,5},{5,4},{6,7},{7,6},{8,9},{9,8},{10,11... | collective-permute-start | bytes 589832 | tf_op jit(solution)/shard_map/ppermute | solution.py:101
  109.2 23.6 %all-to-all-start.3 = ((bf16[8,192,128]{2,1,0:T(8,128)(2,1)}), bf16[8,192,128]{2,1,0:T(8,128)(2,1)S(1)}, u32[]{:S(2)}, u32[]{:S(2)}) async-start(bf16[8,192,128]{2,1,0:T(8,128)(2,1)} %bitcast.33), calls=%async_computation.3 | async-start | bytes 786432 | tf_op jit(solution)/shard_map/all_to_all | solution.py:14
  121.6 3.4 %collective-permute-start.5 = (f32[512,128]{1,0:T(8,128)S(1)}, f32[512,128]{1,0:T(8,128)S(1)}, u32[]{:S(2)}, u32[]{:S(2)}) collective-permute-start(f32[512,128]{1,0:T(8,128)S(1)} %convolution_add_fusion), channel_id=1, source_target_pairs={{0,1},{1,0},{2,3},{3,2},{4,5},{5,4},{6,7},{7,6},{8,9},{9,8},{10,11... | collective-permute-start | bytes 786440 | tf_op jit(solution)/shard_map/ppermute | solution.py:106

commit v6 on v5

v6 whole, which is shorter than its diff:
```python
import jax
import jax.numpy as jnp
from jax import lax
from jax.sharding import Mesh, PartitionSpec as P

BF = jnp.bfloat16
F32 = jnp.float32
XH, ZH, ZL, CORE = 2, 4, 2, 2
QUARTERS = ZL * CORE
SPREAD = ("xh", "zh")
SWAP = [(0, 1), (1, 0)]


def exchange(pieces, axes):
    return lax.all_to_all(pieces, axes, split_axis=0, concat_axis=0, tiled=True)


def dot(a, b):
    return jnp.dot(a, b, preferred_element_type=F32)


def pick(index, pair):
    first = index == 0
    return jnp.where(first, pair[0], pair[1]), jnp.where(first, pair[1], pair[0])


def slots_of(routes, experts, capacity):
    flat = routes.reshape(-1)
    onehot = (flat[:, None] == jnp.arange(experts, dtype=jnp.int32)[None, :]).astype(jnp.int32)
    before = jnp.cumsum(onehot, axis=0) - onehot
    slot = jnp.sum(before * onehot, axis=1)
    target = flat * capacity + slot
    return jnp.arange(experts * capacity, dtype=jnp.int32)[:, None] == target[None, :]


def after(array, earlier):
    return lax.optimization_barrier((array, earlier))[0]


def to_quarters(blocks, zl, core, earlier):
    near, sent = pick(zl, blocks)
    far = after(lax.ppermute(sent, "zl", SWAP), earlier)
    near_mine, near_sent = pick(core, near)
    far_mine, far_sent = pick(core, far)
    mine = jnp.stack([near_mine, far_mine])
    beside = lax.ppermute(jnp.stack([near_sent, far_sent]), "core", SWAP)
    return mine, beside


def per_device(tokens, cotangent, routes, route_weight, w_gate_up, w_down):
    tok_rows, width = tokens.shape
    experts = lax.axis_size("expert")
    dps = lax.axis_size("dp")
    top_count = routes.shape[1]
    capacity = min(tok_rows, 2 * tok_rows * top_count // experts)
    rows = experts * capacity
    hidden_units = w_gate_up.shape[2] // 2
    part = hidden_units // QUARTERS
    step = part // dps
    core = lax.axis_index("core")
    zl = lax.axis_index("zl")

    far_tokens = lax.ppermute(tokens, "zl", SWAP)
    far_cotangent = lax.ppermute(cotangent, "zl", SWAP)
    tokens, cotangent, w_gate_up = lax.optimization_barrier((tokens, cotangent, w_gate_up))

    matches = slots_of(routes, experts, capacity)
    select = jnp.sum(
        matches.reshape(rows, tok_rows, top_count).astype(F32), axis=2
    ).astype(BF)
    w = w_gate_up[0].reshape(width, 2, dps, ZL, CORE, step).transpose(3, 4, 0, 1, 2, 5)
    w_mine, w_beside = to_quarters(w.reshape(ZL, CORE, width, 2 * part), zl, core, ())

    weights_slot = jnp.sum(jnp.where(matches, route_weight.reshape(1, -1), 0.0), axis=1)
    sent = dot(
        select, jnp.concatenate([tokens, far_tokens, cotangent, far_cotangent], axis=1)
    )
    is_token = jnp.arange(4 * width, dtype=jnp.int32)[None, :] < 2 * width
    sent = (sent * jnp.where(is_token, 1.0, weights_slot[:, None])).astype(BF)
    mine = exchange(sent.reshape(experts, capacity, 4 * width), "expert")
    mine = mine.reshape(rows, 4 * width)
    beside = lax.ppermute(mine, "core", SWAP)

    partial = dot(mine[:, : 2 * width], w_mine.reshape(2 * width, 2 * part))
    partial += dot(beside[:, : 2 * width], w_beside.reshape(2 * width, 2 * part))
    groups = XH * ZH
    moved = exchange(partial.astype(BF).reshape(groups, rows // groups, 2 * part), SPREAD)
    gate_up = jnp.sum(moved.astype(F32), axis=0)
    hidden = (jax.nn.silu(gate_up[:, :part]) * gate_up[:, part:]).astype(BF)
    hidden = exchange(jnp.broadcast_to(hidden[None], (groups,) + hidden.shape), SPREAD)
    hidden = hidden.reshape(rows, part)

    by_core = pick(core, jnp.stack([mine[:, 2 * width :], beside[:, 2 * width :]]))
    by_core = [pick(zl, jnp.stack([g[:, :width], g[:, width:]])) for g in by_core]
    slot_grads = [by_core[c][h] for h in range(ZL) for c in range(CORE)]
    slot_grads = jnp.concatenate(slot_grads, axis=1)

    down = w_down[0].reshape(dps, ZL, CORE, step, width).transpose(1, 2, 0, 3, 4)
    down = after(down.reshape(ZL, CORE, part, width), sent)
    down_mine, down_beside = to_quarters(down, zl, core, mine)
    terms = dot(hidden, jnp.concatenate([down_beside[0], down_beside[1]], axis=1))
    came = lax.ppermute(terms, "core", SWAP)
    terms = dot(hidden, jnp.concatenate([down_mine[0], down_mine[1]], axis=1)) + came
    far_terms = terms[:, width:].astype(BF)
    outputs = terms[:, :width] + lax.ppermute(far_terms, "zl", SWAP).astype(F32)

    grads = lax.dot_general(
        hidden, slot_grads, (((0,), (0,)), ((), ())), preferred_element_type=F32
    ).astype(BF)
    grads = jnp.stack(
        [g.reshape(dps, step, width) for g in jnp.split(grads, QUARTERS, axis=1)], axis=1
    )
    moved = exchange(grads.reshape(dps * QUARTERS, step, width), ("dp", "zl", "core"))
    moved = moved.reshape(dps, QUARTERS * step, width)
    grad_share = jnp.sum(moved.astype(F32), axis=0)
    return outputs.astype(BF), grad_share[None]


def solution(mesh):
    dps, experts = mesh.shape["dp"], mesh.shape["expert"]
    fine = Mesh(
        mesh.devices.reshape(dps, experts, XH, ZH, ZL, CORE),
        ("dp", "expert", "xh", "zh", "zl", "core"),
    )
    tensor = ("xh", "zh", "zl", "core")
    in_specs = (
        P(("dp", "expert"), tensor),
        P(("dp", "expert"), tensor),
        P(("dp", "expert"), None),
        P(("dp", "expert"), None),
        P("expert", tensor, None),
        P("expert", None, tensor),
    )
    out_specs = (P(("dp", "expert"), tensor), P("expert", "dp", tensor))
    return jax.shard_map(
        per_device, mesh=fine, in_specs=in_specs, out_specs=out_specs, check_vma=False
    )
```

time: 134 us -> 142 us (1.060)
  blocking collectives: 32.3 us -> 0 us
  waiting for transfers between devices: 26.6 us -> 46.9 us
  starting transfers between devices: 61.9 us -> 79.5 us
  other arithmetic: 2.89 us -> 4.38 us
    all_to_all x1 -> x0, blocking collectives: 32.3 us -> none  [exchange(): return lax.all_to_all(pieces, axes, split_axis=0, concat_axis=0, tiled=True)]
    ppermute x4 -> x6, waiting for transfers between devices: 4.39 us -> 29.8 us  [the longest x2 24.9 us: to_quarters(): far = after(lax.ppermute(sent, 'zl', SWAP), earlier)]
    all_to_all x3 -> x4, starting transfers between devices: 26.4 us -> 39.4 us  [exchange(): return lax.all_to_all(pieces, axes, split_axis=0, concat_axis=0, tiled=True)]
    ppermute x4 -> x6, starting transfers between devices: 15.3 us -> 22 us  [the longest x2 6.71 us: to_quarters(): far = after(lax.ppermute(sent, 'zl', SWAP), earlier)]
    all_to_all x3 -> x4, waiting for transfers between devices: 21.7 us -> 16.4 us  [exchange(): return lax.all_to_all(pieces, axes, split_axis=0, concat_axis=0, tiled=True)]
    ppermute x1, starting transfers between devices: 8.09 us -> 3.32 us  [per_device(): beside = lax.ppermute(mine, 'core', SWAP)]
    ppermute x1 -> x2, starting transfers between devices: 12.1 us -> 14.7 us  [to_quarters(): beside = lax.ppermute(jnp.stack([near_sent, far_sent]), 'core', SWAP)]
    optimization_barrier x0 -> x1, local copies, waits for them, and re-layouts: none -> 1.5 us  [per_device(): lax.optimization_barrier((tokens, cotangent, w_gate_up))]
  transfers between devices with their start and end apart: 9 -> 13, of which waited for: 5 -> 6; matrix products, arithmetic and copies ran while one was open for 7% -> 7% of each run, Pallas kernels for 0% -> 0%
where the time goes in v6:
time: 142 us; the launch traced here: 141 us
  starting transfers between devices  79.5 us (56%)
  waiting for transfers between devices  46.9 us (33%)
  local copies, waits for them, and re-layouts  5.22 us (4%)
  other arithmetic  4.38 us (3%)
  matrix products  3.69 us (3%)
    all_to_all x4, starting transfers between devices, exchange(): return lax.all_to_all(pieces, axes, split_axis=0, concat_axis=0, tiled=True)  39.4 us
    ppermute x2, waiting for transfers between devices, to_quarters(): far = after(lax.ppermute(sent, 'zl', SWAP), earlier)  24.9 us
    all_to_all x4, waiting for transfers between devices, exchange(): return lax.all_to_all(pieces, axes, split_axis=0, concat_axis=0, tiled=True)  16.4 us
    ppermute x2, starting transfers between devices, to_quarters(): beside = lax.ppermute(jnp.stack([near_sent, far_sent]), 'core', SWAP)  14.7 us
    ppermute x2, starting transfers between devices, to_quarters(): far = after(lax.ppermute(sent, 'zl', SWAP), earlier)  6.71 us
    ppermute x1, starting transfers between devices, per_device(): far_tokens = lax.ppermute(tokens, 'zl', SWAP)  5.87 us
    ppermute x1, waiting for transfers between devices, per_device(): outputs = terms[:, :width] + lax.ppermute(far_terms, 'zl', SWAP).astype(F32)  4.87 us
    ppermute x1, starting transfers between devices, per_device(): came = lax.ppermute(terms, 'core', SWAP)  4.23 us
  transfers between devices with their start and end apart: 13, of which 6 were waited for; matrix products, arithmetic and copies ran while one was open for 7% of the time, Pallas kernels for 0%

profile of v6, /device:TPU:1, one launch (start us, length us, event | category | flops | bytes accessed | tf_op | source)
XLA Modules:
  0.0 140.7 jit_solution(6572186827619693249)
XLA Ops:
  0.6 0.0 copy-start.2
  0.6 0.0 copy-start.1
  0.6 5.9 %collective-permute-start = (bf16[128,128]{1,0:T(8,128)(2,1)}, bf16[128,128]{1,0:T(8,128)(2,1)S(1)}, u32[]{:S(2)}, u32[]{:S(2)}) collective-permute-start(bf16[128,128]{1,0:T(8,128)(2,1)} %param.6), channel_id=1, source_target_pairs={{0,2},{2,0},{1,3},{3,1},{4,6},{6,4},{5,7},{7,5},{8,10},{10,8},{9,1... | collective-permute-start | bytes 98312 | tf_op jit(solution)/shard_map/ppermute | solution.py:63
  6.5 1.9 %collective-permute-start.1 = (bf16[128,128]{1,0:T(8,128)(2,1)}, bf16[128,128]{1,0:T(8,128)(2,1)S(1)}, u32[]{:S(2)}, u32[]{:S(2)}) collective-permute-start(bf16[128,128]{1,0:T(8,128)(2,1)} %param.7), channel_id=1, source_target_pairs={{0,2},{2,0},{1,3},{3,1},{4,6},{6,4},{5,7},{7,5},{8,10},{10,8},{9,1... | collective-permute-start | bytes 98312 | tf_op jit(solution)/shard_map/ppermute | solution.py:64
  8.5 0.8 copy.49
  9.2 0.1 eq.59
  9.4 0.1 eq.63
  9.5 0.6 reduce-window.6
  10.1 0.2 slice_reduce_fusion
  10.4 0.1 fusion.29
  10.5 0.1 reduce_sum.48
  10.6 0.1 copy.51
  10.7 0.7 multiply_add_fusion.1
  11.4 0.8 copy.52
  12.2 0.1 broadcast_in_dim.50
  12.3 0.1 convert_reduce_fusion.2
  12.4 0.1 select_reduce_fusion
  12.6 1.5 %copy.53 = bf16[1,128,3072]{1,2,0:T(8,128)(2,1)S(1)} copy(bf16[1,128,3072]{2,1,0:T(8,128)(2,1)} %param.10) | data formatting | bytes 1572864 | tf_op jit(solution)/shard_map/optimization_barrier | solution.py:65
  14.1 0.0 collective-permute-done
  14.1 0.0 collective-permute-done.1
  14.1 0.0 copy-done.2
  14.1 0.0 copy-done.1
  14.1 1.1 fusion
  15.2 7.3 %all-to-all-start = ((bf16[8,64,512]{2,1,0:T(8,128)(2,1)}), bf16[8,64,512]{2,1,0:T(8,128)(2,1)S(1)}, u32[]{:S(2)}, u32[]{:S(2)}) async-start(bf16[8,64,512]{2,1,0:T(8,128)(2,1)} %bitcast.2), calls=%async_computation | async-start | bytes 1048576 | tf_op jit(solution)/shard_map/all_to_all | solution.py:15
  22.5 0.1 broadcast_select_fusion.1
  22.6 3.4 %collective-permute-start.2 = (bf16[2,128,768]{1,2,0:T(8,128)(2,1)S(1)}, bf16[2,128,768]{1,2,0:T(8,128)(2,1)S(1)}, u32[]{:S(2)}, u32[]{:S(2)}) collective-permute-start(bf16[2,128,768]{1,2,0:T(8,128)(2,1)S(1)} %bitcast.78), channel_id=1, source_target_pairs={{0,2},{2,0},{1,3},{3,1},{4,6},{6,4},{5,7},{7,5},{8,10},{10,8},{9,1... | collective-permute-start | bytes 1179656 | tf_op jit(solution)/shard_map/ppermute | solution.py:42
  26.0 5.1 %collective-permute-done.2 = bf16[2,128,768]{1,2,0:T(8,128)(2,1)S(1)} collective-permute-done((bf16[2,128,768]{1,2,0:T(8,128)(2,1)S(1)}, bf16[2,128,768]{1,2,0:T(8,128)(2,1)S(1)}, u32[]{:S(2)}, u32[]{:S(2)}) %collective-permute-start.2) | collective-permute-done | bytes 393248 | tf_op jit(solution)/shard_map/ppermute | solution.py:42
  31.2 11.6 %collective-permute-start.4 = (bf16[2,128,768]{1,2,0:T(8,128)(2,1)S(1)}, bf16[2,128,768]{1,2,0:T(8,128)(2,1)S(1)}, u32[]{:S(2)}, u32[]{:S(2)}) collective-permute-start(bf16[2,128,768]{1,2,0:T(8,128)(2,1)S(1)} %pad_maximum_fusion.1), channel_id=1, source_target_pairs={{0,1},{1,0},{2,3},{3,2},{4,5},{5,4},{6,7},{7,6},{8,9},{9,8},{10,11... | collective-permute-start | bytes 1179656 | tf_op jit(solution)/shard_map/ppermute | solution.py:46
  42.8 0.0 all-to-all-done
  42.8 3.3 %collective-permute-start.3 = (bf16[512,512]{1,0:T(8,128)(2,1)S(1)}, bf16[512,512]{1,0:T(8,128)(2,1)S(1)}, u32[]{:S(2)}, u32[]{:S(2)}) collective-permute-start(bf16[512,512]{1,0:T(8,128)(2,1)S(1)} %bitcast.64), channel_id=1, source_target_pairs={{0,1},{1,0},{2,3},{3,2},{4,5},{5,4},{6,7},{7,6},{8,9},{9,8},{10,11... | collective-permute-start | bytes 1572872 | tf_op jit(solution)/shard_map/ppermute | solution.py:82
  46.2 0.2 copy.55
  46.4 0.0 collective-permute-done.4
  46.4 0.2 copy.56
  46.6 0.4 fusion.10
  46.9 0.7 collective-permute-done.3
  47.7 0.0 copy-start
  47.7 1.3 add_convert_fusion
  48.9 16.2 %all-to-all-start.1 = ((bf16[8,64,768]{2,1,0:T(8,128)(2,1)}), bf16[8,64,768]{2,1,0:T(8,128)(2,1)S(1)}, u32[]{:S(2)}, u32[]{:S(2)}) async-start(bf16[8,64,768]{2,1,0:T(8,128)(2,1)} %bitcast.12), calls=%async_computation.1 | async-start | bytes 1572864 | tf_op jit(solution)/shard_map/all_to_all | solution.py:15
  65.1 0.0 copy-done
  65.2 3.4 %collective-permute-start.5 = (bf16[2,384,128]{2,1,0:T(8,128)(2,1)S(1)}, bf16[2,384,128]{2,1,0:T(8,128)(2,1)S(1)}, u32[]{:S(2)}, u32[]{:S(2)}) collective-permute-start(bf16[2,384,128]{2,1,0:T(8,128)(2,1)S(1)} %get-tuple-element.21), channel_id=1, source_target_pairs={{0,2},{2,0},{1,3},{3,1},{4,6},{6,4},{5,7},{7,5},{8,10},{10,8},{9,1... | collective-permute-start | bytes 589832 | tf_op jit(solution)/shard_map/ppermute | solution.py:42
  68.6 19.8 %collective-permute-done.5 = bf16[2,384,128]{2,1,0:T(8,128)(2,1)S(1)} collective-permute-done((bf16[2,384,128]{2,1,0:T(8,128)(2,1)S(1)}, bf16[2,384,128]{2,1,0:T(8,128)(2,1)S(1)}, u32[]{:S(2)}, u32[]{:S(2)}) %collective-permute-start.5) | collective-permute-done | bytes 196640 | tf_op jit(solution)/shard_map/ppermute | solution.py:42
  88.5 3.1 %collective-permute-start.6 = (bf16[2,384,128]{2,1,0:T(8,128)(2,1)S(1)}, bf16[2,384,128]{2,1,0:T(8,128)(2,1)S(1)}, u32[]{:S(2)}, u32[]{:S(2)}) collective-permute-start(bf16[2,384,128]{2,1,0:T(8,128)(2,1)S(1)} %pad_maximum_fusion.3), channel_id=1, source_target_pairs={{0,1},{1,0},{2,3},{3,2},{4,5},{5,4},{6,7},{7,6},{8,9},{9,8},{10,11... | collective-permute-start | bytes 589832 | tf_op jit(solution)/shard_map/ppermute | solution.py:46
  91.6 0.0 all-to-all-done.1
  91.6 0.1 convert_reduce_fusion
  91.7 0.8 broadcast_in_dim.54
  92.5 10.2 %all-to-all-start.2 = ((bf16[8,64,384]{2,1,0:T(8,128)(2,1)}), bf16[8,64,384]{2,1,0:T(8,128)(2,1)S(1)}, u32[]{:S(2)}, u32[]{:S(2)}) async-start(bf16[8,64,384]{2,1,0:T(8,128)(2,1)} %broadcast_in_dim.54), calls=%async_computation.2 | async-start | bytes 786432 | tf_op jit(solution)/shard_map/all_to_all | solution.py:15
  102.7 0.0 collective-permute-done.6
  102.8 13.7 %all-to-all-done.2 = bf16[8,64,384]{2,1,0:T(8,128)(2,1)S(1)} async-done(((bf16[8,64,384]{2,1,0:T(8,128)(2,1)}), bf16[8,64,384]{2,1,0:T(8,128)(2,1)S(1)}, u32[]{:S(2)}, u32[]{:S(2)}) %all-to-all-start.2) | async-done | bytes 393248 | tf_op jit(solution)/shard_map/all_to_all | solution.py:15
  116.5 0.3 fusion.15
  116.8 4.2 %collective-permute-start.7 = (f32[512,256]{1,0:T(8,128)S(1)}, f32[512,256]{1,0:T(8,128)S(1)}, u32[]{:S(2)}, u32[]{:S(2)}) collective-permute-start(f32[512,256]{1,0:T(8,128)S(1)} %fusion.15), channel_id=1, source_target_pairs={{0,1},{1,0},{2,3},{3,2},{4,5},{5,4},{6,7},{7,6},{8,9},{9,8},{10,11... | collective-permute-start | bytes 1572872 | tf_op jit(solution)/shard_map/ppermute | solution.py:102
  121.0 0.4 convolution_convert_fusion
  121.4 0.1 fusion.35
  121.5 0.8 pad_maximum_fusion.2
  122.3 5.8 %all-to-all-start.3 = ((bf16[16,96,128]{2,1,0:T(8,128)(2,1)}), bf16[16,96,128]{2,1,0:T(8,128)(2,1)S(1)}, u32[]{:S(2)}, u32[]{:S(2)}) async-start(bf16[16,96,128]{2,1,0:T(8,128)(2,1)} %bitcast.31), calls=%async_computation.3 | async-start | bytes 786432 | tf_op jit(solution)/shard_map/all_to_all | solution.py:15
  128.1 0.0 collective-permute-done.7
  128.1 0.3 convolution_add_fusion
  128.5 3.3 %collective-permute-start.8 = (bf16[512,128]{1,0:T(8,128)(2,1)S(1)}, bf16[512,128]{1,0:T(8,128)(2,1)S(1)}, u32[]{:S(2)}, u32[]{:S(2)}) collective-permute-start(bf16[512,128]{1,0:T(8,128)(2,1)S(1)} %slice.205), channel_id=1, source_target_pairs={{0,2},{2,0},{1,3},{3,1},{4,6},{6,4},{5,7},{7,5},{8,10},{10,8},{9,1... | collective-permute-start | bytes 393224 | tf_op jit(solution)/shard_map/ppermute | solution.py:105
  131.8 4.9 %collective-permute-done.8 = bf16[512,128]{1,0:T(8,128)(2,1)S(1)} collective-permute-done((bf16[512,128]{1,0:T(8,128)(2,1)S(1)}, bf16[512,128]{1,0:T(8,128)(2,1)S(1)}, u32[]{:S(2)}, u32[]{:S(2)}) %collective-permute-start.8) | collective-permute-done | bytes 131104 | tf_op jit(solution)/shard_map/ppermute | solution.py:105
  136.6 0.7 fusion.8
  137.3 2.7 %all-to-all-done.3 = bf16[16,96,128]{2,1,0:T(8,128)(2,1)S(1)} async-done(((bf16[16,96,128]{2,1,0:T(8,128)(2,1)}), bf16[16,96,128]{2,1,0:T(8,128)(2,1)S(1)}, u32[]{:S(2)}, u32[]{:S(2)}) %all-to-all-start.3) | async-done | bytes 393248 | tf_op jit(solution)/shard_map/all_to_all | solution.py:15
  140.0 0.7 convert_reduce_fusion.1
  (20 shorter events, 0.5 us)
Async XLA Ops:
  0.6 13.5 %copy-start.2 = (bf16[128,128]{1,0:T(8,128)(2,1)S(1)}, bf16[128,128]{1,0:T(8,128)(2,1)}, u32[]{:S(2)}) copy-start(bf16[128,128]{1,0:T(8,128)(2,1)} %param.6) | copy-start | bytes 98308
  0.6 13.5 %copy-start.1 = (bf16[128,128]{1,0:T(8,128)(2,1)S(1)}, bf16[128,128]{1,0:T(8,128)(2,1)}, u32[]{:S(2)}) copy-start(bf16[128,128]{1,0:T(8,128)(2,1)} %param.7) | copy-start | bytes 98308
  0.6 13.4 %collective-permute-start = (bf16[128,128]{1,0:T(8,128)(2,1)}, bf16[128,128]{1,0:T(8,128)(2,1)S(1)}, u32[]{:S(2)}, u32[]{:S(2)}) collective-permute-start(bf16[128,128]{1,0:T(8,128)(2,1)} %param.6), channel_id=1, source_target_pairs={{0,2},{2,0},{1,3},{3,1},{4,6},{6,4},{5,7},{7,5},{8,10},{10,8},{9,1... | collective-permute-start | bytes 98312 | tf_op jit(solution)/shard_map/ppermute | solution.py:63
  6.5 7.6 %collective-permute-start.1 = (bf16[128,128]{1,0:T(8,128)(2,1)}, bf16[128,128]{1,0:T(8,128)(2,1)S(1)}, u32[]{:S(2)}, u32[]{:S(2)}) collective-permute-start(bf16[128,128]{1,0:T(8,128)(2,1)} %param.7), channel_id=1, source_target_pairs={{0,2},{2,0},{1,3},{3,1},{4,6},{6,4},{5,7},{7,5},{8,10},{10,8},{9,1... | collective-permute-start | bytes 98312 | tf_op jit(solution)/shard_map/ppermute | solution.py:64
  15.2 27.6 %all-to-all-start = ((bf16[8,64,512]{2,1,0:T(8,128)(2,1)}), bf16[8,64,512]{2,1,0:T(8,128)(2,1)S(1)}, u32[]{:S(2)}, u32[]{:S(2)}) async-start(bf16[8,64,512]{2,1,0:T(8,128)(2,1)} %bitcast.2), calls=%async_computation | async-start | bytes 1048576 | tf_op jit(solution)/shard_map/all_to_all | solution.py:15
  22.6 8.5 %collective-permute-start.2 = (bf16[2,128,768]{1,2,0:T(8,128)(2,1)S(1)}, bf16[2,128,768]{1,2,0:T(8,128)(2,1)S(1)}, u32[]{:S(2)}, u32[]{:S(2)}) collective-permute-start(bf16[2,128,768]{1,2,0:T(8,128)(2,1)S(1)} %bitcast.78), channel_id=1, source_target_pairs={{0,2},{2,0},{1,3},{3,1},{4,6},{6,4},{5,7},{7,5},{8,10},{10,8},{9,1... | collective-permute-start | bytes 1179656 | tf_op jit(solution)/shard_map/ppermute | solution.py:42
  31.2 15.2 %collective-permute-start.4 = (bf16[2,128,768]{1,2,0:T(8,128)(2,1)S(1)}, bf16[2,128,768]{1,2,0:T(8,128)(2,1)S(1)}, u32[]{:S(2)}, u32[]{:S(2)}) collective-permute-start(bf16[2,128,768]{1,2,0:T(8,128)(2,1)S(1)} %pad_maximum_fusion.1), channel_id=1, source_target_pairs={{0,1},{1,0},{2,3},{3,2},{4,5},{5,4},{6,7},{7,6},{8,9},{9,8},{10,11... | collective-permute-start | bytes 1179656 | tf_op jit(solution)/shard_map/ppermute | solution.py:46
  42.8 4.8 %collective-permute-start.3 = (bf16[512,512]{1,0:T(8,128)(2,1)S(1)}, bf16[512,512]{1,0:T(8,128)(2,1)S(1)}, u32[]{:S(2)}, u32[]{:S(2)}) collective-permute-start(bf16[512,512]{1,0:T(8,128)(2,1)S(1)} %bitcast.64), channel_id=1, source_target_pairs={{0,1},{1,0},{2,3},{3,2},{4,5},{5,4},{6,7},{7,6},{8,9},{9,8},{10,11... | collective-permute-start | bytes 1572872 | tf_op jit(solution)/shard_map/ppermute | solution.py:82
  47.7 17.5 %copy-start = (bf16[1,1536,128]{2,1,0:T(8,128)(2,1)S(1)}, bf16[1,1536,128]{2,1,0:T(8,128)(2,1)}, u32[]{:S(2)}) copy-start(bf16[1,1536,128]{2,1,0:T(8,128)(2,1)} %param.11) | copy-start | bytes 1179652
  48.9 42.7 %all-to-all-start.1 = ((bf16[8,64,768]{2,1,0:T(8,128)(2,1)}), bf16[8,64,768]{2,1,0:T(8,128)(2,1)S(1)}, u32[]{:S(2)}, u32[]{:S(2)}) async-start(bf16[8,64,768]{2,1,0:T(8,128)(2,1)} %bitcast.12), calls=%async_computation.1 | async-start | bytes 1572864 | tf_op jit(solution)/shard_map/all_to_all | solution.py:15
  65.2 23.2 %collective-permute-start.5 = (bf16[2,384,128]{2,1,0:T(8,128)(2,1)S(1)}, bf16[2,384,128]{2,1,0:T(8,128)(2,1)S(1)}, u32[]{:S(2)}, u32[]{:S(2)}) collective-permute-start(bf16[2,384,128]{2,1,0:T(8,128)(2,1)S(1)} %get-tuple-element.21), channel_id=1, source_target_pairs={{0,2},{2,0},{1,3},{3,1},{4,6},{6,4},{5,7},{7,5},{8,10},{10,8},{9,1... | collective-permute-start | bytes 589832 | tf_op jit(solution)/shard_map/ppermute | solution.py:42
  88.5 14.2 %collective-permute-start.6 = (bf16[2,384,128]{2,1,0:T(8,128)(2,1)S(1)}, bf16[2,384,128]{2,1,0:T(8,128)(2,1)S(1)}, u32[]{:S(2)}, u32[]{:S(2)}) collective-permute-start(bf16[2,384,128]{2,1,0:T(8,128)(2,1)S(1)} %pad_maximum_fusion.3), channel_id=1, source_target_pairs={{0,1},{1,0},{2,3},{3,2},{4,5},{5,4},{6,7},{7,6},{8,9},{9,8},{10,11... | collective-permute-start | bytes 589832 | tf_op jit(solution)/shard_map/ppermute | solution.py:46
  92.5 24.0 %all-to-all-start.2 = ((bf16[8,64,384]{2,1,0:T(8,128)(2,1)}), bf16[8,64,384]{2,1,0:T(8,128)(2,1)S(1)}, u32[]{:S(2)}, u32[]{:S(2)}) async-start(bf16[8,64,384]{2,1,0:T(8,128)(2,1)} %broadcast_in_dim.54), calls=%async_computation.2 | async-start | bytes 786432 | tf_op jit(solution)/shard_map/all_to_all | solution.py:15
  116.8 11.3 %collective-permute-start.7 = (f32[512,256]{1,0:T(8,128)S(1)}, f32[512,256]{1,0:T(8,128)S(1)}, u32[]{:S(2)}, u32[]{:S(2)}) collective-permute-start(f32[512,256]{1,0:T(8,128)S(1)} %fusion.15), channel_id=1, source_target_pairs={{0,1},{1,0},{2,3},{3,2},{4,5},{5,4},{6,7},{7,6},{8,9},{9,8},{10,11... | collective-permute-start | bytes 1572872 | tf_op jit(solution)/shard_map/ppermute | solution.py:102
  122.3 17.7 %all-to-all-start.3 = ((bf16[16,96,128]{2,1,0:T(8,128)(2,1)}), bf16[16,96,128]{2,1,0:T(8,128)(2,1)S(1)}, u32[]{:S(2)}, u32[]{:S(2)}) async-start(bf16[16,96,128]{2,1,0:T(8,128)(2,1)} %bitcast.31), calls=%async_computation.3 | async-start | bytes 786432 | tf_op jit(solution)/shard_map/all_to_all | solution.py:15
  128.5 8.2 %collective-permute-start.8 = (bf16[512,128]{1,0:T(8,128)(2,1)S(1)}, bf16[512,128]{1,0:T(8,128)(2,1)S(1)}, u32[]{:S(2)}, u32[]{:S(2)}) collective-permute-start(bf16[512,128]{1,0:T(8,128)(2,1)S(1)} %slice.205), channel_id=1, source_target_pairs={{0,2},{2,0},{1,3},{3,1},{4,6},{6,4},{5,7},{7,5},{8,10},{10,8},{9,1... | collective-permute-start | bytes 393224 | tf_op jit(solution)/shard_map/ppermute | solution.py:105

commit v7 on v5

--- a/solution.py
+++ b/solution.py
@@ -32,9 +32,13 @@
     return jnp.arange(experts * capacity, dtype=jnp.int32)[:, None] == target[None, :]
 
 
-def to_quarters(blocks, xh, core):
+def after(array, earlier):
+    return lax.optimization_barrier((array, earlier))[0]
+
+
+def to_quarters(blocks, xh, core, earlier=()):
     near, sent = pick(xh, blocks)
-    far = lax.ppermute(sent, "xh", SWAP)
+    far = after(lax.ppermute(sent, "xh", SWAP), earlier)
     near_mine, near_sent = pick(core, near)
     far_mine, far_sent = pick(core, far)
     mine = jnp.stack([near_mine, far_mine])
@@ -56,6 +60,7 @@
     xh = lax.axis_index("xh")
 
     far_tokens = lax.ppermute(tokens, "xh", SWAP)
+    tokens, cotangent, w_gate_up = lax.optimization_barrier((tokens, cotangent, w_gate_up))
 
     matches = slots_of(routes, experts, capacity)
     select = jnp.sum(
@@ -79,31 +84,35 @@
     moved = exchange(partial.astype(BF).reshape(Z, rows // Z, 2 * part), "z")
     gate_up = jnp.sum(moved.astype(F32), axis=0)
     hidden = (jax.nn.silu(gate_up[:, :part]) * gate_up[:, part:]).astype(BF)
-    hidden = exchange(jnp.broadcast_to(hidden[None], (XH * Z,) + hidden.shape), ("xh", "z"))
-    hidden = hidden.reshape(XH, rows, part)
-
-    slot_grads = pick(core, jnp.stack([mine[:, 2 * width :], beside[:, 2 * width :]]))
-
-    def grads_of(half, g):
-        out = lax.dot_general(half, g, (((0,), (0,)), ((), ())), preferred_element_type=F32)
-        return out.astype(BF).reshape(dps, step, width)
-
-    grads = jnp.stack(
-        [jnp.stack([grads_of(hidden[h], g) for h in range(XH)], axis=1) for g in slot_grads],
-        axis=1,
-    )
-    moved = exchange(grads.reshape(dps * CORE, XH * step, width), ("dp", "core"))
-    moved = jnp.sum(moved.reshape(dps, CORE, XH, step, width).astype(F32), axis=0)
-    grad_share = moved.transpose(1, 0, 2, 3).reshape(QUARTERS * step, width)
+    hidden = exchange(jnp.broadcast_to(hidden[None], (Z,) + hidden.shape), "z")
+    hidden = hidden.reshape(rows, part)
 
     down = w_down[0].reshape(dps, XH, CORE, step, width).transpose(2, 1, 0, 3, 4)
-    down_mine, down_sent = pick(core, down.reshape(CORE, XH, part, width))
-    down_beside = lax.ppermute(down_sent, "core", SWAP)
+    down_near, down_sent = pick(core, after(down.reshape(CORE, XH, part, width), sent))
+    down_near = jnp.stack([down_near, lax.ppermute(down_sent, "core", SWAP)], axis=1)
+    down_near, down_sent = pick(xh, after(down_near, mine))
+    down_far = lax.ppermute(down_sent, "xh", SWAP)
 
-    def terms(down):
-        return dot(hidden[0], down[0]) + dot(hidden[1], down[1])
+    near_grads = jnp.stack([mine[:, 2 * width :], beside[:, 2 * width :]])
+    far_grads = after(lax.ppermute(near_grads, "xh", SWAP), down_far)
+    by_xh = pick(xh, jnp.stack([near_grads, far_grads]))
+    slot_grads = jnp.concatenate([g for pair in by_xh for g in pick(core, pair)], axis=1)
 
-    outputs = terms(down_mine) + lax.ppermute(terms(down_beside), "core", SWAP)
+    terms = dot(hidden, jnp.concatenate([down_near[1], down_far[1]], axis=1))
+    came = lax.ppermute(terms, "core", SWAP)
+    terms = dot(hidden, jnp.concatenate([down_near[0], down_far[0]], axis=1)) + came
+    far_terms = terms[:, width:].astype(BF)
+    outputs = terms[:, :width] + lax.ppermute(far_terms, "xh", SWAP).astype(F32)
+
+    grads = lax.dot_general(
+        hidden, slot_grads, (((0,), (0,)), ((), ())), preferred_element_type=F32
+    ).astype(BF)
+    grads = jnp.stack(
+        [g.reshape(dps, step, width) for g in jnp.split(grads, QUARTERS, axis=1)], axis=1
+    )
+    moved = exchange(grads.reshape(dps * QUARTERS, step, width), ("dp", "xh", "core"))
+    moved = moved.reshape(dps, QUARTERS * step, width)
+    grad_share = jnp.sum(moved.astype(F32), axis=0)
     return outputs.astype(BF), grad_share[None]
 
 

time: 134 us -> 135 us (level)
  blocking collectives: 32.3 us -> 0 us
  starting transfers between devices: 61.9 us -> 80.1 us
  waiting for transfers between devices: 26.6 us -> 39 us
  other arithmetic: 2.89 us -> 4.73 us
    all_to_all x1 -> x0, blocking collectives: 32.3 us -> none  [exchange(): return lax.all_to_all(pieces, axes, split_axis=0, concat_axis=0, tiled=True)]
    ppermute x3 -> x6, starting transfers between devices: 7.36 us -> 32.7 us  [the longest x1 12 us: per_device(): lax.ppermute(down_sent, 'core', SWAP)]
    ppermute x1, starting transfers between devices: 12.1 us -> 3.44 us  [to_quarters(): beside = lax.ppermute(jnp.stack([near_sent, far_sent]), 'core', SWAP)]
    ppermute x3 -> x6, waiting for transfers between devices: 4.38 us -> 10.8 us  [the longest x1 10.8 us: per_device(): outputs = terms[:, :width] + lax.ppermute(far_terms, 'xh', SWAP).astype(F32)]
    all_to_all x3 -> x4, waiting for transfers between devices: 21.7 us -> 28.2 us  [exchange(): return lax.all_to_all(pieces, axes, split_axis=0, concat_axis=0, tiled=True)]
    all_to_all x3 -> x4, starting transfers between devices: 26.4 us -> 27.9 us  [exchange(): return lax.all_to_all(pieces, axes, split_axis=0, concat_axis=0, tiled=True)]
    unnamed x13 -> x12, local copies, waits for them, and re-layouts: 1.76 us -> 0.26 us
    optimization_barrier x0 -> x1, local copies, waits for them, and re-layouts: none -> 1.5 us  [per_device(): lax.optimization_barrier((tokens, cotangent, w_gate_up))]
  transfers between devices with their start and end apart: 9 -> 13, of which waited for: 5 -> 3; matrix products, arithmetic and copies ran while one was open for 7% -> 9% of each run, Pallas kernels for 0% -> 0%
where the time goes in v7:
time: 135 us; the launch traced here: 134 us
  starting transfers between devices  80.1 us (59%)
  waiting for transfers between devices  39 us (29%)
  local copies, waits for them, and re-layouts  4.9 us (4%)
  other arithmetic  4.73 us (4%)
  matrix products  3.61 us (3%)
    all_to_all x4, waiting for transfers between devices, exchange(): return lax.all_to_all(pieces, axes, split_axis=0, concat_axis=0, tiled=True)  28.2 us
    all_to_all x4, starting transfers between devices, exchange(): return lax.all_to_all(pieces, axes, split_axis=0, concat_axis=0, tiled=True)  27.9 us
    ppermute x1, starting transfers between devices, per_device(): lax.ppermute(down_sent, 'core', SWAP)  12 us
    ppermute x1, waiting for transfers between devices, per_device(): outputs = terms[:, :width] + lax.ppermute(far_terms, 'xh', SWAP).astype(F32)  10.8 us
    ppermute x1, starting transfers between devices, per_device(): beside = lax.ppermute(mine, 'core', SWAP)  8.1 us
    ppermute x1, starting transfers between devices, per_device(): far_tokens = lax.ppermute(tokens, 'xh', SWAP)  7.94 us
    ppermute x1, starting transfers between devices, per_device(): outputs = terms[:, :width] + lax.ppermute(far_terms, 'xh', SWAP).astype(F32)  7.2 us
    ppermute x1, starting transfers between devices, per_device(): down_far = lax.ppermute(down_sent, 'xh', SWAP)  7.11 us
  transfers between devices with their start and end apart: 13, of which 3 were waited for; matrix products, arithmetic and copies ran while one was open for 9% of the time, Pallas kernels for 0%

profile of v7, /device:TPU:1, one launch (start us, length us, event | category | flops | bytes accessed | tf_op | source)
XLA Modules:
  0.0 133.5 jit_solution(14563855549722610930)
XLA Ops:
  0.6 7.9 %collective-permute-start = (bf16[128,128]{1,0:T(8,128)(2,1)}, bf16[128,128]{1,0:T(8,128)(2,1)S(1)}, u32[]{:S(2)}, u32[]{:S(2)}) collective-permute-start(bf16[128,128]{1,0:T(8,128)(2,1)} %param.6), channel_id=1, source_target_pairs={{0,16},{16,0},{1,17},{17,1},{2,18},{18,2},{3,19},{19,3},{4,20},{20... | collective-permute-start | bytes 98312 | tf_op jit(solution)/shard_map/ppermute | solution.py:62
  8.6 1.5 %copy.66 = bf16[1,128,3072]{1,2,0:T(8,128)(2,1)S(1)} copy(bf16[1,128,3072]{2,1,0:T(8,128)(2,1)} %param.10) | data formatting | bytes 1572864 | tf_op jit(solution)/shard_map/optimization_barrier | solution.py:63
  10.1 0.0 copy-start.1
  10.1 0.0 copy-start.2
  10.1 0.0 copy-start.3
  10.1 0.0 copy-start.4
  10.2 0.1 broadcast_select_fusion.1
  10.3 1.9 %collective-permute-start.1 = (bf16[2,128,768]{1,2,0:T(8,128)(2,1)S(1)}, bf16[2,128,768]{1,2,0:T(8,128)(2,1)S(1)}, u32[]{:S(2)}, u32[]{:S(2)}) collective-permute-start(bf16[2,128,768]{1,2,0:T(8,128)(2,1)S(1)} %bitcast.101), channel_id=1, source_target_pairs={{0,16},{16,0},{1,17},{17,1},{2,18},{18,2},{3,19},{19,3},{4,20},{20... | collective-permute-start | bytes 1179656 | tf_op jit(solution)/shard_map/ppermute | solution.py:41
  12.2 0.0 copy-done.1
  12.2 0.1 copy.62
  12.3 0.1 eq.62
  12.4 0.1 eq.58
  12.6 0.6 reduce-window.6
  13.2 0.2 slice_reduce_fusion
  13.4 0.1 fusion.28
  13.6 0.1 reduce_sum.48
  13.7 0.0 copy-done.2
  13.7 0.1 copy.65
  13.8 0.1 broadcast_in_dim.50
  14.0 0.1 copy.64
  14.0 0.1 convert_reduce_fusion.2
  14.1 0.1 select_reduce_fusion
  14.3 0.0 collective-permute-done
  14.3 0.0 copy-done.3
  14.3 1.0 fusion
  15.3 7.4 %all-to-all-start = ((bf16[8,64,384]{2,1,0:T(8,128)(2,1)}), bf16[8,64,384]{2,1,0:T(8,128)(2,1)S(1)}, u32[]{:S(2)}, u32[]{:S(2)}) async-start(bf16[8,64,384]{2,1,0:T(8,128)(2,1)} %bitcast.2), calls=%async_computation | async-start | bytes 786432 | tf_op jit(solution)/shard_map/all_to_all | solution.py:14
  22.9 12.0 %collective-permute-start.4 = (bf16[2,384,128]{2,1,0:T(8,128)(2,1)S(1)}, bf16[2,384,128]{2,1,0:T(8,128)(2,1)}, u32[]{:S(2)}, u32[]{:S(2)}) collective-permute-start(bf16[2,384,128]{2,1,0:T(8,128)(2,1)S(1)} %get-tuple-element.23), channel_id=1, source_target_pairs={{0,1},{1,0},{2,3},{3,2},{4,5},{5,4},{6,7},{7,6},{8,9},{9,8},{10,11... | collective-permute-start | bytes 589832 | tf_op jit(solution)/shard_map/ppermute | solution.py:92
  34.9 0.0 collective-permute-done.1
  35.0 3.4 %collective-permute-start.3 = (bf16[2,128,768]{1,2,0:T(8,128)(2,1)S(1)}, bf16[2,128,768]{1,2,0:T(8,128)(2,1)}, u32[]{:S(2)}, u32[]{:S(2)}) collective-permute-start(bf16[2,128,768]{1,2,0:T(8,128)(2,1)S(1)} %pad_maximum_fusion.1), channel_id=1, source_target_pairs={{0,1},{1,0},{2,3},{3,2},{4,5},{5,4},{6,7},{7,6},{8,9},{9,8},{10,11... | collective-permute-start | bytes 1179656 | tf_op jit(solution)/shard_map/ppermute | solution.py:45
  38.4 0.0 all-to-all-done
  38.4 8.1 %collective-permute-start.2 = (bf16[512,384]{1,0:T(8,128)(2,1)S(1)}, bf16[512,384]{1,0:T(8,128)(2,1)S(1)}, u32[]{:S(2)}, u32[]{:S(2)}) collective-permute-start(bf16[512,384]{1,0:T(8,128)(2,1)S(1)} %bitcast.87), channel_id=1, source_target_pairs={{0,1},{1,0},{2,3},{3,2},{4,5},{5,4},{6,7},{7,6},{8,9},{9,8},{10,11... | collective-permute-start | bytes 1179656 | tf_op jit(solution)/shard_map/ppermute | solution.py:80
  46.6 0.2 copy.68
  46.8 0.4 fusion.10
  47.1 0.0 collective-permute-done.3
  47.1 1.2 copy.69
  48.3 0.0 collective-permute-done.2
  48.3 1.3 add_convert_fusion
  49.6 10.2 %all-to-all-start.1 = ((bf16[8,64,768]{2,1,0:T(8,128)(2,1)}), bf16[8,64,768]{2,1,0:T(8,128)(2,1)S(1)}, u32[]{:S(2)}, u32[]{:S(2)}) async-start(bf16[8,64,768]{2,1,0:T(8,128)(2,1)} %bitcast.12), calls=%async_computation.1 | async-start | bytes 1572864 | tf_op jit(solution)/shard_map/all_to_all | solution.py:14
  59.8 0.0 collective-permute-done.4
  59.8 1.0 pad_maximum_fusion.2
  60.7 0.1 fusion.12
  60.8 7.1 %collective-permute-start.5 = (bf16[2,384,128]{2,1,0:T(8,128)(2,1)S(1)}, bf16[2,384,128]{2,1,0:T(8,128)(2,1)S(1)}, u32[]{:S(2)}, u32[]{:S(2)}) collective-permute-start(bf16[2,384,128]{2,1,0:T(8,128)(2,1)S(1)} %fusion.12), channel_id=1, source_target_pairs={{0,16},{16,0},{1,17},{17,1},{2,18},{18,2},{3,19},{19,3},{4,20},{20... | collective-permute-start | bytes 589832 | tf_op jit(solution)/shard_map/ppermute | solution.py:94
  67.9 0.1 bitcast_select_fusion.1
  68.1 2.1 %collective-permute-start.8 = (bf16[2,512,128]{2,1,0:T(8,128)(2,1)S(1)}, bf16[2,512,128]{2,1,0:T(8,128)(2,1)S(1)}, u32[]{:S(2)}, u32[]{:S(2)}) collective-permute-start(bf16[2,512,128]{2,1,0:T(8,128)(2,1)S(1)} %pad_maximum_fusion.4), channel_id=1, source_target_pairs={{0,16},{16,0},{1,17},{17,1},{2,18},{18,2},{3,19},{19,3},{4,20},{20... | collective-permute-start | bytes 786440 | tf_op jit(solution)/shard_map/ppermute | solution.py:97
  70.2 13.2 %all-to-all-done.1 = bf16[8,64,768]{2,1,0:T(8,128)(2,1)S(1)} async-done(((bf16[8,64,768]{2,1,0:T(8,128)(2,1)}), bf16[8,64,768]{2,1,0:T(8,128)(2,1)S(1)}, u32[]{:S(2)}, u32[]{:S(2)}) %all-to-all-start.1) | async-done | bytes 786464 | tf_op jit(solution)/shard_map/all_to_all | solution.py:14
  83.4 0.1 convert_reduce_fusion
  83.6 0.8 broadcast_in_dim.54
  84.3 3.5 %all-to-all-start.2 = ((bf16[8,64,384]{2,1,0:T(8,128)(2,1)}), bf16[8,64,384]{2,1,0:T(8,128)(2,1)S(1)}, u32[]{:S(2)}, u32[]{:S(2)}) async-start(bf16[8,64,384]{2,1,0:T(8,128)(2,1)} %broadcast_in_dim.54), calls=%async_computation.2 | async-start | bytes 786432 | tf_op jit(solution)/shard_map/all_to_all | solution.py:14
  87.8 0.0 collective-permute-done.5
  87.8 0.0 collective-permute-done.8
  87.9 14.9 %all-to-all-done.2 = bf16[8,64,384]{2,1,0:T(8,128)(2,1)S(1)} async-done(((bf16[8,64,384]{2,1,0:T(8,128)(2,1)}), bf16[8,64,384]{2,1,0:T(8,128)(2,1)S(1)}, u32[]{:S(2)}, u32[]{:S(2)}) %all-to-all-start.2) | async-done | bytes 393248 | tf_op jit(solution)/shard_map/all_to_all | solution.py:14
  102.9 0.3 fusion.16
  103.2 2.4 %collective-permute-start.6 = (f32[512,256]{1,0:T(8,128)S(1)}, f32[512,256]{1,0:T(8,128)S(1)}, u32[]{:S(2)}, u32[]{:S(2)}) collective-permute-start(f32[512,256]{1,0:T(8,128)S(1)} %fusion.16), channel_id=1, source_target_pairs={{0,1},{1,0},{2,3},{3,2},{4,5},{5,4},{6,7},{7,6},{8,9},{9,8},{10,11... | collective-permute-start | bytes 1572872 | tf_op jit(solution)/shard_map/ppermute | solution.py:102
  105.6 0.4 convolution_convert_fusion
  106.0 0.1 fusion.34
  106.0 0.8 pad_maximum_fusion.3
  106.8 6.9 %all-to-all-start.3 = ((bf16[16,96,128]{2,1,0:T(8,128)(2,1)}), bf16[16,96,128]{2,1,0:T(8,128)(2,1)S(1)}, u32[]{:S(2)}, u32[]{:S(2)}) async-start(bf16[16,96,128]{2,1,0:T(8,128)(2,1)} %bitcast.42), calls=%async_computation.3 | async-start | bytes 786432 | tf_op jit(solution)/shard_map/all_to_all | solution.py:14
  113.7 0.0 collective-permute-done.6
  113.7 0.3 convolution_add_fusion
  114.1 7.2 %collective-permute-start.7 = (bf16[512,128]{1,0:T(8,128)(2,1)S(1)}, bf16[512,128]{1,0:T(8,128)(2,1)S(1)}, u32[]{:S(2)}, u32[]{:S(2)}) collective-permute-start(bf16[512,128]{1,0:T(8,128)(2,1)S(1)} %slice.204), channel_id=1, source_target_pairs={{0,16},{16,0},{1,17},{17,1},{2,18},{18,2},{3,19},{19,3},{4,20},{20... | collective-permute-start | bytes 393224 | tf_op jit(solution)/shard_map/ppermute | solution.py:105
  121.3 10.8 %collective-permute-done.7 = bf16[512,128]{1,0:T(8,128)(2,1)S(1)} collective-permute-done((bf16[512,128]{1,0:T(8,128)(2,1)S(1)}, bf16[512,128]{1,0:T(8,128)(2,1)S(1)}, u32[]{:S(2)}, u32[]{:S(2)}) %collective-permute-start.7) | collective-permute-done | bytes 131104 | tf_op jit(solution)/shard_map/ppermute | solution.py:105
  132.1 0.7 fusion.8
  132.8 0.0 all-to-all-done.3
  132.8 0.7 convert_reduce_fusion.1
  (25 shorter events, 0.5 us)
Async XLA Ops:
  0.6 13.7 %collective-permute-start = (bf16[128,128]{1,0:T(8,128)(2,1)}, bf16[128,128]{1,0:T(8,128)(2,1)S(1)}, u32[]{:S(2)}, u32[]{:S(2)}) collective-permute-start(bf16[128,128]{1,0:T(8,128)(2,1)} %param.6), channel_id=1, source_target_pairs={{0,16},{16,0},{1,17},{17,1},{2,18},{18,2},{3,19},{19,3},{4,20},{20... | collective-permute-start | bytes 98312 | tf_op jit(solution)/shard_map/ppermute | solution.py:62
  10.1 2.1 %copy-start.1 = (s32[128,2]{0,1:T(2,128)S(1)}, s32[128,2]{0,1:T(2,128)}, u32[]{:S(2)}) copy-start(s32[128,2]{0,1:T(2,128)} %param.8) | copy-start | bytes 3076
  10.1 3.6 %copy-start.2 = (f32[128,2]{0,1:T(2,128)S(1)}, f32[128,2]{0,1:T(2,128)}, u32[]{:S(2)}) copy-start(f32[128,2]{0,1:T(2,128)} %param.9) | copy-start | bytes 3076
  10.1 4.2 %copy-start.3 = (bf16[128,128]{1,0:T(8,128)(2,1)S(1)}, bf16[128,128]{1,0:T(8,128)(2,1)}, u32[]{:S(2)}) copy-start(bf16[128,128]{1,0:T(8,128)(2,1)} %param.7) | copy-start | bytes 98308
  10.1 4.2 %copy-start.4 = (bf16[128,128]{1,0:T(8,128)(2,1)S(1)}, bf16[128,128]{1,0:T(8,128)(2,1)}, u32[]{:S(2)}) copy-start(bf16[128,128]{1,0:T(8,128)(2,1)} %param.6) | copy-start | bytes 98308
  10.3 24.6 %collective-permute-start.1 = (bf16[2,128,768]{1,2,0:T(8,128)(2,1)S(1)}, bf16[2,128,768]{1,2,0:T(8,128)(2,1)S(1)}, u32[]{:S(2)}, u32[]{:S(2)}) collective-permute-start(bf16[2,128,768]{1,2,0:T(8,128)(2,1)S(1)} %bitcast.101), channel_id=1, source_target_pairs={{0,16},{16,0},{1,17},{17,1},{2,18},{18,2},{3,19},{19,3},{4,20},{20... | collective-permute-start | bytes 1179656 | tf_op jit(solution)/shard_map/ppermute | solution.py:41
  12.3 10.5 %copy-start = (bf16[1,1536,128]{2,1,0:T(8,128)(2,1)S(1)}, bf16[1,1536,128]{2,1,0:T(8,128)(2,1)}, u32[]{:S(2)}) copy-start(bf16[1,1536,128]{2,1,0:T(8,128)(2,1)} %param.11) | copy-start | bytes 1179652
  15.3 23.1 %all-to-all-start = ((bf16[8,64,384]{2,1,0:T(8,128)(2,1)}), bf16[8,64,384]{2,1,0:T(8,128)(2,1)S(1)}, u32[]{:S(2)}, u32[]{:S(2)}) async-start(bf16[8,64,384]{2,1,0:T(8,128)(2,1)} %bitcast.2), calls=%async_computation | async-start | bytes 786432 | tf_op jit(solution)/shard_map/all_to_all | solution.py:14
  22.9 36.9 %collective-permute-start.4 = (bf16[2,384,128]{2,1,0:T(8,128)(2,1)S(1)}, bf16[2,384,128]{2,1,0:T(8,128)(2,1)}, u32[]{:S(2)}, u32[]{:S(2)}) collective-permute-start(bf16[2,384,128]{2,1,0:T(8,128)(2,1)S(1)} %get-tuple-element.23), channel_id=1, source_target_pairs={{0,1},{1,0},{2,3},{3,2},{4,5},{5,4},{6,7},{7,6},{8,9},{9,8},{10,11... | collective-permute-start | bytes 589832 | tf_op jit(solution)/shard_map/ppermute | solution.py:92
  35.0 12.2 %collective-permute-start.3 = (bf16[2,128,768]{1,2,0:T(8,128)(2,1)S(1)}, bf16[2,128,768]{1,2,0:T(8,128)(2,1)}, u32[]{:S(2)}, u32[]{:S(2)}) collective-permute-start(bf16[2,128,768]{1,2,0:T(8,128)(2,1)S(1)} %pad_maximum_fusion.1), channel_id=1, source_target_pairs={{0,1},{1,0},{2,3},{3,2},{4,5},{5,4},{6,7},{7,6},{8,9},{9,8},{10,11... | collective-permute-start | bytes 1179656 | tf_op jit(solution)/shard_map/ppermute | solution.py:45
  38.4 9.9 %collective-permute-start.2 = (bf16[512,384]{1,0:T(8,128)(2,1)S(1)}, bf16[512,384]{1,0:T(8,128)(2,1)S(1)}, u32[]{:S(2)}, u32[]{:S(2)}) collective-permute-start(bf16[512,384]{1,0:T(8,128)(2,1)S(1)} %bitcast.87), channel_id=1, source_target_pairs={{0,1},{1,0},{2,3},{3,2},{4,5},{5,4},{6,7},{7,6},{8,9},{9,8},{10,11... | collective-permute-start | bytes 1179656 | tf_op jit(solution)/shard_map/ppermute | solution.py:80
  49.6 33.8 %all-to-all-start.1 = ((bf16[8,64,768]{2,1,0:T(8,128)(2,1)}), bf16[8,64,768]{2,1,0:T(8,128)(2,1)S(1)}, u32[]{:S(2)}, u32[]{:S(2)}) async-start(bf16[8,64,768]{2,1,0:T(8,128)(2,1)} %bitcast.12), calls=%async_computation.1 | async-start | bytes 1572864 | tf_op jit(solution)/shard_map/all_to_all | solution.py:14
  60.8 27.0 %collective-permute-start.5 = (bf16[2,384,128]{2,1,0:T(8,128)(2,1)S(1)}, bf16[2,384,128]{2,1,0:T(8,128)(2,1)S(1)}, u32[]{:S(2)}, u32[]{:S(2)}) collective-permute-start(bf16[2,384,128]{2,1,0:T(8,128)(2,1)S(1)} %fusion.12), channel_id=1, source_target_pairs={{0,16},{16,0},{1,17},{17,1},{2,18},{18,2},{3,19},{19,3},{4,20},{20... | collective-permute-start | bytes 589832 | tf_op jit(solution)/shard_map/ppermute | solution.py:94
  68.1 19.8 %collective-permute-start.8 = (bf16[2,512,128]{2,1,0:T(8,128)(2,1)S(1)}, bf16[2,512,128]{2,1,0:T(8,128)(2,1)S(1)}, u32[]{:S(2)}, u32[]{:S(2)}) collective-permute-start(bf16[2,512,128]{2,1,0:T(8,128)(2,1)S(1)} %pad_maximum_fusion.4), channel_id=1, source_target_pairs={{0,16},{16,0},{1,17},{17,1},{2,18},{18,2},{3,19},{19,3},{4,20},{20... | collective-permute-start | bytes 786440 | tf_op jit(solution)/shard_map/ppermute | solution.py:97
  84.3 18.5 %all-to-all-start.2 = ((bf16[8,64,384]{2,1,0:T(8,128)(2,1)}), bf16[8,64,384]{2,1,0:T(8,128)(2,1)S(1)}, u32[]{:S(2)}, u32[]{:S(2)}) async-start(bf16[8,64,384]{2,1,0:T(8,128)(2,1)} %broadcast_in_dim.54), calls=%async_computation.2 | async-start | bytes 786432 | tf_op jit(solution)/shard_map/all_to_all | solution.py:14
  103.2 10.6 %collective-permute-start.6 = (f32[512,256]{1,0:T(8,128)S(1)}, f32[512,256]{1,0:T(8,128)S(1)}, u32[]{:S(2)}, u32[]{:S(2)}) collective-permute-start(f32[512,256]{1,0:T(8,128)S(1)} %fusion.16), channel_id=1, source_target_pairs={{0,1},{1,0},{2,3},{3,2},{4,5},{5,4},{6,7},{7,6},{8,9},{9,8},{10,11... | collective-permute-start | bytes 1572872 | tf_op jit(solution)/shard_map/ppermute | solution.py:102
  106.8 25.9 %all-to-all-start.3 = ((bf16[16,96,128]{2,1,0:T(8,128)(2,1)}), bf16[16,96,128]{2,1,0:T(8,128)(2,1)S(1)}, u32[]{:S(2)}, u32[]{:S(2)}) async-start(bf16[16,96,128]{2,1,0:T(8,128)(2,1)} %bitcast.42), calls=%async_computation.3 | async-start | bytes 786432 | tf_op jit(solution)/shard_map/all_to_all | solution.py:14
  114.1 18.0 %collective-permute-start.7 = (bf16[512,128]{1,0:T(8,128)(2,1)S(1)}, bf16[512,128]{1,0:T(8,128)(2,1)S(1)}, u32[]{:S(2)}, u32[]{:S(2)}) collective-permute-start(bf16[512,128]{1,0:T(8,128)(2,1)S(1)} %slice.204), channel_id=1, source_target_pairs={{0,16},{16,0},{1,17},{17,1},{2,18},{18,2},{3,19},{19,3},{4,20},{20... | collective-permute-start | bytes 393224 | tf_op jit(solution)/shard_map/ppermute | solution.py:105

commit v8 on v5

--- a/solution.py
+++ b/solution.py
@@ -61,7 +61,7 @@
     select = jnp.sum(
         matches.reshape(rows, tok_rows, top_count).astype(F32), axis=2
     ).astype(BF)
-    w = w_gate_up[0].reshape(width, 2, dps, XH, CORE, step).transpose(3, 4, 0, 1, 2, 5)
+    w = w_gate_up[0].reshape(width, 2, dps, CORE, XH, step).transpose(4, 3, 0, 1, 2, 5)
     w_mine, w_beside = to_quarters(
         w.reshape(XH, CORE, width, 2 * part), xh, core
     )
@@ -83,20 +83,20 @@
     hidden = hidden.reshape(XH, rows, part)
 
     slot_grads = pick(core, jnp.stack([mine[:, 2 * width :], beside[:, 2 * width :]]))
+    slot_grads = jnp.concatenate(slot_grads, axis=1)
+    grads = []
+    for columns in hidden:
+        g = lax.dot_general(
+            columns, slot_grads, (((0,), (0,)), ((), ())), preferred_element_type=F32
+        ).astype(BF)
+        g = [half.reshape(dps, step, width) for half in jnp.split(g, CORE, axis=1)]
+        grads.append(jnp.stack(g, axis=1))
+    grads = jnp.stack(grads, axis=2)
+    moved = exchange(grads.reshape(dps * CORE, XH * step, width), ("dp", "core"))
+    moved = moved.reshape(dps, QUARTERS * step, width)
+    grad_share = jnp.sum(moved.astype(F32), axis=0)
 
-    def grads_of(half, g):
-        out = lax.dot_general(half, g, (((0,), (0,)), ((), ())), preferred_element_type=F32)
-        return out.astype(BF).reshape(dps, step, width)
-
-    grads = jnp.stack(
-        [jnp.stack([grads_of(hidden[h], g) for h in range(XH)], axis=1) for g in slot_grads],
-        axis=1,
-    )
-    moved = exchange(grads.reshape(dps * CORE, XH * step, width), ("dp", "core"))
-    moved = jnp.sum(moved.reshape(dps, CORE, XH, step, width).astype(F32), axis=0)
-    grad_share = moved.transpose(1, 0, 2, 3).reshape(QUARTERS * step, width)
-
-    down = w_down[0].reshape(dps, XH, CORE, step, width).transpose(2, 1, 0, 3, 4)
+    down = w_down[0].reshape(dps, CORE, XH, step, width).transpose(1, 2, 0, 3, 4)
     down_mine, down_sent = pick(core, down.reshape(CORE, XH, part, width))
     down_beside = lax.ppermute(down_sent, "core", SWAP)
 

time: 134 us -> 134 us (level)
  no operation moved by 1% of the time
where the time goes in v8:
time: 134 us; the launch traced here: 133 us
  starting transfers between devices  61.9 us (46%)
  blocking collectives  32.3 us (24%)
  waiting for transfers between devices  26.6 us (20%)
  local copies, waits for them, and re-layouts  4.11 us (3%)
  other arithmetic  3.6 us (3%)
  matrix products  3.42 us (3%)
    all_to_all x1, blocking collectives, exchange(): return lax.all_to_all(pieces, axes, split_axis=0, concat_axis=0, tiled=True)  32.3 us
    all_to_all x3, starting transfers between devices, exchange(): return lax.all_to_all(pieces, axes, split_axis=0, concat_axis=0, tiled=True)  26.4 us
    all_to_all x3, waiting for transfers between devices, exchange(): return lax.all_to_all(pieces, axes, split_axis=0, concat_axis=0, tiled=True)  21.7 us
    ppermute x1, starting transfers between devices, to_quarters(): beside = lax.ppermute(jnp.stack([near_sent, far_sent]), 'core', SWAP)  12.1 us
    ppermute x1, starting transfers between devices, per_device(): beside = lax.ppermute(mine, 'core', SWAP)  8.11 us
    ppermute x1, starting transfers between devices, per_device(): far_tokens = lax.ppermute(tokens, 'xh', SWAP)  7.94 us
    ppermute x1, starting transfers between devices, per_device(): down_beside = lax.ppermute(down_sent, 'core', SWAP)  3.52 us
    ppermute x1, waiting for transfers between devices, to_quarters(): far = lax.ppermute(sent, 'xh', SWAP)  3.4 us
  transfers between devices with their start and end apart: 9, of which 5 were waited for; matrix products, arithmetic and copies ran while one was open for 7% of the time, Pallas kernels for 0%

profile of v8, /device:TPU:1, one launch (start us, length us, event | category | flops | bytes accessed | tf_op | source)
XLA Modules:
  0.0 133.0 jit_solution(2991605791051621569)
XLA Ops:
  0.6 7.9 %collective-permute-start = (bf16[128,128]{1,0:T(8,128)(2,1)}, bf16[128,128]{1,0:T(8,128)(2,1)S(1)}, u32[]{:S(2)}, u32[]{:S(2)}) collective-permute-start(bf16[128,128]{1,0:T(8,128)(2,1)} %param.6), channel_id=1, source_target_pairs={{0,16},{16,0},{1,17},{17,1},{2,18},{18,2},{3,19},{19,3},{4,20},{20... | collective-permute-start | bytes 98312 | tf_op jit(solution)/shard_map/ppermute | solution.py:58
  8.6 1.5 %copy.53 = bf16[1,128,3072]{1,2,0:T(8,128)(2,1)S(1)} copy(bf16[1,128,3072]{2,1,0:T(8,128)(2,1)} %param.10) | data formatting | bytes 1572864 | tf_op args[4]
  10.1 0.0 copy-start.1
  10.1 0.0 copy-start.2
  10.1 0.0 copy-start.3
  10.1 0.0 copy-start.4
  10.2 0.1 broadcast_select_fusion.1
  10.3 1.9 %collective-permute-start.1 = (bf16[2,128,768]{1,2,0:T(8,128)(2,1)S(1)}, bf16[2,128,768]{1,2,0:T(8,128)(2,1)S(1)}, u32[]{:S(2)}, u32[]{:S(2)}) collective-permute-start(bf16[2,128,768]{1,2,0:T(8,128)(2,1)S(1)} %bitcast.82), channel_id=1, source_target_pairs={{0,16},{16,0},{1,17},{17,1},{2,18},{18,2},{3,19},{19,3},{4,20},{20... | collective-permute-start | bytes 1179656 | tf_op jit(solution)/shard_map/ppermute | solution.py:37
  12.2 0.0 copy-done.1
  12.2 0.1 copy.49
  12.3 0.1 eq.59
  12.4 0.1 eq.55
  12.6 0.6 reduce-window.6
  13.2 0.2 slice_reduce_fusion
  13.4 0.1 fusion.13
  13.5 0.1 reduce_sum.48
  13.7 0.0 copy-done.2
  13.7 0.1 copy.52
  13.8 0.1 broadcast_in_dim.50
  14.0 0.1 copy.51
  14.0 0.1 convert_reduce_fusion.2
  14.1 0.1 select_reduce_fusion
  14.3 0.0 collective-permute-done
  14.3 0.0 copy-done.3
  14.3 0.0 copy-done.4
  14.3 1.0 fusion
  15.3 7.4 %all-to-all-start = ((bf16[8,64,384]{2,1,0:T(8,128)(2,1)}), bf16[8,64,384]{2,1,0:T(8,128)(2,1)S(1)}, u32[]{:S(2)}, u32[]{:S(2)}) async-start(bf16[8,64,384]{2,1,0:T(8,128)(2,1)} %bitcast.2), calls=%async_computation | async-start | bytes 786432 | tf_op jit(solution)/shard_map/all_to_all | solution.py:14
  22.8 3.4 %collective-permute-done.1 = bf16[2,128,768]{1,2,0:T(8,128)(2,1)S(1)} collective-permute-done((bf16[2,128,768]{1,2,0:T(8,128)(2,1)S(1)}, bf16[2,128,768]{1,2,0:T(8,128)(2,1)S(1)}, u32[]{:S(2)}, u32[]{:S(2)}) %collective-permute-start.1) | collective-permute-done | bytes 393248 | tf_op jit(solution)/shard_map/ppermute | solution.py:37
  26.3 12.1 %collective-permute-start.3 = (bf16[2,128,768]{1,2,0:T(8,128)(2,1)S(1)}, bf16[2,128,768]{1,2,0:T(8,128)(2,1)S(1)}, u32[]{:S(2)}, u32[]{:S(2)}) collective-permute-start(bf16[2,128,768]{1,2,0:T(8,128)(2,1)S(1)} %pad_maximum_fusion.1), channel_id=1, source_target_pairs={{0,1},{1,0},{2,3},{3,2},{4,5},{5,4},{6,7},{7,6},{8,9},{9,8},{10,11... | collective-permute-start | bytes 1179656 | tf_op jit(solution)/shard_map/ppermute | solution.py:41
  38.4 0.0 all-to-all-done
  38.4 8.1 %collective-permute-start.2 = (bf16[512,384]{1,0:T(8,128)(2,1)S(1)}, bf16[512,384]{1,0:T(8,128)(2,1)S(1)}, u32[]{:S(2)}, u32[]{:S(2)}) collective-permute-start(bf16[512,384]{1,0:T(8,128)(2,1)S(1)} %bitcast.74), channel_id=1, source_target_pairs={{0,1},{1,0},{2,3},{3,2},{4,5},{5,4},{6,7},{7,6},{8,9},{9,8},{10,11... | collective-permute-start | bytes 1179656 | tf_op jit(solution)/shard_map/ppermute | solution.py:75
  46.6 0.2 copy.55
  46.8 0.4 fusion.2
  47.1 0.0 collective-permute-done.3
  47.1 0.2 copy.56
  47.3 0.5 collective-permute-done.2
  47.9 0.4 add_convert_fusion
  48.2 32.3 %all_to_all.20 = bf16[8,64,768]{2,1,0:T(8,128)(2,1)S(1)} all-to-all(bf16[8,64,768]{2,1,0:T(8,128)(2,1)S(1)} %bitcast.73), channel_id=1, replica_groups=mesh['dp'=4,'expert'=8,'xh'=2,'z'=8,'core'=2] {'z'}, dimensions={0} | all-to-all | bytes 1572864 | tf_op jit(solution)/shard_map/all_to_all | solution.py:14
  80.5 0.1 convert_reduce_fusion
  80.6 0.0 copy-start
  80.7 1.0 broadcast_in_dim.54
  81.7 7.0 %all-to-all-start.2 = ((bf16[16,64,384]{2,1,0:T(8,128)(2,1)}), bf16[16,64,384]{2,1,0:T(8,128)(2,1)S(1)}, u32[]{:S(2)}, u32[]{:S(2)}) async-start(bf16[16,64,384]{2,1,0:T(8,128)(2,1)} %broadcast_in_dim.54), calls=%async_computation.2 | async-start | bytes 1572864 | tf_op jit(solution)/shard_map/all_to_all | solution.py:14
  88.7 0.0 copy-done
  88.8 3.5 %collective-permute-start.4 = (bf16[2,384,128]{2,1,0:T(8,128)(2,1)S(1)}, bf16[2,384,128]{2,1,0:T(8,128)(2,1)S(1)}, u32[]{:S(2)}, u32[]{:S(2)}) collective-permute-start(bf16[2,384,128]{2,1,0:T(8,128)(2,1)S(1)} %bitcast.90), channel_id=1, source_target_pairs={{0,1},{1,0},{2,3},{3,2},{4,5},{5,4},{6,7},{7,6},{8,9},{9,8},{10,11... | collective-permute-start | bytes 589832 | tf_op jit(solution)/shard_map/ppermute | solution.py:101
  92.3 14.7 %all-to-all-done.2 = bf16[16,64,384]{2,1,0:T(8,128)(2,1)S(1)} async-done(((bf16[16,64,384]{2,1,0:T(8,128)(2,1)}), bf16[16,64,384]{2,1,0:T(8,128)(2,1)S(1)}, u32[]{:S(2)}, u32[]{:S(2)}) %all-to-all-start.2) | async-done | bytes 786464 | tf_op jit(solution)/shard_map/all_to_all | solution.py:14
  107.0 0.1 fusion.18
  107.1 0.3 convolution_convert_fusion
  107.4 0.3 convolution_convert_fusion.1
  107.8 0.8 pad_maximum_fusion.2
  108.6 11.9 %all-to-all-start.3 = ((bf16[8,192,128]{2,1,0:T(8,128)(2,1)}), bf16[8,192,128]{2,1,0:T(8,128)(2,1)S(1)}, u32[]{:S(2)}, u32[]{:S(2)}) async-start(bf16[8,192,128]{2,1,0:T(8,128)(2,1)} %bitcast.33), calls=%async_computation.3 | async-start | bytes 786432 | tf_op jit(solution)/shard_map/all_to_all | solution.py:14
  120.6 0.0 collective-permute-done.4
  120.6 0.3 fusion.5
  120.8 0.3 convolution_add_fusion
  121.1 1.9 %collective-permute-start.5 = (f32[512,128]{1,0:T(8,128)S(1)}, f32[512,128]{1,0:T(8,128)S(1)}, u32[]{:S(2)}, u32[]{:S(2)}) collective-permute-start(f32[512,128]{1,0:T(8,128)S(1)} %convolution_add_fusion), channel_id=1, source_target_pairs={{0,1},{1,0},{2,3},{3,2},{4,5},{5,4},{6,7},{7,6},{8,9},{9,8},{10,11... | collective-permute-start | bytes 786440 | tf_op jit(solution)/shard_map/ppermute | solution.py:106
  123.0 0.3 fusion.22
  123.3 0.3 convolution_add_fusion.1
  123.6 1.0 collective-permute-done.5
  124.5 0.7 add_convert_fusion.1
  125.2 7.0 %all-to-all-done.3 = bf16[8,192,128]{2,1,0:T(8,128)(2,1)S(1)} async-done(((bf16[8,192,128]{2,1,0:T(8,128)(2,1)}), bf16[8,192,128]{2,1,0:T(8,128)(2,1)S(1)}, u32[]{:S(2)}, u32[]{:S(2)}) %all-to-all-start.3) | async-done | bytes 393248 | tf_op jit(solution)/shard_map/all_to_all | solution.py:14
  132.2 0.7 convert_reduce_fusion.1
  (19 shorter events, 0.4 us)
Async XLA Ops:
  0.6 13.6 %collective-permute-start = (bf16[128,128]{1,0:T(8,128)(2,1)}, bf16[128,128]{1,0:T(8,128)(2,1)S(1)}, u32[]{:S(2)}, u32[]{:S(2)}) collective-permute-start(bf16[128,128]{1,0:T(8,128)(2,1)} %param.6), channel_id=1, source_target_pairs={{0,16},{16,0},{1,17},{17,1},{2,18},{18,2},{3,19},{19,3},{4,20},{20... | collective-permute-start | bytes 98312 | tf_op jit(solution)/shard_map/ppermute | solution.py:58
  10.1 2.1 %copy-start.1 = (s32[128,2]{0,1:T(2,128)S(1)}, s32[128,2]{0,1:T(2,128)}, u32[]{:S(2)}) copy-start(s32[128,2]{0,1:T(2,128)} %param.8) | copy-start | bytes 3076
  10.1 3.6 %copy-start.2 = (f32[128,2]{0,1:T(2,128)S(1)}, f32[128,2]{0,1:T(2,128)}, u32[]{:S(2)}) copy-start(f32[128,2]{0,1:T(2,128)} %param.9) | copy-start | bytes 3076
  10.1 4.2 %copy-start.3 = (bf16[128,128]{1,0:T(8,128)(2,1)S(1)}, bf16[128,128]{1,0:T(8,128)(2,1)}, u32[]{:S(2)}) copy-start(bf16[128,128]{1,0:T(8,128)(2,1)} %param.7) | copy-start | bytes 98308
  10.1 4.2 %copy-start.4 = (bf16[128,128]{1,0:T(8,128)(2,1)S(1)}, bf16[128,128]{1,0:T(8,128)(2,1)}, u32[]{:S(2)}) copy-start(bf16[128,128]{1,0:T(8,128)(2,1)} %param.6) | copy-start | bytes 98308
  10.3 15.9 %collective-permute-start.1 = (bf16[2,128,768]{1,2,0:T(8,128)(2,1)S(1)}, bf16[2,128,768]{1,2,0:T(8,128)(2,1)S(1)}, u32[]{:S(2)}, u32[]{:S(2)}) collective-permute-start(bf16[2,128,768]{1,2,0:T(8,128)(2,1)S(1)} %bitcast.82), channel_id=1, source_target_pairs={{0,16},{16,0},{1,17},{17,1},{2,18},{18,2},{3,19},{19,3},{4,20},{20... | collective-permute-start | bytes 1179656 | tf_op jit(solution)/shard_map/ppermute | solution.py:37
  15.3 23.1 %all-to-all-start = ((bf16[8,64,384]{2,1,0:T(8,128)(2,1)}), bf16[8,64,384]{2,1,0:T(8,128)(2,1)S(1)}, u32[]{:S(2)}, u32[]{:S(2)}) async-start(bf16[8,64,384]{2,1,0:T(8,128)(2,1)} %bitcast.2), calls=%async_computation | async-start | bytes 786432 | tf_op jit(solution)/shard_map/all_to_all | solution.py:14
  26.3 20.9 %collective-permute-start.3 = (bf16[2,128,768]{1,2,0:T(8,128)(2,1)S(1)}, bf16[2,128,768]{1,2,0:T(8,128)(2,1)S(1)}, u32[]{:S(2)}, u32[]{:S(2)}) collective-permute-start(bf16[2,128,768]{1,2,0:T(8,128)(2,1)S(1)} %pad_maximum_fusion.1), channel_id=1, source_target_pairs={{0,1},{1,0},{2,3},{3,2},{4,5},{5,4},{6,7},{7,6},{8,9},{9,8},{10,11... | collective-permute-start | bytes 1179656 | tf_op jit(solution)/shard_map/ppermute | solution.py:41
  38.4 9.4 %collective-permute-start.2 = (bf16[512,384]{1,0:T(8,128)(2,1)S(1)}, bf16[512,384]{1,0:T(8,128)(2,1)S(1)}, u32[]{:S(2)}, u32[]{:S(2)}) collective-permute-start(bf16[512,384]{1,0:T(8,128)(2,1)S(1)} %bitcast.74), channel_id=1, source_target_pairs={{0,1},{1,0},{2,3},{3,2},{4,5},{5,4},{6,7},{7,6},{8,9},{9,8},{10,11... | collective-permute-start | bytes 1179656 | tf_op jit(solution)/shard_map/ppermute | solution.py:75
  80.6 8.1 %copy-start = (bf16[1,1536,128]{2,1,0:T(8,128)(2,1)S(1)}, bf16[1,1536,128]{2,1,0:T(8,128)(2,1)}, u32[]{:S(2)}) copy-start(bf16[1,1536,128]{2,1,0:T(8,128)(2,1)} %param.11) | copy-start | bytes 1179652
  81.7 25.3 %all-to-all-start.2 = ((bf16[16,64,384]{2,1,0:T(8,128)(2,1)}), bf16[16,64,384]{2,1,0:T(8,128)(2,1)S(1)}, u32[]{:S(2)}, u32[]{:S(2)}) async-start(bf16[16,64,384]{2,1,0:T(8,128)(2,1)} %broadcast_in_dim.54), calls=%async_computation.2 | async-start | bytes 1572864 | tf_op jit(solution)/shard_map/all_to_all | solution.py:14
  88.8 31.8 %collective-permute-start.4 = (bf16[2,384,128]{2,1,0:T(8,128)(2,1)S(1)}, bf16[2,384,128]{2,1,0:T(8,128)(2,1)S(1)}, u32[]{:S(2)}, u32[]{:S(2)}) collective-permute-start(bf16[2,384,128]{2,1,0:T(8,128)(2,1)S(1)} %bitcast.90), channel_id=1, source_target_pairs={{0,1},{1,0},{2,3},{3,2},{4,5},{5,4},{6,7},{7,6},{8,9},{9,8},{10,11... | collective-permute-start | bytes 589832 | tf_op jit(solution)/shard_map/ppermute | solution.py:101
  108.6 23.6 %all-to-all-start.3 = ((bf16[8,192,128]{2,1,0:T(8,128)(2,1)}), bf16[8,192,128]{2,1,0:T(8,128)(2,1)S(1)}, u32[]{:S(2)}, u32[]{:S(2)}) async-start(bf16[8,192,128]{2,1,0:T(8,128)(2,1)} %bitcast.33), calls=%async_computation.3 | async-start | bytes 786432 | tf_op jit(solution)/shard_map/all_to_all | solution.py:14
  121.1 3.4 %collective-permute-start.5 = (f32[512,128]{1,0:T(8,128)S(1)}, f32[512,128]{1,0:T(8,128)S(1)}, u32[]{:S(2)}, u32[]{:S(2)}) collective-permute-start(f32[512,128]{1,0:T(8,128)S(1)} %convolution_add_fusion), channel_id=1, source_target_pairs={{0,1},{1,0},{2,3},{3,2},{4,5},{5,4},{6,7},{7,6},{8,9},{9,8},{10,11... | collective-permute-start | bytes 786440 | tf_op jit(solution)/shard_map/ppermute | solution.py:106

commit v9 on v8

--- a/solution.py
+++ b/solution.py
@@ -1,3 +1,5 @@
+import functools
+
 import jax
 import jax.numpy as jnp
 from jax import lax
@@ -23,13 +25,20 @@
     return jnp.where(first, pair[0], pair[1]), jnp.where(first, pair[1], pair[0])
 
 
-def slots_of(routes, experts, capacity):
-    flat = routes.reshape(-1)
-    onehot = (flat[:, None] == jnp.arange(experts, dtype=jnp.int32)[None, :]).astype(jnp.int32)
-    before = jnp.cumsum(onehot, axis=0) - onehot
-    slot = jnp.sum(before * onehot, axis=1)
-    target = flat * capacity + slot
-    return jnp.arange(experts * capacity, dtype=jnp.int32)[:, None] == target[None, :]
+def slots_of(routes, route_weight, experts, capacity):
+    tokens = routes.shape[0]
+    ids = jnp.arange(experts, dtype=jnp.int32)[:, None]
+    named = [ids == column for column in routes.T[:, None, :]]
+    gates = sum(jnp.where(n, w, 0.0) for n, w in zip(named, route_weight.T[:, None, :]))
+    named = functools.reduce(jnp.logical_or, named)
+    order = jnp.arange(tokens, dtype=jnp.int32)
+    earlier = (order[:, None] < order[None, :]).astype(BF)
+    slot = dot(named.astype(BF), earlier).astype(jnp.int32)
+    slot = jnp.where(named, slot, -1)
+    places = jnp.arange(capacity, dtype=jnp.int32)[None, :, None]
+    match = slot[:, None, :] == places
+    weights = jnp.sum(jnp.where(match, gates[:, None, :], 0.0), axis=2)
+    return match.astype(BF).reshape(experts * capacity, tokens), weights.reshape(-1)
 
 
 def to_quarters(blocks, xh, core):
@@ -57,16 +66,12 @@
 
     far_tokens = lax.ppermute(tokens, "xh", SWAP)
 
-    matches = slots_of(routes, experts, capacity)
-    select = jnp.sum(
-        matches.reshape(rows, tok_rows, top_count).astype(F32), axis=2
-    ).astype(BF)
+    select, weights_slot = slots_of(routes, route_weight, experts, capacity)
     w = w_gate_up[0].reshape(width, 2, dps, CORE, XH, step).transpose(4, 3, 0, 1, 2, 5)
     w_mine, w_beside = to_quarters(
         w.reshape(XH, CORE, width, 2 * part), xh, core
     )
 
-    weights_slot = jnp.sum(jnp.where(matches, route_weight.reshape(1, -1), 0.0), axis=1)
     sent = dot(select, jnp.concatenate([tokens, far_tokens, cotangent], axis=1))
     is_token = jnp.arange(3 * width, dtype=jnp.int32)[None, :] < 2 * width
     sent = (sent * jnp.where(is_token, 1.0, weights_slot[:, None])).astype(BF)

time: 134 us -> 132 us (0.985)
  starting transfers between devices: 61.9 us -> 60.5 us
  waiting for transfers between devices: 26.6 us -> 28 us
    ppermute x1, waiting for transfers between devices: 3.4 us -> 4.83 us  [to_quarters(): far = lax.ppermute(sent, 'xh', SWAP)]
    ppermute x1, starting transfers between devices: 8.11 us -> 6.68 us  [per_device(): beside = lax.ppermute(mine, 'core', SWAP)]
    dot_general x7 -> x8, matrix products: 2.8 us -> 2.95 us  [dot(): return jnp.dot(a, b, preferred_element_type=F32)]
  transfers between devices with their start and end apart: 9 -> 9, of which waited for: 5 -> 5; matrix products, arithmetic and copies ran while one was open for 7% -> 6% of each run, Pallas kernels for 0% -> 0%
where the time goes in v9:
time: 132 us
  starting transfers between devices  60.5 us (46%)
  blocking collectives  32.3 us (24%)
  waiting for transfers between devices  28 us (21%)
  matrix products  3.56 us (3%)
  local copies, waits for them, and re-layouts  3.21 us (2%)
  other arithmetic  2.93 us (2%)
    all_to_all x1, blocking collectives, exchange(): return lax.all_to_all(pieces, axes, split_axis=0, concat_axis=0, tiled=True)  32.3 us
    all_to_all x3, starting transfers between devices, exchange(): return lax.all_to_all(pieces, axes, split_axis=0, concat_axis=0, tiled=True)  26.4 us
    all_to_all x3, waiting for transfers between devices, exchange(): return lax.all_to_all(pieces, axes, split_axis=0, concat_axis=0, tiled=True)  21.7 us
    ppermute x1, starting transfers between devices, to_quarters(): beside = lax.ppermute(jnp.stack([near_sent, far_sent]), 'core', SWAP)  12.1 us
    ppermute x1, starting transfers between devices, per_device(): far_tokens = lax.ppermute(tokens, 'xh', SWAP)  7.94 us
    ppermute x1, starting transfers between devices, per_device(): beside = lax.ppermute(mine, 'core', SWAP)  6.68 us
    ppermute x1, waiting for transfers between devices, to_quarters(): far = lax.ppermute(sent, 'xh', SWAP)  4.83 us
    ppermute x1, starting transfers between devices, per_device(): down_beside = lax.ppermute(down_sent, 'core', SWAP)  3.52 us
  transfers between devices with their start and end apart: 9, of which 5 were waited for; matrix products, arithmetic and copies ran while one was open for 6% of the time, Pallas kernels for 0%

profile of v9, /device:TPU:1, one launch (start us, length us, event | category | flops | bytes accessed | tf_op | source)
XLA Modules:
  0.0 131.5 jit_solution(3699641307625378793)
XLA Ops:
  0.6 7.9 %collective-permute-start = (bf16[128,128]{1,0:T(8,128)(2,1)}, bf16[128,128]{1,0:T(8,128)(2,1)S(1)}, u32[]{:S(2)}, u32[]{:S(2)}) collective-permute-start(bf16[128,128]{1,0:T(8,128)(2,1)} %param.6), channel_id=1, source_target_pairs={{0,16},{16,0},{1,17},{17,1},{2,18},{18,2},{3,19},{19,3},{4,20},{20... | collective-permute-start | bytes 98312 | tf_op jit(solution)/shard_map/ppermute | solution.py:67
  8.6 1.5 %copy.23 = bf16[1,128,3072]{1,2,0:T(8,128)(2,1)S(1)} copy(bf16[1,128,3072]{2,1,0:T(8,128)(2,1)} %param.10) | data formatting | bytes 1572864 | tf_op args[4]
  10.1 0.0 copy-start.1
  10.1 0.0 copy-start.2
  10.1 0.0 copy-start.3
  10.1 0.0 copy-start.4
  10.2 0.1 broadcast_select_fusion.1
  10.3 1.9 %collective-permute-start.1 = (bf16[2,128,768]{1,2,0:T(8,128)(2,1)S(1)}, bf16[2,128,768]{1,2,0:T(8,128)(2,1)S(1)}, u32[]{:S(2)}, u32[]{:S(2)}) collective-permute-start(bf16[2,128,768]{1,2,0:T(8,128)(2,1)S(1)} %bitcast.86), channel_id=1, source_target_pairs={{0,16},{16,0},{1,17},{17,1},{2,18},{18,2},{3,19},{19,3},{4,20},{20... | collective-permute-start | bytes 1179656 | tf_op jit(solution)/shard_map/ppermute | solution.py:46
  12.2 0.0 copy-done.1
  12.2 0.0 copy-done.2
  12.2 0.1 fusion.1
  12.4 0.1 select_reduce_fusion
  12.5 0.1 broadcast_in_dim.88
  12.6 0.1 eq.82
  12.7 0.1 bitcast_compare_fusion
  12.8 0.0 collective-permute-done
  12.8 0.0 copy-done.3
  12.9 0.0 copy-done.4
  12.9 1.0 fusion
  13.9 7.4 %all-to-all-start = ((bf16[8,64,384]{2,1,0:T(8,128)(2,1)}), bf16[8,64,384]{2,1,0:T(8,128)(2,1)S(1)}, u32[]{:S(2)}, u32[]{:S(2)}) async-start(bf16[8,64,384]{2,1,0:T(8,128)(2,1)} %bitcast.7), calls=%async_computation | async-start | bytes 786432 | tf_op jit(solution)/shard_map/all_to_all | solution.py:16
  21.4 4.8 %collective-permute-done.1 = bf16[2,128,768]{1,2,0:T(8,128)(2,1)S(1)} collective-permute-done((bf16[2,128,768]{1,2,0:T(8,128)(2,1)S(1)}, bf16[2,128,768]{1,2,0:T(8,128)(2,1)S(1)}, u32[]{:S(2)}, u32[]{:S(2)}) %collective-permute-start.1) | collective-permute-done | bytes 393248 | tf_op jit(solution)/shard_map/ppermute | solution.py:46
  26.3 12.1 %collective-permute-start.3 = (bf16[2,128,768]{1,2,0:T(8,128)(2,1)S(1)}, bf16[2,128,768]{1,2,0:T(8,128)(2,1)S(1)}, u32[]{:S(2)}, u32[]{:S(2)}) collective-permute-start(bf16[2,128,768]{1,2,0:T(8,128)(2,1)S(1)} %pad_maximum_fusion.1), channel_id=1, source_target_pairs={{0,1},{1,0},{2,3},{3,2},{4,5},{5,4},{6,7},{7,6},{8,9},{9,8},{10,11... | collective-permute-start | bytes 1179656 | tf_op jit(solution)/shard_map/ppermute | solution.py:50
  38.4 0.0 all-to-all-done
  38.4 6.7 %collective-permute-start.2 = (bf16[512,384]{1,0:T(8,128)(2,1)S(1)}, bf16[512,384]{1,0:T(8,128)(2,1)S(1)}, u32[]{:S(2)}, u32[]{:S(2)}) collective-permute-start(bf16[512,384]{1,0:T(8,128)(2,1)S(1)} %bitcast.78), channel_id=1, source_target_pairs={{0,1},{1,0},{2,3},{3,2},{4,5},{5,4},{6,7},{7,6},{8,9},{9,8},{10,11... | collective-permute-start | bytes 1179656 | tf_op jit(solution)/shard_map/ppermute | solution.py:80
  45.1 0.2 copy.25
  45.3 0.4 fusion.3
  45.7 0.0 collective-permute-done.3
  45.7 0.2 copy.26
  45.9 0.5 collective-permute-done.2
  46.4 0.4 add_convert_fusion
  46.8 32.3 %all_to_all.20 = bf16[8,64,768]{2,1,0:T(8,128)(2,1)S(1)} all-to-all(bf16[8,64,768]{2,1,0:T(8,128)(2,1)S(1)} %bitcast.77), channel_id=1, replica_groups=mesh['dp'=4,'expert'=8,'xh'=2,'z'=8,'core'=2] {'z'}, dimensions={0} | all-to-all | bytes 1572864 | tf_op jit(solution)/shard_map/all_to_all | solution.py:16
  79.1 0.1 convert_reduce_fusion
  79.2 0.0 copy-start
  79.3 1.0 broadcast_in_dim.90
  80.3 7.0 %all-to-all-start.2 = ((bf16[16,64,384]{2,1,0:T(8,128)(2,1)}), bf16[16,64,384]{2,1,0:T(8,128)(2,1)S(1)}, u32[]{:S(2)}, u32[]{:S(2)}) async-start(bf16[16,64,384]{2,1,0:T(8,128)(2,1)} %broadcast_in_dim.90), calls=%async_computation.2 | async-start | bytes 1572864 | tf_op jit(solution)/shard_map/all_to_all | solution.py:16
  87.3 0.0 copy-done
  87.3 3.5 %collective-permute-start.4 = (bf16[2,384,128]{2,1,0:T(8,128)(2,1)S(1)}, bf16[2,384,128]{2,1,0:T(8,128)(2,1)S(1)}, u32[]{:S(2)}, u32[]{:S(2)}) collective-permute-start(bf16[2,384,128]{2,1,0:T(8,128)(2,1)S(1)} %bitcast.94), channel_id=1, source_target_pairs={{0,1},{1,0},{2,3},{3,2},{4,5},{5,4},{6,7},{7,6},{8,9},{9,8},{10,11... | collective-permute-start | bytes 589832 | tf_op jit(solution)/shard_map/ppermute | solution.py:106
  90.9 14.7 %all-to-all-done.2 = bf16[16,64,384]{2,1,0:T(8,128)(2,1)S(1)} async-done(((bf16[16,64,384]{2,1,0:T(8,128)(2,1)}), bf16[16,64,384]{2,1,0:T(8,128)(2,1)S(1)}, u32[]{:S(2)}, u32[]{:S(2)}) %all-to-all-start.2) | async-done | bytes 786464 | tf_op jit(solution)/shard_map/all_to_all | solution.py:16
  105.6 0.1 fusion.19
  105.7 0.3 convolution_convert_fusion
  106.0 0.3 convolution_convert_fusion.1
  106.4 0.8 pad_maximum_fusion.2
  107.2 11.9 %all-to-all-start.3 = ((bf16[8,192,128]{2,1,0:T(8,128)(2,1)}), bf16[8,192,128]{2,1,0:T(8,128)(2,1)S(1)}, u32[]{:S(2)}, u32[]{:S(2)}) async-start(bf16[8,192,128]{2,1,0:T(8,128)(2,1)} %bitcast.38), calls=%async_computation.3 | async-start | bytes 786432 | tf_op jit(solution)/shard_map/all_to_all | solution.py:16
  119.1 0.0 collective-permute-done.4
  119.1 0.3 fusion.5
  119.4 0.3 convolution_add_fusion
  119.7 1.9 %collective-permute-start.5 = (f32[512,128]{1,0:T(8,128)S(1)}, f32[512,128]{1,0:T(8,128)S(1)}, u32[]{:S(2)}, u32[]{:S(2)}) collective-permute-start(f32[512,128]{1,0:T(8,128)S(1)} %convolution_add_fusion), channel_id=1, source_target_pairs={{0,1},{1,0},{2,3},{3,2},{4,5},{5,4},{6,7},{7,6},{8,9},{9,8},{10,11... | collective-permute-start | bytes 786440 | tf_op jit(solution)/shard_map/ppermute | solution.py:111
  121.6 0.3 fusion.23
  121.9 0.3 convolution_add_fusion.1
  122.1 1.0 collective-permute-done.5
  123.1 0.7 add_convert_fusion.1
  123.8 7.0 %all-to-all-done.3 = bf16[8,192,128]{2,1,0:T(8,128)(2,1)S(1)} async-done(((bf16[8,192,128]{2,1,0:T(8,128)(2,1)}), bf16[8,192,128]{2,1,0:T(8,128)(2,1)S(1)}, u32[]{:S(2)}, u32[]{:S(2)}) %all-to-all-start.3) | async-done | bytes 393248 | tf_op jit(solution)/shard_map/all_to_all | solution.py:16
  130.8 0.7 convert_reduce_fusion.1
  (18 shorter events, 0.4 us)
Async XLA Ops:
  0.6 12.2 %collective-permute-start = (bf16[128,128]{1,0:T(8,128)(2,1)}, bf16[128,128]{1,0:T(8,128)(2,1)S(1)}, u32[]{:S(2)}, u32[]{:S(2)}) collective-permute-start(bf16[128,128]{1,0:T(8,128)(2,1)} %param.6), channel_id=1, source_target_pairs={{0,16},{16,0},{1,17},{17,1},{2,18},{18,2},{3,19},{19,3},{4,20},{20... | collective-permute-start | bytes 98312 | tf_op jit(solution)/shard_map/ppermute | solution.py:67
  10.1 2.1 %copy-start.1 = (s32[128,2]{0,1:T(2,128)S(1)}, s32[128,2]{0,1:T(2,128)}, u32[]{:S(2)}) copy-start(s32[128,2]{0,1:T(2,128)} %param.8) | copy-start | bytes 3076
  10.1 2.1 %copy-start.2 = (f32[128,2]{0,1:T(2,128)S(1)}, f32[128,2]{0,1:T(2,128)}, u32[]{:S(2)}) copy-start(f32[128,2]{0,1:T(2,128)} %param.9) | copy-start | bytes 3076
  10.1 2.7 %copy-start.3 = (bf16[128,128]{1,0:T(8,128)(2,1)S(1)}, bf16[128,128]{1,0:T(8,128)(2,1)}, u32[]{:S(2)}) copy-start(bf16[128,128]{1,0:T(8,128)(2,1)} %param.7) | copy-start | bytes 98308
  10.1 2.7 %copy-start.4 = (bf16[128,128]{1,0:T(8,128)(2,1)S(1)}, bf16[128,128]{1,0:T(8,128)(2,1)}, u32[]{:S(2)}) copy-start(bf16[128,128]{1,0:T(8,128)(2,1)} %param.6) | copy-start | bytes 98308
  10.3 15.9 %collective-permute-start.1 = (bf16[2,128,768]{1,2,0:T(8,128)(2,1)S(1)}, bf16[2,128,768]{1,2,0:T(8,128)(2,1)S(1)}, u32[]{:S(2)}, u32[]{:S(2)}) collective-permute-start(bf16[2,128,768]{1,2,0:T(8,128)(2,1)S(1)} %bitcast.86), channel_id=1, source_target_pairs={{0,16},{16,0},{1,17},{17,1},{2,18},{18,2},{3,19},{19,3},{4,20},{20... | collective-permute-start | bytes 1179656 | tf_op jit(solution)/shard_map/ppermute | solution.py:46
  13.9 24.5 %all-to-all-start = ((bf16[8,64,384]{2,1,0:T(8,128)(2,1)}), bf16[8,64,384]{2,1,0:T(8,128)(2,1)S(1)}, u32[]{:S(2)}, u32[]{:S(2)}) async-start(bf16[8,64,384]{2,1,0:T(8,128)(2,1)} %bitcast.7), calls=%async_computation | async-start | bytes 786432 | tf_op jit(solution)/shard_map/all_to_all | solution.py:16
  26.3 19.4 %collective-permute-start.3 = (bf16[2,128,768]{1,2,0:T(8,128)(2,1)S(1)}, bf16[2,128,768]{1,2,0:T(8,128)(2,1)S(1)}, u32[]{:S(2)}, u32[]{:S(2)}) collective-permute-start(bf16[2,128,768]{1,2,0:T(8,128)(2,1)S(1)} %pad_maximum_fusion.1), channel_id=1, source_target_pairs={{0,1},{1,0},{2,3},{3,2},{4,5},{5,4},{6,7},{7,6},{8,9},{9,8},{10,11... | collective-permute-start | bytes 1179656 | tf_op jit(solution)/shard_map/ppermute | solution.py:50
  38.4 8.0 %collective-permute-start.2 = (bf16[512,384]{1,0:T(8,128)(2,1)S(1)}, bf16[512,384]{1,0:T(8,128)(2,1)S(1)}, u32[]{:S(2)}, u32[]{:S(2)}) collective-permute-start(bf16[512,384]{1,0:T(8,128)(2,1)S(1)} %bitcast.78), channel_id=1, source_target_pairs={{0,1},{1,0},{2,3},{3,2},{4,5},{5,4},{6,7},{7,6},{8,9},{9,8},{10,11... | collective-permute-start | bytes 1179656 | tf_op jit(solution)/shard_map/ppermute | solution.py:80
  79.2 8.1 %copy-start = (bf16[1,1536,128]{2,1,0:T(8,128)(2,1)S(1)}, bf16[1,1536,128]{2,1,0:T(8,128)(2,1)}, u32[]{:S(2)}) copy-start(bf16[1,1536,128]{2,1,0:T(8,128)(2,1)} %param.11) | copy-start | bytes 1179652
  80.3 25.3 %all-to-all-start.2 = ((bf16[16,64,384]{2,1,0:T(8,128)(2,1)}), bf16[16,64,384]{2,1,0:T(8,128)(2,1)S(1)}, u32[]{:S(2)}, u32[]{:S(2)}) async-start(bf16[16,64,384]{2,1,0:T(8,128)(2,1)} %broadcast_in_dim.90), calls=%async_computation.2 | async-start | bytes 1572864 | tf_op jit(solution)/shard_map/all_to_all | solution.py:16
  87.3 31.8 %collective-permute-start.4 = (bf16[2,384,128]{2,1,0:T(8,128)(2,1)S(1)}, bf16[2,384,128]{2,1,0:T(8,128)(2,1)S(1)}, u32[]{:S(2)}, u32[]{:S(2)}) collective-permute-start(bf16[2,384,128]{2,1,0:T(8,128)(2,1)S(1)} %bitcast.94), channel_id=1, source_target_pairs={{0,1},{1,0},{2,3},{3,2},{4,5},{5,4},{6,7},{7,6},{8,9},{9,8},{10,11... | collective-permute-start | bytes 589832 | tf_op jit(solution)/shard_map/ppermute | solution.py:106
  107.2 23.6 %all-to-all-start.3 = ((bf16[8,192,128]{2,1,0:T(8,128)(2,1)}), bf16[8,192,128]{2,1,0:T(8,128)(2,1)S(1)}, u32[]{:S(2)}, u32[]{:S(2)}) async-start(bf16[8,192,128]{2,1,0:T(8,128)(2,1)} %bitcast.38), calls=%async_computation.3 | async-start | bytes 786432 | tf_op jit(solution)/shard_map/all_to_all | solution.py:16
  119.7 3.4 %collective-permute-start.5 = (f32[512,128]{1,0:T(8,128)S(1)}, f32[512,128]{1,0:T(8,128)S(1)}, u32[]{:S(2)}, u32[]{:S(2)}) collective-permute-start(f32[512,128]{1,0:T(8,128)S(1)} %convolution_add_fusion), channel_id=1, source_target_pairs={{0,1},{1,0},{2,3},{3,2},{4,5},{5,4},{6,7},{7,6},{8,9},{9,8},{10,11... | collective-permute-start | bytes 786440 | tf_op jit(solution)/shard_map/ppermute | solution.py:111
